TPU v7x, 128 devices: a whole 4x4x4 slice. The times are simulated.
128 devices in a mesh: row: 8 (over z, core), col: 16 (over y, x).
Axes of the slice: x: 4, y: 4, z: 4, core: 2. Of those that a mesh axis runs over, the one named last changes fastest.
Arguments:
- amp_start: float32 [4096, 128, 128], P(('row', 'col')), may hold values from -6 to 6
- exch_blocks: float32 [4096, 128, 128], P(('row', 'col')), may hold values from -24 to 24
- eps_virtual: float32 [4096, 128], P(('row', 'col')), may hold values from 0.5 to 4
- pair_shift: float32 [4096], P(('row', 'col')), may hold values from -2 to -0.5
- pno_sizes: int32 [4096], P(('row', 'col')), may hold values from 120 to 128, as said below
- over_ik: bfloat16 [4096, 8, 128, 128], P(('row', 'col')), may hold values from -0.5 to 0.5
- over_kj: bfloat16 [4096, 8, 128, 128], P(('row', 'col')), may hold values from -0.5 to 0.5
- fock_ik: float32 [4096, 8], P(('row', 'col')), may hold values from -0.5 to 0.5
- fock_kj: float32 [4096, 8], P(('row', 'col')), may hold values from -0.5 to 0.5
- ik_slot: int32 [4096, 8], P(('row', 'col')), may hold values from 0 to 31
- kj_slot: int32 [4096, 8], P(('row', 'col')), may hold values from 0 to 31
- col_wants: int32 [8, 16, 32], P('row', 'col'), may hold values from 0 to 31
- row_wants: int32 [8, 16, 32], P('row', 'col'), may hold values from 0 to 31
Outputs:
- amplitudes: float32 [4096, 128, 128], P(('row', 'col'))
- residual: float32 [4096, 128, 128], P(('row', 'col'))
Inputs may be any that keep to these rules, and one draw needn't show every extreme that they name: `pno_sizes`: each device holds a pair with all 128 orbitals live.
All inputs are finite; a program needn't handle non-finite values.
Results may differ from a plain program's by a relative error of at most 0.0042.
Values may be sent and summed in bfloat16 or wider, within the bound.
No kernel may reach another device: no remote copies, remote signals or barrier semaphores. Data moves between devices by JAX's collectives and lax.ppermute only.
A program may use at most 128 MiB of HBM per device.

v0:
```python
import functools

import jax
import jax.numpy as jnp
from jax import lax
from jax.experimental import pallas as pl
from jax.experimental.pallas import tpu as pltpu
from jax.sharding import PartitionSpec as P

F32 = jnp.float32
BF16 = jnp.bfloat16
W = 128
PAIRS = 32
NK = 8
CHUNK = 4
CHUNKS = PAIRS // CHUNK
NZ = 4
ANY = pl.BlockSpec(memory_space=pl.ANY)
SMEM = pl.BlockSpec(memory_space=pltpu.SMEM)
VMEM = pl.BlockSpec(memory_space=pltpu.VMEM)


def live(size):
    rows = lax.broadcasted_iota(jnp.int32, (W, W), 0) < size
    lanes = lax.broadcasted_iota(jnp.int32, (W, W), 1) < size
    return jnp.logical_and(rows, lanes)


def spread_body(wants, out):
    lane = lax.broadcasted_iota(jnp.int32, (1, W), 1)
    for q in range(out.shape[0]):
        out[q] = jnp.where(lane == 0, wants[0, 0, 2 * q], wants[0, 0, 2 * q + 1])


def spread_wants(col_wants):
    return pl.pallas_call(
        spread_body,
        in_specs=[SMEM],
        out_specs=VMEM,
        out_shape=jax.ShapeDtypeStruct((16, 1, W), jnp.int32),
        name="spread_wants",
    )(col_wants)


def fill_outgoing(rounded, col_asked, lists, out_col, out_row):
    me = lax.axis_index("row")
    for k in range(2 * 16):
        out_col[k] = rounded[col_asked[k // 2, 0, k % 2]]
    for dz in range(NZ):
        back = (NZ - dz) % NZ
        for part in range(2):
            for e in range(4):
                out_row[dz][4 * part + e] = rounded[lists[4 * part + back][0, 0, 4 * me + e]]


def first_body(sizes, col_asked, *refs):
    lists, amp, out_col, out_row, rounded = refs[:8], refs[8], refs[9], refs[10:14], refs[14]

    def step(p, carry):
        rounded[p] = jnp.where(live(sizes[p]), amp[p], 0.0).astype(BF16)
        return carry

    lax.fori_loop(0, PAIRS, step, 0)
    fill_outgoing(rounded, col_asked, lists, out_col, out_row)


OUTGOING = [jax.ShapeDtypeStruct((PAIRS, W, W), BF16)] + [jax.ShapeDtypeStruct((8, W, W), BF16)] * NZ


def first_outgoing(sizes, col_asked, lists, amp_start):
    return pl.pallas_call(
        first_body,
        in_specs=[SMEM, SMEM] + [SMEM] * 8 + [VMEM],
        out_specs=[VMEM] * 5,
        out_shape=OUTGOING,
        scratch_shapes=[pltpu.VMEM((PAIRS, W, W), BF16)],
        compiler_params=pltpu.CompilerParams(vmem_limit_bytes=60 * 2**20),
        name="first_outgoing",
    )(sizes, col_asked, *lists, amp_start)


def dot(a, b):
    return jnp.dot(a, b, preferred_element_type=F32)


def dot_t(a, b):
    return lax.dot_general(a, b, (((1,), (1,)), ((), ())), preferred_element_type=F32)


def two_halves(over, table, slot, fock, p, j, zero, lane):
    a, b = 2 * j, 2 * j + 1
    left = jnp.concatenate([over[p, a], over[p, b]], 1)
    blocks = jnp.concatenate(
        [
            jnp.concatenate([table[slot[a, p]], zero], 1),
            jnp.concatenate([zero, table[slot[b, p]]], 1),
        ],
        0,
    )
    return (dot(left, blocks) * jnp.where(lane < W, fock[a, p], fock[b, p])).astype(BF16)


def all_pairs(over, table, slot, fock, ready, finish):
    zero = jnp.zeros((W, W), BF16)
    lane = lax.broadcasted_iota(jnp.int32, (W, 2 * W), 1)
    halves = None
    for p in range(PAIRS + 1):
        if p < PAIRS:
            if p % CHUNK == 0:
                ready(p // CHUNK)
            following = [two_halves(over, table, slot, fock, p, j, zero, lane) for j in range(NK // 2)]
        if p > 0:
            right = jnp.concatenate([over[p - 1, s] for s in range(NK)], 1)
            finish(p - 1, dot_t(jnp.concatenate(halves, 1), right))
        halves = following


def chunk_copy(src, dst, sem, c):
    part = pl.ds(c * CHUNK, CHUNK)
    return pltpu.make_async_copy(src.at[part], dst.at[part], sem.at[c])


def row_body(first, slot, fock, sizes, shift, eps, eps_t, *refs):
    pieces, refs = refs[:8], refs[8:]
    over_h, amp_h, exch_h, refs = refs[0], refs[1], refs[2], refs[3:]
    base_h, refs = refs[0], refs[1:]
    over, table, amp, exch, base, table_sem, over_sem, amp_sem, exch_sem, base_sem = refs
    loads = []
    for dz in range(NZ):
        loads.append(pltpu.make_async_copy(pieces[dz].at[pl.ds(0, 4)], table.at[pl.ds(8 * dz, 4)], table_sem.at[dz]))
        loads.append(pltpu.make_async_copy(pieces[4 + dz].at[pl.ds(4, 4)], table.at[pl.ds(8 * dz + 4, 4)], table_sem.at[4 + dz]))
    for copy in loads:
        copy.start()
    for c in range(CHUNKS):
        chunk_copy(over_h, over, over_sem, c).start()
        chunk_copy(amp_h, amp, amp_sem, c).start()
        chunk_copy(exch_h, exch, exch_sem, c).start()
    for copy in loads:
        copy.wait()

    def ready(c):
        chunk_copy(over_h, over, over_sem, c).wait()
        chunk_copy(amp_h, amp, amp_sem, c).wait()
        chunk_copy(exch_h, exch, exch_sem, c).wait()

    def finish(p, coupling):
        here = amp[p]
        if first:
            here = jnp.where(live(sizes[p]), here, 0.0)
        denominator = eps_t[:, p : p + 1] + eps[p : p + 1, :] - shift[p]
        base[p] = exch[p] + denominator * here - coupling
        if p % CHUNK == CHUNK - 1:
            chunk_copy(base, base_h, base_sem, p // CHUNK).start()

    all_pairs(over, table, slot, fock, ready, finish)
    for c in range(CHUNKS):
        chunk_copy(base, base_h, base_sem, c).wait()


def chunked(dtype=F32):
    return pltpu.VMEM((PAIRS, W, W), dtype)


COST = pl.CostEstimate(flops=2 * 2 * 256 * W * W * W, bytes_accessed=16 * 2**20, transcendentals=0)


def row_part(first, slot, fock, sizes, shift, eps, eps_t, pieces, over, amp, exch):
    return pl.pallas_call(
        functools.partial(row_body, first),
        in_specs=[SMEM] * 4 + [VMEM] * 2 + [ANY] * 11,
        out_specs=ANY,
        out_shape=jax.ShapeDtypeStruct((PAIRS, W, W), F32),
        scratch_shapes=[
            pltpu.VMEM((PAIRS, NK, W, W), BF16),
            chunked(BF16),
            chunked(),
            chunked(),
            chunked(),
            pltpu.SemaphoreType.DMA((8,)),
        ]
        + [pltpu.SemaphoreType.DMA((CHUNKS,))] * 4,
        compiler_params=pltpu.CompilerParams(vmem_limit_bytes=60 * 2**20),
        cost_estimate=COST,
        name="row_part",
    )(slot, fock, sizes, shift, eps, eps_t, *pieces, over, amp, exch)


def col_body(first, slot, fock, sizes, shift, eps, eps_t, *refs):
    if first:
        col_asked, lists, refs = refs[0], refs[1:9], refs[9:]
    over_h, table_h, amp_h, base_h, refs = refs[0], refs[1], refs[2], refs[3], refs[4:]
    amp_out, refs = refs[0], refs[1:]
    if first:
        out_col, out_row, refs = refs[0], refs[1:5], refs[5:]
    else:
        residual_out, refs = refs[0], refs[1:]
    over, table, amp, base, third, table_sem, over_sem, amp_sem, base_sem, amp_out_sem, res_sem = refs
    load = pltpu.make_async_copy(table_h, table, table_sem)
    load.start()
    for c in range(CHUNKS):
        chunk_copy(over_h, over, over_sem, c).start()
        chunk_copy(amp_h, amp, amp_sem, c).start()
        chunk_copy(base_h, base, base_sem, c).start()
    load.wait()

    def ready(c):
        chunk_copy(over_h, over, over_sem, c).wait()
        chunk_copy(amp_h, amp, amp_sem, c).wait()
        chunk_copy(base_h, base, base_sem, c).wait()

    def finish(p, coupling):
        here = amp[p]
        alive = live(sizes[p])
        if first:
            here = jnp.where(alive, here, 0.0)
        denominator = eps_t[:, p : p + 1] + eps[p : p + 1, :] - shift[p]
        residual = jnp.where(alive, base[p] - coupling, 0.0)
        new = here - residual / denominator
        amp[p] = new
        if first:
            third[p] = new.astype(BF16)
        else:
            third[p] = residual
        if p % CHUNK == CHUNK - 1:
            chunk_copy(amp, amp_out, amp_out_sem, p // CHUNK).start()
            if not first:
                chunk_copy(third, residual_out, res_sem, p // CHUNK).start()

    all_pairs(over, table, slot, fock, ready, finish)
    if first:
        fill_outgoing(third, col_asked, lists, out_col, out_row)
    for c in range(CHUNKS):
        chunk_copy(amp, amp_out, amp_out_sem, c).wait()
        if not first:
            chunk_copy(third, residual_out, res_sem, c).wait()


def col_part(first, slot, fock, sizes, shift, eps, eps_t, asked, over, table, amp, base):
    whole = jax.ShapeDtypeStruct((PAIRS, W, W), F32)
    return pl.pallas_call(
        functools.partial(col_body, first),
        in_specs=[SMEM] * 4 + [VMEM] * 2 + [SMEM] * len(asked) + [ANY] * 4,
        out_specs=[ANY] + [VMEM] * 5 if first else [ANY] * 2,
        out_shape=[whole] + OUTGOING if first else [whole] * 2,
        scratch_shapes=[
            pltpu.VMEM((PAIRS, NK, W, W), BF16),
            chunked(BF16),
            chunked(),
            chunked(),
            chunked(BF16 if first else F32),
            pltpu.SemaphoreType.DMA,
        ]
        + [pltpu.SemaphoreType.DMA((CHUNKS,))] * 5,
        compiler_params=pltpu.CompilerParams(vmem_limit_bytes=60 * 2**20),
        cost_estimate=COST,
        name="col_part",
    )(slot, fock, sizes, shift, eps, eps_t, *asked, over, table, amp, base)


def swap_core(x):
    return lax.ppermute(x, "row", [(i, i ^ 1) for i in range(8)])


def shift_z(x, dz):
    return lax.ppermute(x, "row", [(i, (i + 2 * dz) % 8) for i in range(8)])


def row_exchange(bufs):
    same = [bufs[0]] + [shift_z(bufs[dz], dz) for dz in range(1, NZ)]
    return same + [swap_core(x) for x in same]


def shards(
    amp_start,
    exch_blocks,
    eps_virtual,
    pair_shift,
    pno_sizes,
    over_ik,
    over_kj,
    fock_ik,
    fock_kj,
    ik_slot,
    kj_slot,
    col_wants,
    row_wants,
):
    me = lax.axis_index("row")
    kj = kj_slot.T
    holder = kj // 4
    kj_place = ((me // 2 - holder // 2) % 4) * 8 + ((holder % 2) ^ (me % 2)) * 4 + kj % 4
    ik = ik_slot.T
    f_ik, f_kj = fock_ik.T, fock_kj.T
    eps_t = eps_virtual.T

    col_asked = lax.all_to_all(spread_wants(col_wants), "col", 0, 0, tiled=True)
    lists = row_exchange([row_wants, row_wants, row_wants, row_wants])
    asked = [col_asked] + lists
    amp = amp_start
    out = first_outgoing(pno_sizes, col_asked, lists, amp_start)
    for iteration in range(2):
        first = iteration == 0
        table = lax.all_to_all(out[0].reshape(16, 2, W, W), "col", 0, 0, tiled=True).reshape(PAIRS, W, W)
        pieces = row_exchange(out[1:])
        base = row_part(first, kj_place, f_ik, pno_sizes, pair_shift, eps_virtual, eps_t, pieces, over_kj, amp, exch_blocks)
        amp, *out = col_part(
            first, ik, f_kj, pno_sizes, pair_shift, eps_virtual, eps_t, asked if first else [], over_ik, table, amp, base
        )
    return (amp, out[0])


def solution(mesh):
    placed = (
        P(("row", "col"), None, None),
        P(("row", "col"), None, None),
        P(("row", "col"), None),
        P(("row", "col")),
        P(("row", "col")),
        P(("row", "col"), None, None, None),
        P(("row", "col"), None, None, None),
        P(("row", "col"), None),
        P(("row", "col"), None),
        P(("row", "col"), None),
        P(("row", "col"), None),
        P("row", "col", None),
        P("row", "col", None),
    )
    return jax.shard_map(
        shards,
        mesh=mesh,
        in_specs=placed,
        out_specs=(P(("row", "col"), None, None), P(("row", "col"), None, None)),
        check_vma=False,
    )
```

profile of v0, /device:TPU:1, one launch (start us, length us, event | category | flops | bytes accessed | tf_op | source)
XLA Modules:
  0.0 130.0 jit_solution(5050359225791359744)
XLA Ops:
  0.6 1.3 spread_wants.1
  1.9 7.6 %all-to-all-start = ((s32[16,1,128]{2,1,0:T(1,128)}), s32[16,1,128]{2,1,0:T(1,128)S(1)}, u32[]{:S(2)}, u32[]{:S(2)}) async-start(s32[16,1,128]{2,1,0:T(1,128)} %spread_wants.1), calls=%async_computation | async-start | bytes 16384 | tf_op jit(solution)/shard_map/all_to_all | solution.py:296
  9.5 0.0 copy-start.2
  9.5 0.0 copy-start.20
  9.5 1.0 collective-permute-start.3
  10.6 3.8 %collective-permute-start.2 = (s32[1,1,32]{2,1,0:T(1,128)}, s32[1,1,32]{2,1,0:T(1,128)S(1)}, u32[]{:S(2)}, u32[]{:S(2)}) collective-permute-start(s32[1,1,32]{2,1,0:T(1,128)} %refs_1_.1), channel_id=1, source_target_pairs={{0,96},{16,112},{32,0},{48,16},{64,32},{80,48},{96,64},{112,80},{1... | collective-permute-start | bytes 392 | tf_op jit(solution)/shard_map/ppermute | solution.py:265
  14.3 0.0 collective-permute-start.1
  14.3 0.7 collective-permute-start
  15.0 0.2 collective-permute-done.2.refs_3_.refs_4_
  15.2 0.9 collective-permute-start.6
  16.1 2.2 %collective-permute-done.1.refs_2_.refs_3_ = s32[1,1,32]{2,1,0:T(1,128)S(1)} collective-permute-done((s32[1,1,32]{2,1,0:T(1,128)}, s32[1,1,32]{2,1,0:T(1,128)S(1)}, u32[]{:S(2)}, u32[]{:S(2)}) %collective-permute-start.1) | collective-permute-done | bytes 160 | tf_op jit(solution)/shard_map/ppermute | solution.py:265
  18.4 1.5 %collective-permute-start.5 = (s32[1,1,32]{2,1,0:T(1,128)S(1)}, s32[1,1,32]{2,1,0:T(1,128)S(1)}, u32[]{:S(2)}, u32[]{:S(2)}) collective-permute-start(s32[1,1,32]{2,1,0:T(1,128)S(1)} %collective-permute-done.1.refs_2_.refs_3_), channel_id=1, source_target_pairs={{0,16},{16,0},{32,48},{48,32},{64,80},{80,64},{96,112},{112,96},{1... | collective-permute-start | bytes 392 | tf_op jit(solution)/shard_map/ppermute | solution.py:261
  19.9 0.0 collective-permute-done.refs_1_.refs_2_
  19.9 0.1 collective-permute-start.4
  20.0 0.0 collective-permute-done.3.refs_4_.refs_5_
  20.0 0.7 collective-permute-done.5.refs_6_.refs_7_
  20.7 0.3 collective-permute-done.4.refs_5_.refs_6_
  21.0 0.0 all-to-all-done.col_asked.refs_0_
  21.0 0.2 copy-done.26
  21.2 0.3 copy-done.27
  21.5 0.6 copy-done.19
  22.1 3.5 %first_outgoing.1 = (bf16[32,128,128]{2,1,0:T(8,128)(2,1)}, bf16[8,128,128]{2,1,0:T(8,128)(2,1)}, bf16[8,128,128]{2,1,0:T(8,128)(2,1)}, bf16[8,128,128]{2,1,0:T(8,128)(2,1)}, bf16[8,128,128]{2,1,0:T(8,128)(2,1)}) custom-call(s32[32]{0:T(128)} %sizes.9, s32[16,1,128]{2,1,0:T(1,128)} %copy-done.19, s32[1,1,32]{2,1,0:T(1,128)} %refs_1_.1, ...), custom_call_target="tpu_custom_call" | custom-call | tf_op jit(solution)/shard_map/first_outgoing/pallas_call | solution.py:71
  25.6 7.1 %all-to-all-start.1 = ((bf16[16,2,128,128]{3,2,1,0:T(8,128)(2,1)}), bf16[16,2,128,128]{3,2,1,0:T(8,128)(2,1)S(1)}, u32[]{:S(2)}, u32[]{:S(2)}) async-start(bf16[16,2,128,128]{3,2,1,0:T(8,128)(2,1)} %bitcast.32), calls=%async_computation.1 | async-start | bytes 2097152 | tf_op jit(solution)/shard_map/all_to_all | solution.py:303
  32.7 0.1 collective-permute-start.7
  32.8 1.5 %collective-permute-start.8 = (bf16[8,128,128]{2,1,0:T(8,128)(2,1)S(1)}, bf16[8,128,128]{2,1,0:T(8,128)(2,1)S(1)}, u32[]{:S(2)}, u32[]{:S(2)}) collective-permute-start(bf16[8,128,128]{2,1,0:T(8,128)(2,1)S(1)} %copy-done.32), channel_id=1, source_target_pairs={{0,64},{16,80},{32,96},{48,112},{64,0},{80,16},{96,32},{112,48},{1... | collective-permute-start | bytes 786440 | tf_op jit(solution)/shard_map/ppermute | solution.py:265
  34.3 2.0 %collective-permute-start.9 = (bf16[8,128,128]{2,1,0:T(8,128)(2,1)S(1)}, bf16[8,128,128]{2,1,0:T(8,128)(2,1)S(1)}, u32[]{:S(2)}, u32[]{:S(2)}) collective-permute-start(bf16[8,128,128]{2,1,0:T(8,128)(2,1)S(1)} %copy-done.30), channel_id=1, source_target_pairs={{0,96},{16,112},{32,0},{48,16},{64,32},{80,48},{96,64},{112,80},{1... | collective-permute-start | bytes 786440 | tf_op jit(solution)/shard_map/ppermute | solution.py:265
  36.3 1.4 %collective-permute-start.10 = (bf16[8,128,128]{2,1,0:T(8,128)(2,1)S(1)}, bf16[8,128,128]{2,1,0:T(8,128)(2,1)S(1)}, u32[]{:S(2)}, u32[]{:S(2)}) collective-permute-start(bf16[8,128,128]{2,1,0:T(8,128)(2,1)S(1)} %copy-done.3), channel_id=1, source_target_pairs={{0,16},{16,0},{32,48},{48,32},{64,80},{80,64},{96,112},{112,96},{1... | collective-permute-start | bytes 786440 | tf_op jit(solution)/shard_map/ppermute | solution.py:261
  37.7 9.3 %collective-permute-done.7.refs_1_ = bf16[8,128,128]{2,1,0:T(8,128)(2,1)S(1)} collective-permute-done((bf16[8,128,128]{2,1,0:T(8,128)(2,1)S(1)}, bf16[8,128,128]{2,1,0:T(8,128)(2,1)S(1)}, u32[]{:S(2)}, u32[]{:S(2)}) %collective-permute-start.7) | collective-permute-done | bytes 262176 | tf_op jit(solution)/shard_map/ppermute | solution.py:265
  47.0 1.3 %collective-permute-start.11 = (bf16[8,128,128]{2,1,0:T(8,128)(2,1)S(1)}, bf16[8,128,128]{2,1,0:T(8,128)(2,1)S(1)}, u32[]{:S(2)}, u32[]{:S(2)}) collective-permute-start(bf16[8,128,128]{2,1,0:T(8,128)(2,1)S(1)} %collective-permute-done.7.refs_1_), channel_id=1, source_target_pairs={{0,16},{16,0},{32,48},{48,32},{64,80},{80,64},{96,112},{112,96},{1... | collective-permute-start | bytes 786440 | tf_op jit(solution)/shard_map/ppermute | solution.py:261
  48.3 0.0 collective-permute-done.8.refs_2_
  48.4 0.1 collective-permute-start.12
  48.4 0.0 collective-permute-done.9.refs_3_
  48.5 0.5 collective-permute-start.13
  49.0 0.7 copy.15
  49.7 0.6 fusion.4.slot
  50.3 0.0 collective-permute-done.10.refs_4_
  50.3 0.0 collective-permute-done.12.refs_6_
  50.3 0.0 collective-permute-done.13.refs_7_
  50.4 0.6 copy-done.7
  51.0 0.1 copy-done.8
  51.1 0.1 copy-done.9
  51.2 0.1 copy-done.10
  51.3 12.3 %row_part.2.refs_12_ = f32[32,128,128]{2,1,0:T(8,128)} custom-call(s32[8,32]{1,0:T(8,128)} %fusion.4.slot, f32[8,32]{1,0:T(8,128)} %bitcast.38, s32[32]{0:T(128)} %sizes.9, f32[32]{0:T(128)} %shift.7, f32[32,128]{1,0:T(8,128)} %eps.7, f32[128,32]{1,0:T(8,128)} %bitcast.28, bf16[8,128,128]{2,1,0:T(8,128)(2,1)} %get-tuple-element.14.refs_0_, ...), custom_call_target="tpu_custom_call" | custom-call | flops 2147483648 | bytes 16777216 | tf_op jit(solution)/shard_map/row_part/pallas_call | solution.py:168
  63.6 0.0 all-to-all-done.1
  63.6 0.0 copy-start
  63.6 1.0 copy-done
  64.6 14.0 %col_part.2 = (f32[32,128,128]{2,1,0:T(8,128)}, bf16[32,128,128]{2,1,0:T(8,128)(2,1)}, bf16[8,128,128]{2,1,0:T(8,128)(2,1)}, bf16[8,128,128]{2,1,0:T(8,128)(2,1)...) custom-call(s32[8,32]{1,0:T(8,128)} %bitcast.34, f32[8,32]{1,0:T(8,128)} %bitcast.36, s32[32]{0:T(128)} %sizes.9, ...), custom_call_target="tpu_custom_call" | custom-call | flops 2147483648 | bytes 16777216 | tf_op jit(solution)/shard_map/col_part/pallas_call | solution.py:240
  78.6 6.8 %all-to-all-start.2 = ((bf16[16,2,128,128]{3,2,1,0:T(8,128)(2,1)}), bf16[16,2,128,128]{3,2,1,0:T(8,128)(2,1)S(1)}, u32[]{:S(2)}, u32[]{:S(2)}) async-start(bf16[16,2,128,128]{3,2,1,0:T(8,128)(2,1)} %bitcast.33), calls=%async_computation.2 | async-start | bytes 2097152 | tf_op jit(solution)/shard_map/all_to_all | solution.py:303
  85.4 0.9 collective-permute-start.14
  86.3 2.7 %collective-permute-start.15 = (bf16[8,128,128]{2,1,0:T(8,128)(2,1)S(1)}, bf16[8,128,128]{2,1,0:T(8,128)(2,1)S(1)}, u32[]{:S(2)}, u32[]{:S(2)}) collective-permute-start(bf16[8,128,128]{2,1,0:T(8,128)(2,1)S(1)} %copy-done.29), channel_id=1, source_target_pairs={{0,64},{16,80},{32,96},{48,112},{64,0},{80,16},{96,32},{112,48},{1... | collective-permute-start | bytes 786440 | tf_op jit(solution)/shard_map/ppermute | solution.py:265
  89.0 0.0 collective-permute-start.16
  89.0 1.1 collective-permute-start.17
  90.1 4.0 %collective-permute-done.14.refs_1_ = bf16[8,128,128]{2,1,0:T(8,128)(2,1)S(1)} collective-permute-done((bf16[8,128,128]{2,1,0:T(8,128)(2,1)S(1)}, bf16[8,128,128]{2,1,0:T(8,128)(2,1)S(1)}, u32[]{:S(2)}, u32[]{:S(2)}) %collective-permute-start.14) | collective-permute-done | bytes 262176 | tf_op jit(solution)/shard_map/ppermute | solution.py:265
  94.1 1.3 collective-permute-start.18
  95.4 5.4 %collective-permute-done.15.refs_2_ = bf16[8,128,128]{2,1,0:T(8,128)(2,1)S(1)} collective-permute-done((bf16[8,128,128]{2,1,0:T(8,128)(2,1)S(1)}, bf16[8,128,128]{2,1,0:T(8,128)(2,1)S(1)}, u32[]{:S(2)}, u32[]{:S(2)}) %collective-permute-start.15) | collective-permute-done | bytes 262176 | tf_op jit(solution)/shard_map/ppermute | solution.py:265
  100.8 1.1 collective-permute-start.19
  101.9 0.1 collective-permute-start.20
  102.0 1.0 collective-permute-done.19.refs_6_
  103.0 0.4 collective-permute-done.20.refs_7_
  103.5 0.3 copy-done.17
  103.8 0.4 copy-done.18
  104.1 12.3 %row_part.3.refs_3_ = f32[32,128,128]{2,1,0:T(8,128)} custom-call(s32[8,32]{1,0:T(8,128)} %fusion.4.slot, f32[8,32]{1,0:T(8,128)} %bitcast.39, s32[32]{0:T(128)} %sizes.9, f32[32]{0:T(128)} %shift.7, f32[32,128]{1,0:T(8,128)} %eps.7, f32[128,32]{1,0:T(8,128)} %bitcast.30, bf16[8,128,128]{2,1,0:T(8,128)(2,1)} %get-tuple-element.20.refs_0_, ...), custom_call_target="tpu_custom_call" | custom-call | flops 2147483648 | bytes 16777216 | tf_op jit(solution)/shard_map/row_part/pallas_call | solution.py:168
  116.4 1.0 copy-done.1
  117.4 12.4 %col_part.3 = (f32[32,128,128]{2,1,0:T(8,128)}, f32[32,128,128]{2,1,0:T(8,128)}) custom-call(s32[8,32]{1,0:T(8,128)} %bitcast.35, f32[8,32]{1,0:T(8,128)} %bitcast.37, s32[32]{0:T(128)} %sizes.9, f32[32]{0:T(128)} %shift.7, f32[32,128]{1,0:T(8,128)} %eps.7, f32[128,32]{1,0:T(8,128)} %bitcast.31, bf16[32,8,128,128]{3,2,1,0:T(8,128)(2,1)} %refs_0_.3, ...), custom_call_target="tpu_custom_call" | custom-call | flops 2147483648 | bytes 16777216 | tf_op jit(solution)/shard_map/col_part/pallas_call | solution.py:240
  (60 shorter events, 0.1 us)
Async XLA Ops:
  1.9 19.1 %all-to-all-start = ((s32[16,1,128]{2,1,0:T(1,128)}), s32[16,1,128]{2,1,0:T(1,128)S(1)}, u32[]{:S(2)}, u32[]{:S(2)}) async-start(s32[16,1,128]{2,1,0:T(1,128)} %spread_wants.1), calls=%async_computation | async-start | bytes 16384 | tf_op jit(solution)/shard_map/all_to_all | solution.py:296
  9.5 39.5 %copy-start.2 = (f32[32,128]{1,0:T(8,128)S(1)}, f32[32,128]{1,0:T(8,128)}, u32[]{:S(2)}) copy-start(f32[32,128]{1,0:T(8,128)} %eps.7) | copy-start | bytes 49156
  9.5 40.2 %copy-start.20 = (s32[32,8]{0,1:T(8,128)S(1)}, s32[32,8]{0,1:T(8,128)}, u32[]{:S(2)}) copy-start(s32[32,8]{0,1:T(8,128)} %param.23) | copy-start | bytes 3076
  9.5 10.4 %collective-permute-start.3 = (s32[1,1,32]{2,1,0:T(1,128)}, s32[1,1,32]{2,1,0:T(1,128)S(1)}, u32[]{:S(2)}, u32[]{:S(2)}) collective-permute-start(s32[1,1,32]{2,1,0:T(1,128)} %refs_1_.1), channel_id=1, source_target_pairs={{0,16},{16,0},{32,48},{48,32},{64,80},{80,64},{96,112},{112,96},{1... | collective-permute-start | bytes 392 | tf_op jit(solution)/shard_map/ppermute | solution.py:261
  10.6 4.6 %collective-permute-start.2 = (s32[1,1,32]{2,1,0:T(1,128)}, s32[1,1,32]{2,1,0:T(1,128)S(1)}, u32[]{:S(2)}, u32[]{:S(2)}) collective-permute-start(s32[1,1,32]{2,1,0:T(1,128)} %refs_1_.1), channel_id=1, source_target_pairs={{0,96},{16,112},{32,0},{48,16},{64,32},{80,48},{96,64},{112,80},{1... | collective-permute-start | bytes 392 | tf_op jit(solution)/shard_map/ppermute | solution.py:265
  14.3 4.0 %collective-permute-start.1 = (s32[1,1,32]{2,1,0:T(1,128)}, s32[1,1,32]{2,1,0:T(1,128)S(1)}, u32[]{:S(2)}, u32[]{:S(2)}) collective-permute-start(s32[1,1,32]{2,1,0:T(1,128)} %refs_1_.1), channel_id=1, source_target_pairs={{0,64},{16,80},{32,96},{48,112},{64,0},{80,16},{96,32},{112,48},{1... | collective-permute-start | bytes 392 | tf_op jit(solution)/shard_map/ppermute | solution.py:265
  14.3 5.5 %collective-permute-start = (s32[1,1,32]{2,1,0:T(1,128)}, s32[1,1,32]{2,1,0:T(1,128)S(1)}, u32[]{:S(2)}, u32[]{:S(2)}) collective-permute-start(s32[1,1,32]{2,1,0:T(1,128)} %refs_1_.1), channel_id=1, source_target_pairs={{0,32},{16,48},{32,64},{48,80},{64,96},{80,112},{96,0},{112,16},{1... | collective-permute-start | bytes 392 | tf_op jit(solution)/shard_map/ppermute | solution.py:265
  15.2 5.8 %copy-start.22 = (s32[1,1,32]{2,1,0:T(1,128)}, s32[1,1,32]{2,1,0:T(1,128)S(1)}, u32[]{:S(2)}) copy-start(s32[1,1,32]{2,1,0:T(1,128)S(1)} %collective-permute-done.2.refs_3_.refs_4_) | copy-start | bytes 388
  15.2 4.8 %collective-permute-start.6 = (s32[1,1,32]{2,1,0:T(1,128)S(1)}, s32[1,1,32]{2,1,0:T(1,128)S(1)}, u32[]{:S(2)}, u32[]{:S(2)}) collective-permute-start(s32[1,1,32]{2,1,0:T(1,128)S(1)} %collective-permute-done.2.refs_3_.refs_4_), channel_id=1, source_target_pairs={{0,16},{16,0},{32,48},{48,32},{64,80},{80,64},{96,112},{112,96},{1... | collective-permute-start | bytes 392 | tf_op jit(solution)/shard_map/ppermute | solution.py:261
  18.4 2.6 %copy-start.23 = (s32[1,1,32]{2,1,0:T(1,128)}, s32[1,1,32]{2,1,0:T(1,128)S(1)}, u32[]{:S(2)}) copy-start(s32[1,1,32]{2,1,0:T(1,128)S(1)} %collective-permute-done.1.refs_2_.refs_3_) | copy-start | bytes 388
  18.4 2.3 %collective-permute-start.5 = (s32[1,1,32]{2,1,0:T(1,128)S(1)}, s32[1,1,32]{2,1,0:T(1,128)S(1)}, u32[]{:S(2)}, u32[]{:S(2)}) collective-permute-start(s32[1,1,32]{2,1,0:T(1,128)S(1)} %collective-permute-done.1.refs_2_.refs_3_), channel_id=1, source_target_pairs={{0,16},{16,0},{32,48},{48,32},{64,80},{80,64},{96,112},{112,96},{1... | collective-permute-start | bytes 392 | tf_op jit(solution)/shard_map/ppermute | solution.py:261
  19.9 1.1 copy-start.24
  19.9 1.1 collective-permute-start.4
  20.0 1.1 copy-start.21
  20.0 1.1 copy-start.25
  20.7 0.6 copy-start.26
  21.0 0.5 copy-start.27
  21.5 0.6 copy-start.19
  25.6 7.1 %copy-start.33 = (bf16[8,128,128]{2,1,0:T(8,128)(2,1)S(1)}, bf16[8,128,128]{2,1,0:T(8,128)(2,1)}, u32[]{:S(2)}) copy-start(bf16[8,128,128]{2,1,0:T(8,128)(2,1)} %get-tuple-element.15) | copy-start | bytes 786436
  25.6 7.2 %copy-start.32 = (bf16[8,128,128]{2,1,0:T(8,128)(2,1)S(1)}, bf16[8,128,128]{2,1,0:T(8,128)(2,1)}, u32[]{:S(2)}) copy-start(bf16[8,128,128]{2,1,0:T(8,128)(2,1)} %get-tuple-element.16) | copy-start | bytes 786436
  25.6 8.7 %copy-start.30 = (bf16[8,128,128]{2,1,0:T(8,128)(2,1)S(1)}, bf16[8,128,128]{2,1,0:T(8,128)(2,1)}, u32[]{:S(2)}) copy-start(bf16[8,128,128]{2,1,0:T(8,128)(2,1)} %get-tuple-element.17) | copy-start | bytes 786436
  25.6 10.7 %copy-start.3 = (bf16[8,128,128]{2,1,0:T(8,128)(2,1)S(1)}, bf16[8,128,128]{2,1,0:T(8,128)(2,1)}, u32[]{:S(2)}) copy-start(bf16[8,128,128]{2,1,0:T(8,128)(2,1)} %get-tuple-element.14.refs_0_) | copy-start | bytes 786436
  25.6 37.9 %all-to-all-start.1 = ((bf16[16,2,128,128]{3,2,1,0:T(8,128)(2,1)}), bf16[16,2,128,128]{3,2,1,0:T(8,128)(2,1)S(1)}, u32[]{:S(2)}, u32[]{:S(2)}) async-start(bf16[16,2,128,128]{3,2,1,0:T(8,128)(2,1)} %bitcast.32), calls=%async_computation.1 | async-start | bytes 2097152 | tf_op jit(solution)/shard_map/all_to_all | solution.py:303
  32.7 14.3 %collective-permute-start.7 = (bf16[8,128,128]{2,1,0:T(8,128)(2,1)S(1)}, bf16[8,128,128]{2,1,0:T(8,128)(2,1)S(1)}, u32[]{:S(2)}, u32[]{:S(2)}) collective-permute-start(bf16[8,128,128]{2,1,0:T(8,128)(2,1)S(1)} %copy-done.33), channel_id=1, source_target_pairs={{0,32},{16,48},{32,64},{48,80},{64,96},{80,112},{96,0},{112,16},{1... | collective-permute-start | bytes 786440 | tf_op jit(solution)/shard_map/ppermute | solution.py:265
  32.8 15.5 %collective-permute-start.8 = (bf16[8,128,128]{2,1,0:T(8,128)(2,1)S(1)}, bf16[8,128,128]{2,1,0:T(8,128)(2,1)S(1)}, u32[]{:S(2)}, u32[]{:S(2)}) collective-permute-start(bf16[8,128,128]{2,1,0:T(8,128)(2,1)S(1)} %copy-done.32), channel_id=1, source_target_pairs={{0,64},{16,80},{32,96},{48,112},{64,0},{80,16},{96,32},{112,48},{1... | collective-permute-start | bytes 786440 | tf_op jit(solution)/shard_map/ppermute | solution.py:265
  34.3 14.1 %collective-permute-start.9 = (bf16[8,128,128]{2,1,0:T(8,128)(2,1)S(1)}, bf16[8,128,128]{2,1,0:T(8,128)(2,1)S(1)}, u32[]{:S(2)}, u32[]{:S(2)}) collective-permute-start(bf16[8,128,128]{2,1,0:T(8,128)(2,1)S(1)} %copy-done.30), channel_id=1, source_target_pairs={{0,96},{16,112},{32,0},{48,16},{64,32},{80,48},{96,64},{112,80},{1... | collective-permute-start | bytes 786440 | tf_op jit(solution)/shard_map/ppermute | solution.py:265
  36.3 14.0 %collective-permute-start.10 = (bf16[8,128,128]{2,1,0:T(8,128)(2,1)S(1)}, bf16[8,128,128]{2,1,0:T(8,128)(2,1)S(1)}, u32[]{:S(2)}, u32[]{:S(2)}) collective-permute-start(bf16[8,128,128]{2,1,0:T(8,128)(2,1)S(1)} %copy-done.3), channel_id=1, source_target_pairs={{0,16},{16,0},{32,48},{48,32},{64,80},{80,64},{96,112},{112,96},{1... | collective-permute-start | bytes 786440 | tf_op jit(solution)/shard_map/ppermute | solution.py:261
  47.0 3.4 %copy-start.4 = (bf16[8,128,128]{2,1,0:T(8,128)(2,1)}, bf16[8,128,128]{2,1,0:T(8,128)(2,1)S(1)}, u32[]{:S(2)}) copy-start(bf16[8,128,128]{2,1,0:T(8,128)(2,1)S(1)} %collective-permute-done.7.refs_1_) | copy-start | bytes 786436
  47.0 3.3 %collective-permute-start.11 = (bf16[8,128,128]{2,1,0:T(8,128)(2,1)S(1)}, bf16[8,128,128]{2,1,0:T(8,128)(2,1)S(1)}, u32[]{:S(2)}, u32[]{:S(2)}) collective-permute-start(bf16[8,128,128]{2,1,0:T(8,128)(2,1)S(1)} %collective-permute-done.7.refs_1_), channel_id=1, source_target_pairs={{0,16},{16,0},{32,48},{48,32},{64,80},{80,64},{96,112},{112,96},{1... | collective-permute-start | bytes 786440 | tf_op jit(solution)/shard_map/ppermute | solution.py:261
  48.4 2.0 %copy-start.5 = (bf16[8,128,128]{2,1,0:T(8,128)(2,1)}, bf16[8,128,128]{2,1,0:T(8,128)(2,1)S(1)}, u32[]{:S(2)}) copy-start(bf16[8,128,128]{2,1,0:T(8,128)(2,1)S(1)} %collective-permute-done.8.refs_2_) | copy-start | bytes 786436
  48.4 2.0 %collective-permute-start.12 = (bf16[8,128,128]{2,1,0:T(8,128)(2,1)S(1)}, bf16[8,128,128]{2,1,0:T(8,128)(2,1)S(1)}, u32[]{:S(2)}, u32[]{:S(2)}) collective-permute-start(bf16[8,128,128]{2,1,0:T(8,128)(2,1)S(1)} %collective-permute-done.8.refs_2_), channel_id=1, source_target_pairs={{0,16},{16,0},{32,48},{48,32},{64,80},{80,64},{96,112},{112,96},{1... | collective-permute-start | bytes 786440 | tf_op jit(solution)/shard_map/ppermute | solution.py:261
  48.5 1.9 %copy-start.6 = (bf16[8,128,128]{2,1,0:T(8,128)(2,1)}, bf16[8,128,128]{2,1,0:T(8,128)(2,1)S(1)}, u32[]{:S(2)}) copy-start(bf16[8,128,128]{2,1,0:T(8,128)(2,1)S(1)} %collective-permute-done.9.refs_3_) | copy-start | bytes 786436
  48.5 1.9 %collective-permute-start.13 = (bf16[8,128,128]{2,1,0:T(8,128)(2,1)S(1)}, bf16[8,128,128]{2,1,0:T(8,128)(2,1)S(1)}, u32[]{:S(2)}, u32[]{:S(2)}) collective-permute-start(bf16[8,128,128]{2,1,0:T(8,128)(2,1)S(1)} %collective-permute-done.9.refs_3_), channel_id=1, source_target_pairs={{0,16},{16,0},{32,48},{48,32},{64,80},{80,64},{96,112},{112,96},{1... | collective-permute-start | bytes 786440 | tf_op jit(solution)/shard_map/ppermute | solution.py:261
  50.3 0.7 copy-start.7
  50.3 0.8 copy-start.8
  50.3 0.9 copy-start.9
  50.4 0.9 copy-start.10
  63.6 1.0 copy-start
  78.5 6.9 %copy-start.31 = (bf16[8,128,128]{2,1,0:T(8,128)(2,1)S(1)}, bf16[8,128,128]{2,1,0:T(8,128)(2,1)}, u32[]{:S(2)}) copy-start(bf16[8,128,128]{2,1,0:T(8,128)(2,1)} %get-tuple-element.21) | copy-start | bytes 786436
  78.6 7.7 %copy-start.29 = (bf16[8,128,128]{2,1,0:T(8,128)(2,1)S(1)}, bf16[8,128,128]{2,1,0:T(8,128)(2,1)}, u32[]{:S(2)}) copy-start(bf16[8,128,128]{2,1,0:T(8,128)(2,1)} %get-tuple-element.22) | copy-start | bytes 786436
  78.6 10.4 %copy-start.28 = (bf16[8,128,128]{2,1,0:T(8,128)(2,1)S(1)}, bf16[8,128,128]{2,1,0:T(8,128)(2,1)}, u32[]{:S(2)}) copy-start(bf16[8,128,128]{2,1,0:T(8,128)(2,1)} %get-tuple-element.23) | copy-start | bytes 786436
  78.6 10.4 %copy-start.11 = (bf16[8,128,128]{2,1,0:T(8,128)(2,1)S(1)}, bf16[8,128,128]{2,1,0:T(8,128)(2,1)}, u32[]{:S(2)}) copy-start(bf16[8,128,128]{2,1,0:T(8,128)(2,1)} %get-tuple-element.20.refs_0_) | copy-start | bytes 786436
  78.6 37.8 %all-to-all-start.2 = ((bf16[16,2,128,128]{3,2,1,0:T(8,128)(2,1)}), bf16[16,2,128,128]{3,2,1,0:T(8,128)(2,1)S(1)}, u32[]{:S(2)}, u32[]{:S(2)}) async-start(bf16[16,2,128,128]{3,2,1,0:T(8,128)(2,1)} %bitcast.33), calls=%async_computation.2 | async-start | bytes 2097152 | tf_op jit(solution)/shard_map/all_to_all | solution.py:303
  85.4 8.7 %collective-permute-start.14 = (bf16[8,128,128]{2,1,0:T(8,128)(2,1)S(1)}, bf16[8,128,128]{2,1,0:T(8,128)(2,1)S(1)}, u32[]{:S(2)}, u32[]{:S(2)}) collective-permute-start(bf16[8,128,128]{2,1,0:T(8,128)(2,1)S(1)} %copy-done.31), channel_id=1, source_target_pairs={{0,32},{16,48},{32,64},{48,80},{64,96},{80,112},{96,0},{112,16},{1... | collective-permute-start | bytes 786440 | tf_op jit(solution)/shard_map/ppermute | solution.py:265
  86.3 14.5 %collective-permute-start.15 = (bf16[8,128,128]{2,1,0:T(8,128)(2,1)S(1)}, bf16[8,128,128]{2,1,0:T(8,128)(2,1)S(1)}, u32[]{:S(2)}, u32[]{:S(2)}) collective-permute-start(bf16[8,128,128]{2,1,0:T(8,128)(2,1)S(1)} %copy-done.29), channel_id=1, source_target_pairs={{0,64},{16,80},{32,96},{48,112},{64,0},{80,16},{96,32},{112,48},{1... | collective-permute-start | bytes 786440 | tf_op jit(solution)/shard_map/ppermute | solution.py:265
  89.0 12.9 %collective-permute-start.16 = (bf16[8,128,128]{2,1,0:T(8,128)(2,1)S(1)}, bf16[8,128,128]{2,1,0:T(8,128)(2,1)S(1)}, u32[]{:S(2)}, u32[]{:S(2)}) collective-permute-start(bf16[8,128,128]{2,1,0:T(8,128)(2,1)S(1)} %copy-done.28), channel_id=1, source_target_pairs={{0,96},{16,112},{32,0},{48,16},{64,32},{80,48},{96,64},{112,80},{1... | collective-permute-start | bytes 786440 | tf_op jit(solution)/shard_map/ppermute | solution.py:265
  89.0 13.0 %collective-permute-start.17 = (bf16[8,128,128]{2,1,0:T(8,128)(2,1)S(1)}, bf16[8,128,128]{2,1,0:T(8,128)(2,1)S(1)}, u32[]{:S(2)}, u32[]{:S(2)}) collective-permute-start(bf16[8,128,128]{2,1,0:T(8,128)(2,1)S(1)} %copy-done.11), channel_id=1, source_target_pairs={{0,16},{16,0},{32,48},{48,32},{64,80},{80,64},{96,112},{112,96},{1... | collective-permute-start | bytes 786440 | tf_op jit(solution)/shard_map/ppermute | solution.py:261
  94.1 9.3 %copy-start.12 = (bf16[8,128,128]{2,1,0:T(8,128)(2,1)}, bf16[8,128,128]{2,1,0:T(8,128)(2,1)S(1)}, u32[]{:S(2)}) copy-start(bf16[8,128,128]{2,1,0:T(8,128)(2,1)S(1)} %collective-permute-done.14.refs_1_) | copy-start | bytes 786436
  94.1 7.9 %collective-permute-start.18 = (bf16[8,128,128]{2,1,0:T(8,128)(2,1)S(1)}, bf16[8,128,128]{2,1,0:T(8,128)(2,1)S(1)}, u32[]{:S(2)}, u32[]{:S(2)}) collective-permute-start(bf16[8,128,128]{2,1,0:T(8,128)(2,1)S(1)} %collective-permute-done.14.refs_1_), channel_id=1, source_target_pairs={{0,16},{16,0},{32,48},{48,32},{64,80},{80,64},{96,112},{112,96},{1... | collective-permute-start | bytes 786440 | tf_op jit(solution)/shard_map/ppermute | solution.py:261
  100.8 2.7 %copy-start.13 = (bf16[8,128,128]{2,1,0:T(8,128)(2,1)}, bf16[8,128,128]{2,1,0:T(8,128)(2,1)S(1)}, u32[]{:S(2)}) copy-start(bf16[8,128,128]{2,1,0:T(8,128)(2,1)S(1)} %collective-permute-done.15.refs_2_) | copy-start | bytes 786436
  100.8 2.3 %collective-permute-start.19 = (bf16[8,128,128]{2,1,0:T(8,128)(2,1)S(1)}, bf16[8,128,128]{2,1,0:T(8,128)(2,1)S(1)}, u32[]{:S(2)}, u32[]{:S(2)}) collective-permute-start(bf16[8,128,128]{2,1,0:T(8,128)(2,1)S(1)} %collective-permute-done.15.refs_2_), channel_id=1, source_target_pairs={{0,16},{16,0},{32,48},{48,32},{64,80},{80,64},{96,112},{112,96},{1... | collective-permute-start | bytes 786440 | tf_op jit(solution)/shard_map/ppermute | solution.py:261
  101.9 1.5 %copy-start.14 = (bf16[8,128,128]{2,1,0:T(8,128)(2,1)}, bf16[8,128,128]{2,1,0:T(8,128)(2,1)S(1)}, u32[]{:S(2)}) copy-start(bf16[8,128,128]{2,1,0:T(8,128)(2,1)S(1)} %collective-permute-done.16.refs_3_) | copy-start | bytes 786436
  101.9 1.5 %collective-permute-start.20 = (bf16[8,128,128]{2,1,0:T(8,128)(2,1)S(1)}, bf16[8,128,128]{2,1,0:T(8,128)(2,1)S(1)}, u32[]{:S(2)}, u32[]{:S(2)}) collective-permute-start(bf16[8,128,128]{2,1,0:T(8,128)(2,1)S(1)} %collective-permute-done.16.refs_3_), channel_id=1, source_target_pairs={{0,16},{16,0},{32,48},{48,32},{64,80},{80,64},{96,112},{112,96},{1... | collective-permute-start | bytes 786440 | tf_op jit(solution)/shard_map/ppermute | solution.py:261
  102.0 1.5 %copy-start.15 = (bf16[8,128,128]{2,1,0:T(8,128)(2,1)}, bf16[8,128,128]{2,1,0:T(8,128)(2,1)S(1)}, u32[]{:S(2)}) copy-start(bf16[8,128,128]{2,1,0:T(8,128)(2,1)S(1)} %collective-permute-done.17.refs_4_) | copy-start | bytes 786436
  102.0 1.5 %copy-start.16 = (bf16[8,128,128]{2,1,0:T(8,128)(2,1)}, bf16[8,128,128]{2,1,0:T(8,128)(2,1)S(1)}, u32[]{:S(2)}) copy-start(bf16[8,128,128]{2,1,0:T(8,128)(2,1)S(1)} %collective-permute-done.18.refs_5_) | copy-start | bytes 786436
  103.0 0.7 copy-start.17
  103.4 0.7 copy-start.18
  116.4 1.0 copy-start.1
where the time goes:
time: 131 us; the launch traced here: 130 us
  Pallas kernels  55.7 us (43%)
  starting transfers between devices  43.6 us (33%)
  waiting for transfers between devices  23.5 us (18%)
  local copies, waits for them, and re-layouts  5.41 us (4%)
    pallas_call x2, Pallas kernels, col_part(): pl.pallas_call(functools.partial(col_body, first), in_specs=[SMEM] * 4 +...  26.4 us
    pallas_call x2, Pallas kernels, row_part(): pl.pallas_call(functools.partial(row_body, first), in_specs=[SMEM] * 4 +...  24.5 us
    ppermute x9, waiting for transfers between devices, shift_z(): return lax.ppermute(x, 'row', [(i, (i + 2 * dz) % 8) for i in range(8)])  21 us
    all_to_all x2, starting transfers between devices, shards(): lax.all_to_all(out[0].reshape(16, 2, W, W), 'col', 0, 0, tiled=True)  13.9 us
    ppermute x9, starting transfers between devices, shift_z(): return lax.ppermute(x, 'row', [(i, (i + 2 * dz) % 8) for i in range(8)])  11.6 us
    ppermute x12, starting transfers between devices, swap_core(): return lax.ppermute(x, 'row', [(i, i ^ 1) for i in range(8)])  10.5 us
    all_to_all x1, starting transfers between devices, shards(): col_asked = lax.all_to_all(spread_wants(col_wants), 'col', 0, 0, tiled=True)  7.58 us
    unnamed x69, local copies, waits for them, and re-layouts  5.41 us
  transfers between devices with their start and end apart: 24, of which 9 were waited for; matrix products, arithmetic and copies ran while one was open for 1% of the time, Pallas kernels for 19%

commit v1 on v0

v1 whole, which is shorter than its diff:
```python
import functools

import jax
import jax.numpy as jnp
from jax import lax
from jax.experimental import pallas as pl
from jax.experimental.pallas import tpu as pltpu
from jax.sharding import PartitionSpec as P

F32 = jnp.float32
BF16 = jnp.bfloat16
W = 128
PAIRS = 32
NK = 8
CUTS = (0, 4, 12, 20, 28, 32)
CHUNKS = len(CUTS) - 1
AHEAD = 2
NZ = 4
ANY = pl.BlockSpec(memory_space=pl.ANY)
SMEM = pl.BlockSpec(memory_space=pltpu.SMEM)
VMEM = pl.BlockSpec(memory_space=pltpu.VMEM)


def live(size):
    rows = lax.broadcasted_iota(jnp.int32, (W, W), 0) < size
    lanes = lax.broadcasted_iota(jnp.int32, (W, W), 1) < size
    return jnp.logical_and(rows, lanes)


def spread_body(wants, out):
    lane = lax.broadcasted_iota(jnp.int32, (1, W), 1)
    for q in range(out.shape[0]):
        out[q] = jnp.where(lane == 0, wants[0, 0, 2 * q], wants[0, 0, 2 * q + 1])


def spread_wants(col_wants):
    return pl.pallas_call(
        spread_body,
        in_specs=[SMEM],
        out_specs=VMEM,
        out_shape=jax.ShapeDtypeStruct((16, 1, W), jnp.int32),
        name="spread_wants",
    )(col_wants)


def start_outgoing(rounded, col_asked, lists, out_col, out_row, sems):
    me = lax.axis_index("row")
    copies = []
    for dz in range(NZ):
        back = (NZ - dz) % NZ
        for part in range(2):
            for e in range(4):
                wanted = lists[4 * part + back][0, 0, 4 * me + e]
                spot = 4 * part + e
                copies.append(pltpu.make_async_copy(rounded.at[wanted], out_row[dz].at[spot], sems.at[8 * dz + spot]))
    for k in range(PAIRS):
        wanted = col_asked[k // 2, 0, k % 2]
        copies.append(pltpu.make_async_copy(rounded.at[wanted], out_col.at[k], sems.at[PAIRS + k]))
    for copy in copies:
        copy.start()
    return copies


def first_body(sizes, col_asked, *refs):
    lists, amp, out_col, out_row, rounded, sems = refs[:8], refs[8], refs[9], refs[10:14], refs[14], refs[15]

    def step(p, carry):
        rounded[p] = jnp.where(live(sizes[p]), amp[p], 0.0).astype(BF16)
        return carry

    lax.fori_loop(0, PAIRS, step, 0, unroll=4)
    for copy in start_outgoing(rounded, col_asked, lists, out_col, out_row, sems):
        copy.wait()


OUTGOING = [jax.ShapeDtypeStruct((PAIRS, W, W), BF16)] + [jax.ShapeDtypeStruct((8, W, W), BF16)] * NZ


def first_outgoing(sizes, asked, amp_start):
    return pl.pallas_call(
        first_body,
        in_specs=[SMEM] + [SMEM] * 9 + [VMEM],
        out_specs=[ANY] * 5,
        out_shape=OUTGOING,
        scratch_shapes=[pltpu.VMEM((PAIRS, W, W), BF16), pltpu.SemaphoreType.DMA((2 * PAIRS,))],
        compiler_params=pltpu.CompilerParams(vmem_limit_bytes=60 * 2**20),
        name="first_outgoing",
    )(sizes, *asked, amp_start)


def dot(a, b):
    return jnp.dot(a, b, preferred_element_type=F32)


def dot_t(a, b):
    return lax.dot_general(a, b, (((1,), (1,)), ((), ())), preferred_element_type=F32)


def two_halves(over, table, slot, fock, p, j, zero, lane):
    a, b = 2 * j, 2 * j + 1
    left = jnp.concatenate([over[p, a], over[p, b]], 1)
    blocks = jnp.concatenate(
        [
            jnp.concatenate([table[slot[a, p]], zero], 1),
            jnp.concatenate([zero, table[slot[b, p]]], 1),
        ],
        0,
    )
    return (dot(left, blocks) * jnp.where(lane < W, fock[a, p], fock[b, p])).astype(BF16)


def all_pairs(over, table, slot, fock, ready, finish):
    zero = jnp.zeros((W, W), BF16)
    lane = lax.broadcasted_iota(jnp.int32, (W, 2 * W), 1)
    halves = None
    for p in range(PAIRS + 1):
        if p < PAIRS:
            if p in CUTS:
                ready(CUTS.index(p))
            following = [two_halves(over, table, slot, fock, p, j, zero, lane) for j in range(NK // 2)]
        if p > 0:
            right = jnp.concatenate([over[p - 1, s] for s in range(NK)], 1)
            finish(p - 1, dot_t(jnp.concatenate(halves, 1), right))
        halves = following


def chunk_copy(src, dst, sem, c):
    part = pl.ds(CUTS[c], CUTS[c + 1] - CUTS[c])
    return pltpu.make_async_copy(src.at[part], dst.at[part], sem.at[c])


def row_body(first, slot, fock, sizes, shift, eps, *refs):
    pieces, refs = refs[:8], refs[8:]
    over_h, amp_h, exch_h, refs = refs[0], refs[1], refs[2], refs[3:]
    base_h, refs = refs[0], refs[1:]
    over, table, amp, exch, base, table_sem, over_sem, amp_sem, exch_sem, base_sem = refs
    me = lax.axis_index("row")
    core = lax.rem(me, 2)
    loads = []
    for dz in range(NZ):
        chip = 8 * lax.rem(me // 2 + NZ - dz, NZ)
        for part, from_core in ((0, core), (1, 1 - core)):
            source = pieces[NZ * part + dz].at[pl.ds(4 * part, 4)]
            loads.append(pltpu.make_async_copy(source, table.at[pl.ds(chip + 4 * from_core, 4)], table_sem.at[NZ * part + dz]))
    for copy in loads:
        copy.start()
    def fetch(c):
        chunk_copy(over_h, over, over_sem, c).start()
        chunk_copy(amp_h, amp, amp_sem, c).start()
        chunk_copy(exch_h, exch, exch_sem, c).start()

    for c in range(AHEAD):
        fetch(c)
    eps_t = jnp.transpose(eps[...])
    for copy in loads:
        copy.wait()

    def ready(c):
        if c + AHEAD < CHUNKS:
            fetch(c + AHEAD)
        chunk_copy(over_h, over, over_sem, c).wait()
        chunk_copy(amp_h, amp, amp_sem, c).wait()
        chunk_copy(exch_h, exch, exch_sem, c).wait()

    def finish(p, coupling):
        here = amp[p]
        if first:
            here = jnp.where(live(sizes[p]), here, 0.0)
        denominator = eps_t[:, p : p + 1] + eps[p : p + 1, :] - shift[p]
        base[p] = exch[p] + denominator * here - coupling
        if p + 1 in CUTS:
            chunk_copy(base, base_h, base_sem, CUTS.index(p + 1) - 1).start()

    all_pairs(over, table, slot, fock, ready, finish)
    for c in range(CHUNKS):
        chunk_copy(base, base_h, base_sem, c).wait()


def chunked(dtype=F32):
    return pltpu.VMEM((PAIRS, W, W), dtype)


FLOPS = 2 * 2 * 256 * W * W * W


def cost(times):
    return pl.CostEstimate(flops=times * FLOPS, bytes_accessed=16 * 2**20, transcendentals=0)


def row_part(first, slot, fock, sizes, shift, eps, pieces, over, amp, exch):
    return pl.pallas_call(
        functools.partial(row_body, first),
        in_specs=[SMEM] * 4 + [VMEM] + [ANY] * 11,
        out_specs=ANY,
        out_shape=jax.ShapeDtypeStruct((PAIRS, W, W), F32),
        scratch_shapes=[
            pltpu.VMEM((PAIRS, NK, W, W), BF16),
            chunked(BF16),
            chunked(),
            chunked(),
            chunked(),
            pltpu.SemaphoreType.DMA((8,)),
        ]
        + [pltpu.SemaphoreType.DMA((CHUNKS,))] * 4,
        compiler_params=pltpu.CompilerParams(vmem_limit_bytes=60 * 2**20),
        cost_estimate=cost(12),
        name="row_part",
    )(slot, fock, sizes, shift, eps, *pieces, over, amp, exch)


def col_body(first, slot, fock, sizes, shift, eps, *refs):
    if first:
        col_asked, lists, refs = refs[0], refs[1:9], refs[9:]
    over_h, table_h, amp_h, base_h, refs = refs[0], refs[1], refs[2], refs[3], refs[4:]
    amp_out, refs = refs[0], refs[1:]
    if first:
        out_col, out_row, refs = refs[0], refs[1:5], refs[5:]
    else:
        third_out, refs = refs[0], refs[1:]
    over, table, amp, base, third, table_sem, over_sem, amp_sem, base_sem, amp_out_sem, third_sem, sems = refs
    load = pltpu.make_async_copy(table_h, table, table_sem)
    load.start()
    def fetch(c):
        chunk_copy(over_h, over, over_sem, c).start()
        chunk_copy(amp_h, amp, amp_sem, c).start()
        chunk_copy(base_h, base, base_sem, c).start()

    for c in range(AHEAD):
        fetch(c)
    eps_t = jnp.transpose(eps[...])
    load.wait()

    def ready(c):
        if c + AHEAD < CHUNKS:
            fetch(c + AHEAD)
        chunk_copy(over_h, over, over_sem, c).wait()
        chunk_copy(amp_h, amp, amp_sem, c).wait()
        chunk_copy(base_h, base, base_sem, c).wait()

    def finish(p, coupling):
        here = amp[p]
        alive = live(sizes[p])
        if first:
            here = jnp.where(alive, here, 0.0)
        denominator = eps_t[:, p : p + 1] + eps[p : p + 1, :] - shift[p]
        residual = jnp.where(alive, base[p] - coupling, 0.0)
        new = here - residual / denominator
        amp[p] = new
        if first:
            third[p] = new.astype(BF16)
        else:
            third[p] = residual
        if p + 1 in CUTS:
            chunk_copy(amp, amp_out, amp_out_sem, CUTS.index(p + 1) - 1).start()
            if not first:
                chunk_copy(third, third_out, third_sem, CUTS.index(p + 1) - 1).start()

    all_pairs(over, table, slot, fock, ready, finish)
    if first:
        for copy in start_outgoing(third, col_asked, lists, out_col, out_row, sems):
            copy.wait()
    for c in range(CHUNKS):
        chunk_copy(amp, amp_out, amp_out_sem, c).wait()
        if not first:
            chunk_copy(third, third_out, third_sem, c).wait()


def col_part(first, slot, fock, sizes, shift, eps, asked, over, table, amp, base):
    whole = jax.ShapeDtypeStruct((PAIRS, W, W), F32)
    return pl.pallas_call(
        functools.partial(col_body, first),
        in_specs=[SMEM] * 4 + [VMEM] + [SMEM] * len(asked) + [ANY] * 4,
        out_specs=[ANY] * 6 if first else [ANY] * 2,
        out_shape=[whole] + OUTGOING if first else [whole] * 2,
        scratch_shapes=[
            pltpu.VMEM((PAIRS, NK, W, W), BF16),
            chunked(BF16),
            chunked(),
            chunked(),
            chunked(BF16 if first else F32),
            pltpu.SemaphoreType.DMA,
        ]
        + [pltpu.SemaphoreType.DMA((CHUNKS,))] * 5
        + [pltpu.SemaphoreType.DMA((2 * PAIRS,))],
        compiler_params=pltpu.CompilerParams(vmem_limit_bytes=60 * 2**20),
        cost_estimate=cost(1),
        name="col_part",
    )(slot, fock, sizes, shift, eps, *asked, over, table, amp, base)


def swap_core(x):
    return lax.ppermute(x, "row", [(i, i ^ 1) for i in range(8)])


def shift_z(x, dz):
    return lax.ppermute(x, "row", [(i, (i + 2 * dz) % 8) for i in range(8)])


def row_exchange(bufs):
    same = [bufs[0]] + [shift_z(bufs[dz], dz) for dz in range(1, NZ)]
    return same + [swap_core(x) for x in same]


def shards(
    amp_start,
    exch_blocks,
    eps_virtual,
    pair_shift,
    pno_sizes,
    over_ik,
    over_kj,
    fock_ik,
    fock_kj,
    ik_slot,
    kj_slot,
    col_wants,
    row_wants,
):
    kj, ik = kj_slot.T, ik_slot.T
    f_ik, f_kj = fock_ik.T, fock_kj.T
    col_asked = lax.all_to_all(spread_wants(col_wants), "col", 0, 0, tiled=True)
    asked = [col_asked] + row_exchange([row_wants] * NZ)
    amp = amp_start
    out = first_outgoing(pno_sizes, asked, amp_start)
    for iteration in range(2):
        first = iteration == 0
        pieces = row_exchange(out[1:])
        table = lax.all_to_all(out[0].reshape(16, 2, W, W), "col", 0, 0, tiled=True).reshape(PAIRS, W, W)
        base = row_part(first, kj, f_ik, pno_sizes, pair_shift, eps_virtual, pieces, over_kj, amp, exch_blocks)
        amp, *out = col_part(
            first, ik, f_kj, pno_sizes, pair_shift, eps_virtual, asked if first else [], over_ik, table, amp, base
        )
    return (amp, out[0])


def solution(mesh):
    placed = (
        P(("row", "col"), None, None),
        P(("row", "col"), None, None),
        P(("row", "col"), None),
        P(("row", "col")),
        P(("row", "col")),
        P(("row", "col"), None, None, None),
        P(("row", "col"), None, None, None),
        P(("row", "col"), None),
        P(("row", "col"), None),
        P(("row", "col"), None),
        P(("row", "col"), None),
        P("row", "col", None),
        P("row", "col", None),
    )
    return jax.shard_map(
        shards,
        mesh=mesh,
        in_specs=placed,
        out_specs=(P(("row", "col"), None, None), P(("row", "col"), None, None)),
        check_vma=False,
    )
```

time: 131 us -> 127 us (0.969)
  Pallas kernels: 55.7 us -> 43.8 us
  waiting for transfers between devices: 23.5 us -> 31.9 us
    all_to_all x2, waiting for transfers between devices: 0.01 us -> 13.4 us  [shards(): lax.all_to_all(out[0].reshape(16, 2, W, W), 'col', 0, 0, tiled=True)]
    pallas_call x2, Pallas kernels: 24.5 us -> 18.4 us  [row_part(): pl.pallas_call(functools.partial(row_body, first), in_specs=[SMEM] * 4 +...]
    pallas_call x2, Pallas kernels: 26.4 us -> 20.4 us  [col_part(): pl.pallas_call(functools.partial(col_body, first), in_specs=[SMEM] * 4 +...]
    ppermute x12, starting transfers between devices: 10.5 us -> 14.5 us  [swap_core(): return lax.ppermute(x, 'row', [(i, i ^ 1) for i in range(8)])]
    ppermute x9, waiting for transfers between devices: 21 us -> 17.5 us  [shift_z(): return lax.ppermute(x, 'row', [(i, (i + 2 * dz) % 8) for i in range(8)])]
    all_to_all x2, starting transfers between devices: 13.9 us -> 10.6 us  [shards(): lax.all_to_all(out[0].reshape(16, 2, W, W), 'col', 0, 0, tiled=True)]
    ppermute x12, waiting for transfers between devices: 2.45 us -> 1.03 us  [swap_core(): return lax.ppermute(x, 'row', [(i, i ^ 1) for i in range(8)])]
    unnamed x69 -> x48, local copies, waits for them, and re-layouts: 5.41 us -> 4.92 us
  transfers between devices with their start and end apart: 24 -> 24, of which waited for: 9 -> 9; matrix products, arithmetic and copies ran while one was open for 1% -> 0% of each run, Pallas kernels for 19% -> 15%
where the time goes in v1:
time: 127 us; the launch traced here: 126 us
  starting transfers between devices  44.3 us (35%)
  Pallas kernels  43.8 us (34%)
  waiting for transfers between devices  31.9 us (25%)
  local copies, waits for them, and re-layouts  4.92 us (4%)
    pallas_call x2, Pallas kernels, col_part(): pl.pallas_call(functools.partial(col_body, first), in_specs=[SMEM] * 4 +...  20.4 us
    pallas_call x2, Pallas kernels, row_part(): pl.pallas_call(functools.partial(row_body, first), in_specs=[SMEM] * 4 +...  18.4 us
    ppermute x9, waiting for transfers between devices, shift_z(): return lax.ppermute(x, 'row', [(i, (i + 2 * dz) % 8) for i in range(8)])  17.5 us
    ppermute x12, starting transfers between devices, swap_core(): return lax.ppermute(x, 'row', [(i, i ^ 1) for i in range(8)])  14.5 us
    all_to_all x2, waiting for transfers between devices, shards(): lax.all_to_all(out[0].reshape(16, 2, W, W), 'col', 0, 0, tiled=True)  13.4 us
    ppermute x9, starting transfers between devices, shift_z(): return lax.ppermute(x, 'row', [(i, (i + 2 * dz) % 8) for i in range(8)])  11.6 us
    all_to_all x2, starting transfers between devices, shards(): lax.all_to_all(out[0].reshape(16, 2, W, W), 'col', 0, 0, tiled=True)  10.6 us
    all_to_all x1, starting transfers between devices, shards(): col_asked = lax.all_to_all(spread_wants(col_wants), 'col', 0, 0, tiled=True)  7.58 us
  transfers between devices with their start and end apart: 24, of which 9 were waited for; matrix products, arithmetic and copies ran while one was open for 0% of the time, Pallas kernels for 15%

profile of v1, /device:TPU:1, one launch (start us, length us, event | category | flops | bytes accessed | tf_op | source)
XLA Modules:
  0.0 126.1 jit_solution(442065670068282823)
XLA Ops:
  0.6 1.3 %spread_wants.1 = s32[16,1,128]{2,1,0:T(1,128)} custom-call(s32[1,1,32]{2,1,0:T(1,128)} %wants.1), custom_call_target="tpu_custom_call" | custom-call | tf_op jit(solution)/shard_map/spread_wants/pallas_call | solution.py:37
  1.9 7.6 %all-to-all-start = ((s32[16,1,128]{2,1,0:T(1,128)}), s32[16,1,128]{2,1,0:T(1,128)S(1)}, u32[]{:S(2)}, u32[]{:S(2)}) async-start(s32[16,1,128]{2,1,0:T(1,128)} %spread_wants.1), calls=%async_computation | async-start | bytes 16384 | tf_op jit(solution)/shard_map/all_to_all | solution.py:321
  9.5 1.0 collective-permute-start.3
  10.5 3.8 %collective-permute-start.2 = (s32[1,1,32]{2,1,0:T(1,128)}, s32[1,1,32]{2,1,0:T(1,128)S(1)}, u32[]{:S(2)}, u32[]{:S(2)}) collective-permute-start(s32[1,1,32]{2,1,0:T(1,128)} %refs_1_.1), channel_id=1, source_target_pairs={{0,96},{16,112},{32,0},{48,16},{64,32},{80,48},{96,64},{112,80},{1... | collective-permute-start | bytes 392 | tf_op jit(solution)/shard_map/ppermute | solution.py:296
  14.3 0.0 collective-permute-start.1
  14.3 0.7 collective-permute-start
  15.0 0.2 collective-permute-done.2.refs_3_.refs_4_
  15.2 0.9 collective-permute-start.6
  16.1 2.2 %collective-permute-done.1.refs_2_.refs_3_ = s32[1,1,32]{2,1,0:T(1,128)S(1)} collective-permute-done((s32[1,1,32]{2,1,0:T(1,128)}, s32[1,1,32]{2,1,0:T(1,128)S(1)}, u32[]{:S(2)}, u32[]{:S(2)}) %collective-permute-start.1) | collective-permute-done | bytes 160 | tf_op jit(solution)/shard_map/ppermute | solution.py:296
  18.3 1.5 %collective-permute-start.5 = (s32[1,1,32]{2,1,0:T(1,128)S(1)}, s32[1,1,32]{2,1,0:T(1,128)S(1)}, u32[]{:S(2)}, u32[]{:S(2)}) collective-permute-start(s32[1,1,32]{2,1,0:T(1,128)S(1)} %collective-permute-done.1.refs_2_.refs_3_), channel_id=1, source_target_pairs={{0,16},{16,0},{32,48},{48,32},{64,80},{80,64},{96,112},{112,96},{1... | collective-permute-start | bytes 392 | tf_op jit(solution)/shard_map/ppermute | solution.py:292
  19.8 0.0 collective-permute-done.refs_1_.refs_2_
  19.8 0.1 collective-permute-start.4
  19.9 0.0 collective-permute-done.3.refs_4_.refs_5_
  19.9 0.0 collective-permute-done.6.refs_7_.refs_8_
  20.0 0.7 collective-permute-done.5.refs_6_.refs_7_
  20.7 0.3 collective-permute-done.4.refs_5_.refs_6_
  21.0 0.0 all-to-all-done.col_asked.refs_0_
  21.0 0.2 copy-done.8
  21.2 0.4 copy-done.9
  21.6 0.6 copy-done.2
  22.1 3.8 %first_outgoing.1 = (bf16[32,128,128]{2,1,0:T(8,128)(2,1)}, bf16[8,128,128]{2,1,0:T(8,128)(2,1)}, bf16[8,128,128]{2,1,0:T(8,128)(2,1)}, bf16[8,128,128]{2,1,0:T(8,128)(2,1)}, bf16[8,128,128]{2,1,0:T(8,128)(2,1)}) custom-call(s32[32]{0:T(128)} %sizes.9, s32[16,1,128]{2,1,0:T(1,128)} %copy-done.2, s32[1,1,32]{2,1,0:T(1,128)} %refs_1_.1, ...), custom_call_target="tpu_custom_call" | custom-call | tf_op jit(solution)/shard_map/first_outgoing/pallas_call | solution.py:80
  25.9 0.1 collective-permute-start.7
  26.0 1.5 %collective-permute-start.8 = (bf16[8,128,128]{2,1,0:T(8,128)(2,1)}, bf16[8,128,128]{2,1,0:T(8,128)(2,1)S(1)}, u32[]{:S(2)}, u32[]{:S(2)}) collective-permute-start(bf16[8,128,128]{2,1,0:T(8,128)(2,1)} %get-tuple-element.16), channel_id=1, source_target_pairs={{0,64},{16,80},{32,96},{48,112},{64,0},{80,16},{96,32},{112,48},{1... | collective-permute-start | bytes 786440 | tf_op jit(solution)/shard_map/ppermute | solution.py:296
  27.5 2.0 %collective-permute-start.9 = (bf16[8,128,128]{2,1,0:T(8,128)(2,1)}, bf16[8,128,128]{2,1,0:T(8,128)(2,1)S(1)}, u32[]{:S(2)}, u32[]{:S(2)}) collective-permute-start(bf16[8,128,128]{2,1,0:T(8,128)(2,1)} %get-tuple-element.17), channel_id=1, source_target_pairs={{0,96},{16,112},{32,0},{48,16},{64,32},{80,48},{96,64},{112,80},{1... | collective-permute-start | bytes 786440 | tf_op jit(solution)/shard_map/ppermute | solution.py:296
  29.5 1.1 collective-permute-start.10
  30.6 10.1 %collective-permute-done.7.refs_1_ = bf16[8,128,128]{2,1,0:T(8,128)(2,1)S(1)} collective-permute-done((bf16[8,128,128]{2,1,0:T(8,128)(2,1)}, bf16[8,128,128]{2,1,0:T(8,128)(2,1)S(1)}, u32[]{:S(2)}, u32[]{:S(2)}) %collective-permute-start.7) | collective-permute-done | bytes 262176 | tf_op jit(solution)/shard_map/ppermute | solution.py:296
  40.7 1.0 collective-permute-start.11
  41.7 0.0 collective-permute-done.8.refs_2_
  41.8 0.1 collective-permute-start.12
  41.8 0.0 collective-permute-done.9.refs_3_
  41.9 0.5 collective-permute-start.13
  42.4 6.9 %all-to-all-start.1 = ((bf16[16,2,128,128]{3,2,1,0:T(8,128)(2,1)}), bf16[16,2,128,128]{3,2,1,0:T(8,128)(2,1)S(1)}, u32[]{:S(2)}, u32[]{:S(2)}) async-start(bf16[16,2,128,128]{3,2,1,0:T(8,128)(2,1)} %bitcast.11), calls=%async_computation.1 | async-start | bytes 2097152 | tf_op jit(solution)/shard_map/all_to_all | solution.py:328
  49.2 0.0 collective-permute-done.10.refs_4_
  49.3 0.0 collective-permute-done.12.refs_6_
  49.3 0.0 collective-permute-done.13.refs_7_
  49.3 0.6 copy-done.16
  50.0 0.1 copy-done.18
  50.1 0.0 copy-done.20
  50.1 0.1 copy-done.22
  50.2 9.2 %row_part.2.refs_12_ = f32[32,128,128]{2,1,0:T(8,128)} custom-call(s32[8,32]{1,0:T(8,128)} %bitcast.16, f32[8,32]{1,0:T(8,128)} %bitcast.18, s32[32]{0:T(128)} %sizes.9, f32[32]{0:T(128)} %shift.7, f32[32,128]{1,0:T(8,128)} %eps.7, bf16[8,128,128]{2,1,0:T(8,128)(2,1)} %get-tuple-element.14.refs_0_, bf16[8,128,128]{2,1,0:T(8,128)(2,1)} %copy-done.10, ...), custom_call_target="tpu_custom_call" | custom-call | flops 25769803776 | bytes 16777216 | tf_op jit(solution)/shard_map/row_part/pallas_call | solution.py:191
  59.4 7.4 %all-to-all-done.1 = bf16[16,2,128,128]{3,2,1,0:T(8,128)(2,1)S(1)} async-done(((bf16[16,2,128,128]{3,2,1,0:T(8,128)(2,1)}), bf16[16,2,128,128]{3,2,1,0:T(8,128)(2,1)S(1)}, u32[]{:S(2)}, u32[]{:S(2)}) %all-to-all-start.1) | async-done | bytes 1048608 | tf_op jit(solution)/shard_map/all_to_all | solution.py:328
  66.8 1.0 copy-done
  67.8 10.7 %col_part.2 = (f32[32,128,128]{2,1,0:T(8,128)}, bf16[32,128,128]{2,1,0:T(8,128)(2,1)}, bf16[8,128,128]{2,1,0:T(8,128)(2,1)}, bf16[8,128,128]{2,1,0:T(8,128)(2,1)...) custom-call(s32[8,32]{1,0:T(8,128)} %bitcast.12, f32[8,32]{1,0:T(8,128)} %bitcast.14, s32[32]{0:T(128)} %sizes.9, ...), custom_call_target="tpu_custom_call" | custom-call | flops 2147483648 | bytes 16777216 | tf_op jit(solution)/shard_map/col_part/pallas_call | solution.py:270
  78.4 0.8 collective-permute-start.14
  79.2 2.7 %collective-permute-start.15 = (bf16[8,128,128]{2,1,0:T(8,128)(2,1)}, bf16[8,128,128]{2,1,0:T(8,128)(2,1)S(1)}, u32[]{:S(2)}, u32[]{:S(2)}) collective-permute-start(bf16[8,128,128]{2,1,0:T(8,128)(2,1)} %get-tuple-element.22), channel_id=1, source_target_pairs={{0,64},{16,80},{32,96},{48,112},{64,0},{80,16},{96,32},{112,48},{1... | collective-permute-start | bytes 786440 | tf_op jit(solution)/shard_map/ppermute | solution.py:296
  82.0 0.0 collective-permute-start.16
  82.0 2.2 %collective-permute-start.17 = (bf16[8,128,128]{2,1,0:T(8,128)(2,1)}, bf16[8,128,128]{2,1,0:T(8,128)(2,1)S(1)}, u32[]{:S(2)}, u32[]{:S(2)}) collective-permute-start(bf16[8,128,128]{2,1,0:T(8,128)(2,1)} %get-tuple-element.20.refs_0_), channel_id=1, source_target_pairs={{0,16},{16,0},{32,48},{48,32},{64,80},{80,64},{96,112},{112,96},{1... | collective-permute-start | bytes 786440 | tf_op jit(solution)/shard_map/ppermute | solution.py:292
  84.3 2.1 %collective-permute-done.14.refs_1_ = bf16[8,128,128]{2,1,0:T(8,128)(2,1)S(1)} collective-permute-done((bf16[8,128,128]{2,1,0:T(8,128)(2,1)}, bf16[8,128,128]{2,1,0:T(8,128)(2,1)S(1)}, u32[]{:S(2)}, u32[]{:S(2)}) %collective-permute-start.14) | collective-permute-done | bytes 262176 | tf_op jit(solution)/shard_map/ppermute | solution.py:296
  86.3 3.5 %collective-permute-start.18 = (bf16[8,128,128]{2,1,0:T(8,128)(2,1)S(1)}, bf16[8,128,128]{2,1,0:T(8,128)(2,1)S(1)}, u32[]{:S(2)}, u32[]{:S(2)}) collective-permute-start(bf16[8,128,128]{2,1,0:T(8,128)(2,1)S(1)} %collective-permute-done.14.refs_1_), channel_id=1, source_target_pairs={{0,16},{16,0},{32,48},{48,32},{64,80},{80,64},{96,112},{112,96},{1... | collective-permute-start | bytes 786440 | tf_op jit(solution)/shard_map/ppermute | solution.py:292
  89.8 2.9 %collective-permute-done.15.refs_2_ = bf16[8,128,128]{2,1,0:T(8,128)(2,1)S(1)} collective-permute-done((bf16[8,128,128]{2,1,0:T(8,128)(2,1)}, bf16[8,128,128]{2,1,0:T(8,128)(2,1)S(1)}, u32[]{:S(2)}, u32[]{:S(2)}) %collective-permute-start.15) | collective-permute-done | bytes 262176 | tf_op jit(solution)/shard_map/ppermute | solution.py:296
  92.7 2.4 %collective-permute-start.19 = (bf16[8,128,128]{2,1,0:T(8,128)(2,1)S(1)}, bf16[8,128,128]{2,1,0:T(8,128)(2,1)S(1)}, u32[]{:S(2)}, u32[]{:S(2)}) collective-permute-start(bf16[8,128,128]{2,1,0:T(8,128)(2,1)S(1)} %collective-permute-done.15.refs_2_), channel_id=1, source_target_pairs={{0,16},{16,0},{32,48},{48,32},{64,80},{80,64},{96,112},{112,96},{1... | collective-permute-start | bytes 786440 | tf_op jit(solution)/shard_map/ppermute | solution.py:292
  95.1 0.1 collective-permute-start.20
  95.2 3.7 %all-to-all-start.2 = ((bf16[16,2,128,128]{3,2,1,0:T(8,128)(2,1)}), bf16[16,2,128,128]{3,2,1,0:T(8,128)(2,1)S(1)}, u32[]{:S(2)}, u32[]{:S(2)}) async-start(bf16[16,2,128,128]{3,2,1,0:T(8,128)(2,1)} %bitcast.10), calls=%async_computation.2 | async-start | bytes 2097152 | tf_op jit(solution)/shard_map/all_to_all | solution.py:328
  98.9 0.0 collective-permute-done.17.refs_4_
  98.9 0.0 collective-permute-done.18.refs_5_
  99.0 0.0 collective-permute-done.20.refs_7_
  99.0 0.6 copy-done.17
  99.6 0.1 copy-done.19
  99.7 0.1 copy-done.21
  99.8 0.1 copy-done.23
  99.9 9.2 %row_part.3.refs_3_ = f32[32,128,128]{2,1,0:T(8,128)} custom-call(s32[8,32]{1,0:T(8,128)} %bitcast.17, f32[8,32]{1,0:T(8,128)} %bitcast.19, s32[32]{0:T(128)} %sizes.9, f32[32]{0:T(128)} %shift.7, f32[32,128]{1,0:T(8,128)} %eps.7, bf16[8,128,128]{2,1,0:T(8,128)(2,1)} %get-tuple-element.20.refs_0_, bf16[8,128,128]{2,1,0:T(8,128)(2,1)} %copy-done.11, ...), custom_call_target="tpu_custom_call" | custom-call | flops 25769803776 | bytes 16777216 | tf_op jit(solution)/shard_map/row_part/pallas_call | solution.py:191
  109.1 6.1 %all-to-all-done.2 = bf16[16,2,128,128]{3,2,1,0:T(8,128)(2,1)S(1)} async-done(((bf16[16,2,128,128]{3,2,1,0:T(8,128)(2,1)}), bf16[16,2,128,128]{3,2,1,0:T(8,128)(2,1)S(1)}, u32[]{:S(2)}, u32[]{:S(2)}) %all-to-all-start.2) | async-done | bytes 1048608 | tf_op jit(solution)/shard_map/all_to_all | solution.py:328
  115.2 1.0 copy-done.1
  116.2 9.7 %col_part.3 = (f32[32,128,128]{2,1,0:T(8,128)}, f32[32,128,128]{2,1,0:T(8,128)}) custom-call(s32[8,32]{1,0:T(8,128)} %bitcast.13, f32[8,32]{1,0:T(8,128)} %bitcast.15, s32[32]{0:T(128)} %sizes.9, f32[32]{0:T(128)} %shift.7, f32[32,128]{1,0:T(8,128)} %eps.7, bf16[32,8,128,128]{3,2,1,0:T(8,128)(2,1)} %refs_0_.3, bf16[32,128,128]{2,1,0:T(8,128)(2,1)} %bitcast.9, ...), custom_call_target="tpu_custom_call" | custom-call | flops 2147483648 | bytes 16777216 | tf_op jit(solution)/shard_map/col_part/pallas_call | solution.py:270
  (38 shorter events, 0.1 us)
Async XLA Ops:
  1.9 19.1 %all-to-all-start = ((s32[16,1,128]{2,1,0:T(1,128)}), s32[16,1,128]{2,1,0:T(1,128)S(1)}, u32[]{:S(2)}, u32[]{:S(2)}) async-start(s32[16,1,128]{2,1,0:T(1,128)} %spread_wants.1), calls=%async_computation | async-start | bytes 16384 | tf_op jit(solution)/shard_map/all_to_all | solution.py:321
  9.5 10.4 %collective-permute-start.3 = (s32[1,1,32]{2,1,0:T(1,128)}, s32[1,1,32]{2,1,0:T(1,128)S(1)}, u32[]{:S(2)}, u32[]{:S(2)}) collective-permute-start(s32[1,1,32]{2,1,0:T(1,128)} %refs_1_.1), channel_id=1, source_target_pairs={{0,16},{16,0},{32,48},{48,32},{64,80},{80,64},{96,112},{112,96},{1... | collective-permute-start | bytes 392 | tf_op jit(solution)/shard_map/ppermute | solution.py:292
  10.5 4.6 %collective-permute-start.2 = (s32[1,1,32]{2,1,0:T(1,128)}, s32[1,1,32]{2,1,0:T(1,128)S(1)}, u32[]{:S(2)}, u32[]{:S(2)}) collective-permute-start(s32[1,1,32]{2,1,0:T(1,128)} %refs_1_.1), channel_id=1, source_target_pairs={{0,96},{16,112},{32,0},{48,16},{64,32},{80,48},{96,64},{112,80},{1... | collective-permute-start | bytes 392 | tf_op jit(solution)/shard_map/ppermute | solution.py:296
  14.3 4.0 %collective-permute-start.1 = (s32[1,1,32]{2,1,0:T(1,128)}, s32[1,1,32]{2,1,0:T(1,128)S(1)}, u32[]{:S(2)}, u32[]{:S(2)}) collective-permute-start(s32[1,1,32]{2,1,0:T(1,128)} %refs_1_.1), channel_id=1, source_target_pairs={{0,64},{16,80},{32,96},{48,112},{64,0},{80,16},{96,32},{112,48},{1... | collective-permute-start | bytes 392 | tf_op jit(solution)/shard_map/ppermute | solution.py:296
  14.3 5.5 %collective-permute-start = (s32[1,1,32]{2,1,0:T(1,128)}, s32[1,1,32]{2,1,0:T(1,128)S(1)}, u32[]{:S(2)}, u32[]{:S(2)}) collective-permute-start(s32[1,1,32]{2,1,0:T(1,128)} %refs_1_.1), channel_id=1, source_target_pairs={{0,32},{16,48},{32,64},{48,80},{64,96},{80,112},{96,0},{112,16},{1... | collective-permute-start | bytes 392 | tf_op jit(solution)/shard_map/ppermute | solution.py:296
  15.2 5.8 %copy-start.4 = (s32[1,1,32]{2,1,0:T(1,128)}, s32[1,1,32]{2,1,0:T(1,128)S(1)}, u32[]{:S(2)}) copy-start(s32[1,1,32]{2,1,0:T(1,128)S(1)} %collective-permute-done.2.refs_3_.refs_4_) | copy-start | bytes 388
  15.2 4.8 %collective-permute-start.6 = (s32[1,1,32]{2,1,0:T(1,128)S(1)}, s32[1,1,32]{2,1,0:T(1,128)S(1)}, u32[]{:S(2)}, u32[]{:S(2)}) collective-permute-start(s32[1,1,32]{2,1,0:T(1,128)S(1)} %collective-permute-done.2.refs_3_.refs_4_), channel_id=1, source_target_pairs={{0,16},{16,0},{32,48},{48,32},{64,80},{80,64},{96,112},{112,96},{1... | collective-permute-start | bytes 392 | tf_op jit(solution)/shard_map/ppermute | solution.py:292
  18.3 2.6 %copy-start.5 = (s32[1,1,32]{2,1,0:T(1,128)}, s32[1,1,32]{2,1,0:T(1,128)S(1)}, u32[]{:S(2)}) copy-start(s32[1,1,32]{2,1,0:T(1,128)S(1)} %collective-permute-done.1.refs_2_.refs_3_) | copy-start | bytes 388
  18.3 2.3 %collective-permute-start.5 = (s32[1,1,32]{2,1,0:T(1,128)S(1)}, s32[1,1,32]{2,1,0:T(1,128)S(1)}, u32[]{:S(2)}, u32[]{:S(2)}) collective-permute-start(s32[1,1,32]{2,1,0:T(1,128)S(1)} %collective-permute-done.1.refs_2_.refs_3_), channel_id=1, source_target_pairs={{0,16},{16,0},{32,48},{48,32},{64,80},{80,64},{96,112},{112,96},{1... | collective-permute-start | bytes 392 | tf_op jit(solution)/shard_map/ppermute | solution.py:292
  19.8 1.1 copy-start.6
  19.8 1.1 collective-permute-start.4
  19.9 1.1 copy-start.3
  19.9 1.1 copy-start.7
  20.7 0.5 copy-start.8
  21.0 0.6 copy-start.9
  21.6 0.6 copy-start.2
  25.9 14.8 %collective-permute-start.7 = (bf16[8,128,128]{2,1,0:T(8,128)(2,1)}, bf16[8,128,128]{2,1,0:T(8,128)(2,1)S(1)}, u32[]{:S(2)}, u32[]{:S(2)}) collective-permute-start(bf16[8,128,128]{2,1,0:T(8,128)(2,1)} %get-tuple-element.15), channel_id=1, source_target_pairs={{0,32},{16,48},{32,64},{48,80},{64,96},{80,112},{96,0},{112,16},{1... | collective-permute-start | bytes 786440 | tf_op jit(solution)/shard_map/ppermute | solution.py:296
  26.0 15.8 %collective-permute-start.8 = (bf16[8,128,128]{2,1,0:T(8,128)(2,1)}, bf16[8,128,128]{2,1,0:T(8,128)(2,1)S(1)}, u32[]{:S(2)}, u32[]{:S(2)}) collective-permute-start(bf16[8,128,128]{2,1,0:T(8,128)(2,1)} %get-tuple-element.16), channel_id=1, source_target_pairs={{0,64},{16,80},{32,96},{48,112},{64,0},{80,16},{96,32},{112,48},{1... | collective-permute-start | bytes 786440 | tf_op jit(solution)/shard_map/ppermute | solution.py:296
  27.5 14.3 %collective-permute-start.9 = (bf16[8,128,128]{2,1,0:T(8,128)(2,1)}, bf16[8,128,128]{2,1,0:T(8,128)(2,1)S(1)}, u32[]{:S(2)}, u32[]{:S(2)}) collective-permute-start(bf16[8,128,128]{2,1,0:T(8,128)(2,1)} %get-tuple-element.17), channel_id=1, source_target_pairs={{0,96},{16,112},{32,0},{48,16},{64,32},{80,48},{96,64},{112,80},{1... | collective-permute-start | bytes 786440 | tf_op jit(solution)/shard_map/ppermute | solution.py:296
  29.5 19.7 %collective-permute-start.10 = (bf16[8,128,128]{2,1,0:T(8,128)(2,1)}, bf16[8,128,128]{2,1,0:T(8,128)(2,1)S(1)}, u32[]{:S(2)}, u32[]{:S(2)}) collective-permute-start(bf16[8,128,128]{2,1,0:T(8,128)(2,1)} %get-tuple-element.14.refs_0_), channel_id=1, source_target_pairs={{0,16},{16,0},{32,48},{48,32},{64,80},{80,64},{96,112},{112,96},{1... | collective-permute-start | bytes 786440 | tf_op jit(solution)/shard_map/ppermute | solution.py:292
  40.7 8.6 %copy-start.10 = (bf16[8,128,128]{2,1,0:T(8,128)(2,1)}, bf16[8,128,128]{2,1,0:T(8,128)(2,1)S(1)}, u32[]{:S(2)}) copy-start(bf16[8,128,128]{2,1,0:T(8,128)(2,1)S(1)} %collective-permute-done.7.refs_1_) | copy-start | bytes 786436
  40.7 8.5 %collective-permute-start.11 = (bf16[8,128,128]{2,1,0:T(8,128)(2,1)S(1)}, bf16[8,128,128]{2,1,0:T(8,128)(2,1)S(1)}, u32[]{:S(2)}, u32[]{:S(2)}) collective-permute-start(bf16[8,128,128]{2,1,0:T(8,128)(2,1)S(1)} %collective-permute-done.7.refs_1_), channel_id=1, source_target_pairs={{0,16},{16,0},{32,48},{48,32},{64,80},{80,64},{96,112},{112,96},{1... | collective-permute-start | bytes 786440 | tf_op jit(solution)/shard_map/ppermute | solution.py:292
  41.8 7.6 %copy-start.12 = (bf16[8,128,128]{2,1,0:T(8,128)(2,1)}, bf16[8,128,128]{2,1,0:T(8,128)(2,1)S(1)}, u32[]{:S(2)}) copy-start(bf16[8,128,128]{2,1,0:T(8,128)(2,1)S(1)} %collective-permute-done.8.refs_2_) | copy-start | bytes 786436
  41.8 7.5 %collective-permute-start.12 = (bf16[8,128,128]{2,1,0:T(8,128)(2,1)S(1)}, bf16[8,128,128]{2,1,0:T(8,128)(2,1)S(1)}, u32[]{:S(2)}, u32[]{:S(2)}) collective-permute-start(bf16[8,128,128]{2,1,0:T(8,128)(2,1)S(1)} %collective-permute-done.8.refs_2_), channel_id=1, source_target_pairs={{0,16},{16,0},{32,48},{48,32},{64,80},{80,64},{96,112},{112,96},{1... | collective-permute-start | bytes 786440 | tf_op jit(solution)/shard_map/ppermute | solution.py:292
  41.8 7.5 %copy-start.14 = (bf16[8,128,128]{2,1,0:T(8,128)(2,1)}, bf16[8,128,128]{2,1,0:T(8,128)(2,1)S(1)}, u32[]{:S(2)}) copy-start(bf16[8,128,128]{2,1,0:T(8,128)(2,1)S(1)} %collective-permute-done.9.refs_3_) | copy-start | bytes 786436
  41.9 7.5 %collective-permute-start.13 = (bf16[8,128,128]{2,1,0:T(8,128)(2,1)S(1)}, bf16[8,128,128]{2,1,0:T(8,128)(2,1)S(1)}, u32[]{:S(2)}, u32[]{:S(2)}) collective-permute-start(bf16[8,128,128]{2,1,0:T(8,128)(2,1)S(1)} %collective-permute-done.9.refs_3_), channel_id=1, source_target_pairs={{0,16},{16,0},{32,48},{48,32},{64,80},{80,64},{96,112},{112,96},{1... | collective-permute-start | bytes 786440 | tf_op jit(solution)/shard_map/ppermute | solution.py:292
  42.4 24.4 %all-to-all-start.1 = ((bf16[16,2,128,128]{3,2,1,0:T(8,128)(2,1)}), bf16[16,2,128,128]{3,2,1,0:T(8,128)(2,1)S(1)}, u32[]{:S(2)}, u32[]{:S(2)}) async-start(bf16[16,2,128,128]{3,2,1,0:T(8,128)(2,1)} %bitcast.11), calls=%async_computation.1 | async-start | bytes 2097152 | tf_op jit(solution)/shard_map/all_to_all | solution.py:328
  49.2 0.7 copy-start.16
  49.3 0.8 copy-start.18
  49.3 0.8 copy-start.20
  49.3 0.9 copy-start.22
  66.8 1.0 copy-start
  78.4 7.9 %collective-permute-start.14 = (bf16[8,128,128]{2,1,0:T(8,128)(2,1)}, bf16[8,128,128]{2,1,0:T(8,128)(2,1)S(1)}, u32[]{:S(2)}, u32[]{:S(2)}) collective-permute-start(bf16[8,128,128]{2,1,0:T(8,128)(2,1)} %get-tuple-element.21), channel_id=1, source_target_pairs={{0,32},{16,48},{32,64},{48,80},{64,96},{80,112},{96,0},{112,16},{1... | collective-permute-start | bytes 786440 | tf_op jit(solution)/shard_map/ppermute | solution.py:296
  79.2 13.5 %collective-permute-start.15 = (bf16[8,128,128]{2,1,0:T(8,128)(2,1)}, bf16[8,128,128]{2,1,0:T(8,128)(2,1)S(1)}, u32[]{:S(2)}, u32[]{:S(2)}) collective-permute-start(bf16[8,128,128]{2,1,0:T(8,128)(2,1)} %get-tuple-element.22), channel_id=1, source_target_pairs={{0,64},{16,80},{32,96},{48,112},{64,0},{80,16},{96,32},{112,48},{1... | collective-permute-start | bytes 786440 | tf_op jit(solution)/shard_map/ppermute | solution.py:296
  82.0 13.1 %collective-permute-start.16 = (bf16[8,128,128]{2,1,0:T(8,128)(2,1)}, bf16[8,128,128]{2,1,0:T(8,128)(2,1)S(1)}, u32[]{:S(2)}, u32[]{:S(2)}) collective-permute-start(bf16[8,128,128]{2,1,0:T(8,128)(2,1)} %get-tuple-element.23), channel_id=1, source_target_pairs={{0,96},{16,112},{32,0},{48,16},{64,32},{80,48},{96,64},{112,80},{1... | collective-permute-start | bytes 786440 | tf_op jit(solution)/shard_map/ppermute | solution.py:296
  82.0 16.9 %collective-permute-start.17 = (bf16[8,128,128]{2,1,0:T(8,128)(2,1)}, bf16[8,128,128]{2,1,0:T(8,128)(2,1)S(1)}, u32[]{:S(2)}, u32[]{:S(2)}) collective-permute-start(bf16[8,128,128]{2,1,0:T(8,128)(2,1)} %get-tuple-element.20.refs_0_), channel_id=1, source_target_pairs={{0,16},{16,0},{32,48},{48,32},{64,80},{80,64},{96,112},{112,96},{1... | collective-permute-start | bytes 786440 | tf_op jit(solution)/shard_map/ppermute | solution.py:292
  86.3 12.7 %copy-start.11 = (bf16[8,128,128]{2,1,0:T(8,128)(2,1)}, bf16[8,128,128]{2,1,0:T(8,128)(2,1)S(1)}, u32[]{:S(2)}) copy-start(bf16[8,128,128]{2,1,0:T(8,128)(2,1)S(1)} %collective-permute-done.14.refs_1_) | copy-start | bytes 786436
  86.3 12.6 %collective-permute-start.18 = (bf16[8,128,128]{2,1,0:T(8,128)(2,1)S(1)}, bf16[8,128,128]{2,1,0:T(8,128)(2,1)S(1)}, u32[]{:S(2)}, u32[]{:S(2)}) collective-permute-start(bf16[8,128,128]{2,1,0:T(8,128)(2,1)S(1)} %collective-permute-done.14.refs_1_), channel_id=1, source_target_pairs={{0,16},{16,0},{32,48},{48,32},{64,80},{80,64},{96,112},{112,96},{1... | collective-permute-start | bytes 786440 | tf_op jit(solution)/shard_map/ppermute | solution.py:292
  92.7 6.3 %copy-start.13 = (bf16[8,128,128]{2,1,0:T(8,128)(2,1)}, bf16[8,128,128]{2,1,0:T(8,128)(2,1)S(1)}, u32[]{:S(2)}) copy-start(bf16[8,128,128]{2,1,0:T(8,128)(2,1)S(1)} %collective-permute-done.15.refs_2_) | copy-start | bytes 786436
  92.7 6.2 %collective-permute-start.19 = (bf16[8,128,128]{2,1,0:T(8,128)(2,1)S(1)}, bf16[8,128,128]{2,1,0:T(8,128)(2,1)S(1)}, u32[]{:S(2)}, u32[]{:S(2)}) collective-permute-start(bf16[8,128,128]{2,1,0:T(8,128)(2,1)S(1)} %collective-permute-done.15.refs_2_), channel_id=1, source_target_pairs={{0,16},{16,0},{32,48},{48,32},{64,80},{80,64},{96,112},{112,96},{1... | collective-permute-start | bytes 786440 | tf_op jit(solution)/shard_map/ppermute | solution.py:292
  95.1 3.9 %copy-start.15 = (bf16[8,128,128]{2,1,0:T(8,128)(2,1)}, bf16[8,128,128]{2,1,0:T(8,128)(2,1)S(1)}, u32[]{:S(2)}) copy-start(bf16[8,128,128]{2,1,0:T(8,128)(2,1)S(1)} %collective-permute-done.16.refs_3_) | copy-start | bytes 786436
  95.1 3.9 %collective-permute-start.20 = (bf16[8,128,128]{2,1,0:T(8,128)(2,1)S(1)}, bf16[8,128,128]{2,1,0:T(8,128)(2,1)S(1)}, u32[]{:S(2)}, u32[]{:S(2)}) collective-permute-start(bf16[8,128,128]{2,1,0:T(8,128)(2,1)S(1)} %collective-permute-done.16.refs_3_), channel_id=1, source_target_pairs={{0,16},{16,0},{32,48},{48,32},{64,80},{80,64},{96,112},{112,96},{1... | collective-permute-start | bytes 786440 | tf_op jit(solution)/shard_map/ppermute | solution.py:292
  95.2 20.0 %all-to-all-start.2 = ((bf16[16,2,128,128]{3,2,1,0:T(8,128)(2,1)}), bf16[16,2,128,128]{3,2,1,0:T(8,128)(2,1)S(1)}, u32[]{:S(2)}, u32[]{:S(2)}) async-start(bf16[16,2,128,128]{3,2,1,0:T(8,128)(2,1)} %bitcast.10), calls=%async_computation.2 | async-start | bytes 2097152 | tf_op jit(solution)/shard_map/all_to_all | solution.py:328
  98.9 0.7 copy-start.17
  98.9 0.8 copy-start.19
  99.0 0.9 copy-start.21
  99.0 0.9 copy-start.23
  115.2 1.0 copy-start.1

commit v2 on v1

--- a/solution.py
+++ b/solution.py
@@ -83,7 +83,7 @@
         out_specs=[ANY] * 5,
         out_shape=OUTGOING,
         scratch_shapes=[pltpu.VMEM((PAIRS, W, W), BF16), pltpu.SemaphoreType.DMA((2 * PAIRS,))],
-        compiler_params=pltpu.CompilerParams(vmem_limit_bytes=60 * 2**20),
+        compiler_params=pltpu.CompilerParams(vmem_limit_bytes=52 * 2**20),
         name="first_outgoing",
     )(sizes, *asked, amp_start)
 
@@ -190,7 +190,7 @@
 def row_part(first, slot, fock, sizes, shift, eps, pieces, over, amp, exch):
     return pl.pallas_call(
         functools.partial(row_body, first),
-        in_specs=[SMEM] * 4 + [VMEM] + [ANY] * 11,
+        in_specs=[SMEM] * 4 + [VMEM] + [VMEM] * 8 + [ANY] * 3,
         out_specs=ANY,
         out_shape=jax.ShapeDtypeStruct((PAIRS, W, W), F32),
         scratch_shapes=[
@@ -202,8 +202,8 @@
             pltpu.SemaphoreType.DMA((8,)),
         ]
         + [pltpu.SemaphoreType.DMA((CHUNKS,))] * 4,
-        compiler_params=pltpu.CompilerParams(vmem_limit_bytes=60 * 2**20),
-        cost_estimate=cost(12),
+        compiler_params=pltpu.CompilerParams(vmem_limit_bytes=52 * 2**20),
+        cost_estimate=cost(3),
         name="row_part",
     )(slot, fock, sizes, shift, eps, *pieces, over, amp, exch)
 
@@ -211,15 +211,13 @@
 def col_body(first, slot, fock, sizes, shift, eps, *refs):
     if first:
         col_asked, lists, refs = refs[0], refs[1:9], refs[9:]
-    over_h, table_h, amp_h, base_h, refs = refs[0], refs[1], refs[2], refs[3], refs[4:]
+    over_h, table, amp_h, base_h, refs = refs[0], refs[1], refs[2], refs[3], refs[4:]
     amp_out, refs = refs[0], refs[1:]
     if first:
         out_col, out_row, refs = refs[0], refs[1:5], refs[5:]
     else:
         third_out, refs = refs[0], refs[1:]
-    over, table, amp, base, third, table_sem, over_sem, amp_sem, base_sem, amp_out_sem, third_sem, sems = refs
-    load = pltpu.make_async_copy(table_h, table, table_sem)
-    load.start()
+    over, amp, base, third, over_sem, amp_sem, base_sem, amp_out_sem, third_sem, sems = refs
     def fetch(c):
         chunk_copy(over_h, over, over_sem, c).start()
         chunk_copy(amp_h, amp, amp_sem, c).start()
@@ -228,7 +226,6 @@
     for c in range(AHEAD):
         fetch(c)
     eps_t = jnp.transpose(eps[...])
-    load.wait()
 
     def ready(c):
         if c + AHEAD < CHUNKS:
@@ -269,20 +266,18 @@
     whole = jax.ShapeDtypeStruct((PAIRS, W, W), F32)
     return pl.pallas_call(
         functools.partial(col_body, first),
-        in_specs=[SMEM] * 4 + [VMEM] + [SMEM] * len(asked) + [ANY] * 4,
+        in_specs=[SMEM] * 4 + [VMEM] + [SMEM] * len(asked) + [ANY, VMEM, ANY, ANY],
         out_specs=[ANY] * 6 if first else [ANY] * 2,
         out_shape=[whole] + OUTGOING if first else [whole] * 2,
         scratch_shapes=[
             pltpu.VMEM((PAIRS, NK, W, W), BF16),
-            chunked(BF16),
             chunked(),
             chunked(),
             chunked(BF16 if first else F32),
-            pltpu.SemaphoreType.DMA,
         ]
         + [pltpu.SemaphoreType.DMA((CHUNKS,))] * 5
         + [pltpu.SemaphoreType.DMA((2 * PAIRS,))],
-        compiler_params=pltpu.CompilerParams(vmem_limit_bytes=60 * 2**20),
+        compiler_params=pltpu.CompilerParams(vmem_limit_bytes=52 * 2**20),
         cost_estimate=cost(1),
         name="col_part",
     )(slot, fock, sizes, shift, eps, *asked, over, table, amp, base)

time: 127 us -> 107 us (0.84)
  waiting for transfers between devices: 31.9 us -> 11.9 us
  Pallas kernels: 43.8 us -> 48.2 us
  local copies, waits for them, and re-layouts: 4.92 us -> 2.76 us
  starting transfers between devices: 44.3 us -> 42.6 us
    all_to_all x2, waiting for transfers between devices: 13.4 us -> 0.01 us  [shards(): lax.all_to_all(out[0].reshape(16, 2, W, W), 'col', 0, 0, tiled=True)]
    ppermute x9, waiting for transfers between devices: 17.5 us -> 8.02 us  [shift_z(): return lax.ppermute(x, 'row', [(i, (i + 2 * dz) % 8) for i in range(8)])]
    ppermute x12, starting transfers between devices: 14.5 us -> 9.45 us  [swap_core(): return lax.ppermute(x, 'row', [(i, i ^ 1) for i in range(8)])]
    all_to_all x2, starting transfers between devices: 10.6 us -> 13.9 us  [shards(): lax.all_to_all(out[0].reshape(16, 2, W, W), 'col', 0, 0, tiled=True)]
    ppermute x12, waiting for transfers between devices: 1.03 us -> 3.92 us  [swap_core(): return lax.ppermute(x, 'row', [(i, i ^ 1) for i in range(8)])]
    pallas_call x2, Pallas kernels: 18.4 us -> 20.8 us  [row_part(): pl.pallas_call(functools.partial(row_body, first), in_specs=[SMEM] * 4 +...]
    unnamed x48 -> x24, local copies, waits for them, and re-layouts: 4.92 us -> 2.76 us
  transfers between devices with their start and end apart: 24 -> 24, of which waited for: 9 -> 11; matrix products, arithmetic and copies ran while one was open for 0% -> 0% of each run, Pallas kernels for 15% -> 20%
where the time goes in v2:
time: 107 us
  Pallas kernels  48.2 us (45%)
  starting transfers between devices  42.6 us (40%)
  waiting for transfers between devices  11.9 us (11%)
  local copies, waits for them, and re-layouts  2.76 us (3%)
    pallas_call x2, Pallas kernels, col_part(): pl.pallas_call(functools.partial(col_body, first), in_specs=[SMEM] * 4 +...  21.1 us
    pallas_call x2, Pallas kernels, row_part(): pl.pallas_call(functools.partial(row_body, first), in_specs=[SMEM] * 4 +...  20.8 us
    all_to_all x2, starting transfers between devices, shards(): lax.all_to_all(out[0].reshape(16, 2, W, W), 'col', 0, 0, tiled=True)  13.9 us
    ppermute x9, starting transfers between devices, shift_z(): return lax.ppermute(x, 'row', [(i, (i + 2 * dz) % 8) for i in range(8)])  11.5 us
    ppermute x12, starting transfers between devices, swap_core(): return lax.ppermute(x, 'row', [(i, i ^ 1) for i in range(8)])  9.45 us
    ppermute x9, waiting for transfers between devices, shift_z(): return lax.ppermute(x, 'row', [(i, (i + 2 * dz) % 8) for i in range(8)])  8.02 us
    all_to_all x1, starting transfers between devices, shards(): col_asked = lax.all_to_all(spread_wants(col_wants), 'col', 0, 0, tiled=True)  7.73 us
    pallas_call x1, Pallas kernels, first_outgoing(): pl.pallas_call(first_body, in_specs=[SMEM] + [SMEM] * 9 + [VMEM], out_spe...  5.01 us
  transfers between devices with their start and end apart: 24, of which 11 were waited for; matrix products, arithmetic and copies ran while one was open for 0% of the time, Pallas kernels for 20%

profile of v2, /device:TPU:1, one launch (start us, length us, event | category | flops | bytes accessed | tf_op | source)
XLA Modules:
  0.0 106.5 jit_solution(1108548059181620443)
XLA Ops:
  0.6 1.3 %spread_wants.1 = s32[16,1,128]{2,1,0:T(1,128)} custom-call(s32[1,1,32]{2,1,0:T(1,128)} %wants.1), custom_call_target="tpu_custom_call" | custom-call | tf_op jit(solution)/shard_map/spread_wants/pallas_call | solution.py:37
  1.9 7.7 %all-to-all-start = ((s32[16,1,128]{2,1,0:T(1,128)}), s32[16,1,128]{2,1,0:T(1,128)S(1)}, u32[]{:S(2)}, u32[]{:S(2)}) async-start(s32[16,1,128]{2,1,0:T(1,128)} %spread_wants.1), calls=%async_computation | async-start | bytes 16384 | tf_op jit(solution)/shard_map/all_to_all | solution.py:316
  9.6 0.0 copy-start
  9.7 1.0 collective-permute-start.3
  10.7 3.8 %collective-permute-start.2 = (s32[1,1,32]{2,1,0:T(1,128)}, s32[1,1,32]{2,1,0:T(1,128)S(1)}, u32[]{:S(2)}, u32[]{:S(2)}) collective-permute-start(s32[1,1,32]{2,1,0:T(1,128)} %refs_1_.1), channel_id=1, source_target_pairs={{0,96},{16,112},{32,0},{48,16},{64,32},{80,48},{96,64},{112,80},{1... | collective-permute-start | bytes 392 | tf_op jit(solution)/shard_map/ppermute | solution.py:291
  14.5 0.0 collective-permute-start.1
  14.5 0.7 collective-permute-start
  15.2 0.2 collective-permute-done.2.refs_3_.refs_4_
  15.3 0.9 collective-permute-start.6
  16.2 2.2 %collective-permute-done.1.refs_2_.refs_3_ = s32[1,1,32]{2,1,0:T(1,128)S(1)} collective-permute-done((s32[1,1,32]{2,1,0:T(1,128)}, s32[1,1,32]{2,1,0:T(1,128)S(1)}, u32[]{:S(2)}, u32[]{:S(2)}) %collective-permute-start.1) | collective-permute-done | bytes 160 | tf_op jit(solution)/shard_map/ppermute | solution.py:291
  18.5 1.5 %collective-permute-start.5 = (s32[1,1,32]{2,1,0:T(1,128)S(1)}, s32[1,1,32]{2,1,0:T(1,128)S(1)}, u32[]{:S(2)}, u32[]{:S(2)}) collective-permute-start(s32[1,1,32]{2,1,0:T(1,128)S(1)} %collective-permute-done.1.refs_2_.refs_3_), channel_id=1, source_target_pairs={{0,16},{16,0},{32,48},{48,32},{64,80},{80,64},{96,112},{112,96},{1... | collective-permute-start | bytes 392 | tf_op jit(solution)/shard_map/ppermute | solution.py:287
  20.0 0.0 collective-permute-done.refs_1_.refs_2_
  20.0 0.0 collective-permute-start.4
  20.0 0.0 collective-permute-done.3.refs_4_.refs_5_
  20.0 0.0 collective-permute-done.6.refs_7_.refs_8_
  20.0 0.8 collective-permute-done.5.refs_6_.refs_7_
  20.8 0.3 collective-permute-done.4.refs_5_.refs_6_
  21.1 0.0 all-to-all-done.col_asked.refs_0_
  21.1 0.7 copy-done.3
  21.8 0.7 copy-done.5
  22.4 5.0 %first_outgoing.1 = (bf16[32,128,128]{2,1,0:T(8,128)(2,1)}, bf16[8,128,128]{2,1,0:T(8,128)(2,1)S(1)}, bf16[8,128,128]{2,1,0:T(8,128)(2,1)S(1)}, bf16[8,128,128]{2,1,0:T(8,128)(2,1)S(1)}, bf16[8,128,128]{2,1,0:T(8,128)(2,1)S(1)}) custom-call(s32[32]{0:T(128)S(1)} %copy-done.3, s32[16,1,128]{2,1,0:T(1,128)S(1)} %all-to-all-done.col_asked.refs_0_, ...), custom_call_target="tpu_custom_call" | custom-call | tf_op jit(solution)/shard_map/first_outgoing/pallas_call | solution.py:80
  27.5 0.1 collective-permute-start.7
  27.5 1.5 %collective-permute-start.8 = (bf16[8,128,128]{2,1,0:T(8,128)(2,1)S(1)}, bf16[8,128,128]{2,1,0:T(8,128)(2,1)S(1)}, u32[]{:S(2)}, u32[]{:S(2)}) collective-permute-start(bf16[8,128,128]{2,1,0:T(8,128)(2,1)S(1)} %get-tuple-element.16), channel_id=1, source_target_pairs={{0,64},{16,80},{32,96},{48,112},{64,0},{80,16},{96,32},{112,48},{1... | collective-permute-start | bytes 786440 | tf_op jit(solution)/shard_map/ppermute | solution.py:291
  29.1 2.0 %collective-permute-start.9 = (bf16[8,128,128]{2,1,0:T(8,128)(2,1)S(1)}, bf16[8,128,128]{2,1,0:T(8,128)(2,1)S(1)}, u32[]{:S(2)}, u32[]{:S(2)}) collective-permute-start(bf16[8,128,128]{2,1,0:T(8,128)(2,1)S(1)} %get-tuple-element.17), channel_id=1, source_target_pairs={{0,96},{16,112},{32,0},{48,16},{64,32},{80,48},{96,64},{112,80},{1... | collective-permute-start | bytes 786440 | tf_op jit(solution)/shard_map/ppermute | solution.py:291
  31.0 7.0 %all-to-all-start.1 = ((bf16[16,2,128,128]{3,2,1,0:T(8,128)(2,1)}), bf16[16,2,128,128]{3,2,1,0:T(8,128)(2,1)}, u32[]{:S(2)}, u32[]{:S(2)}) async-start(bf16[16,2,128,128]{3,2,1,0:T(8,128)(2,1)} %bitcast.18), calls=%async_computation.1 | async-start | bytes 2097152 | tf_op jit(solution)/shard_map/all_to_all | solution.py:323
  38.0 1.5 %collective-permute-start.10 = (bf16[8,128,128]{2,1,0:T(8,128)(2,1)S(1)}, bf16[8,128,128]{2,1,0:T(8,128)(2,1)S(1)}, u32[]{:S(2)}, u32[]{:S(2)}) collective-permute-start(bf16[8,128,128]{2,1,0:T(8,128)(2,1)S(1)} %get-tuple-element.14.refs_0_), channel_id=1, source_target_pairs={{0,16},{16,0},{32,48},{48,32},{64,80},{80,64},{96,112},{112,96},{1... | collective-permute-start | bytes 786440 | tf_op jit(solution)/shard_map/ppermute | solution.py:287
  39.5 2.5 %collective-permute-done.7.refs_1_ = bf16[8,128,128]{2,1,0:T(8,128)(2,1)S(1)} collective-permute-done((bf16[8,128,128]{2,1,0:T(8,128)(2,1)S(1)}, bf16[8,128,128]{2,1,0:T(8,128)(2,1)S(1)}, u32[]{:S(2)}, u32[]{:S(2)}) %collective-permute-start.7) | collective-permute-done | bytes 262176 | tf_op jit(solution)/shard_map/ppermute | solution.py:291
  42.1 1.0 collective-permute-start.11
  43.1 0.0 collective-permute-done.8.refs_2_
  43.1 0.0 collective-permute-start.12
  43.1 0.0 collective-permute-done.9.refs_3_
  43.1 0.6 collective-permute-start.13
  43.7 0.0 collective-permute-done.10.refs_4_
  43.7 0.5 collective-permute-done.11.refs_5_
  44.2 0.4 collective-permute-done.12.refs_6_
  44.6 0.4 collective-permute-done.13.refs_7_
  45.0 0.7 copy-done.11
  45.7 0.0 copy-done.7
  45.7 0.0 copy-done.9
  45.7 0.0 copy-start.1
  45.7 0.0 copy-start.2
  45.7 0.0 copy-start.6
  45.8 10.4 %row_part.2.refs_12_ = f32[32,128,128]{2,1,0:T(8,128)} custom-call(s32[8,32]{1,0:T(8,128)S(1)} %bitcast.13, f32[8,32]{1,0:T(8,128)S(1)} %bitcast.15, s32[32]{0:T(128)S(1)} %copy-done.4, f32[32]{0:T(128)S(1)} %copy-done.7, f32[32,128]{1,0:T(8,128)S(1)} %copy-done, bf16[8,128,128]{2,1,0:T(8,128)(2,1)S(1)} %get-tuple-element.14.refs_0_, ...), custom_call_target="tpu_custom_call" | custom-call | flops 6442450944 | bytes 16777216 | tf_op jit(solution)/shard_map/row_part/pallas_call | solution.py:191
  56.2 0.0 all-to-all-done.1
  56.2 11.7 %col_part.2 = (f32[32,128,128]{2,1,0:T(8,128)}, bf16[32,128,128]{2,1,0:T(8,128)(2,1)}, bf16[8,128,128]{2,1,0:T(8,128)(2,1)S(1)}, bf16[8,128,128]{2,1,0:T(8,128)(...) custom-call(s32[8,32]{1,0:T(8,128)S(1)} %bitcast.9, f32[8,32]{1,0:T(8,128)S(1)} %bitcast.11, ...), custom_call_target="tpu_custom_call" | custom-call | flops 2147483648 | bytes 16777216 | tf_op jit(solution)/shard_map/col_part/pallas_call | solution.py:267
  68.0 0.7 collective-permute-start.14
  68.7 2.7 %collective-permute-start.15 = (bf16[8,128,128]{2,1,0:T(8,128)(2,1)S(1)}, bf16[8,128,128]{2,1,0:T(8,128)(2,1)S(1)}, u32[]{:S(2)}, u32[]{:S(2)}) collective-permute-start(bf16[8,128,128]{2,1,0:T(8,128)(2,1)S(1)} %get-tuple-element.22), channel_id=1, source_target_pairs={{0,64},{16,80},{32,96},{48,112},{64,0},{80,16},{96,32},{112,48},{1... | collective-permute-start | bytes 786440 | tf_op jit(solution)/shard_map/ppermute | solution.py:291
  71.4 0.0 collective-permute-start.16
  71.4 6.9 %all-to-all-start.2 = ((bf16[16,2,128,128]{3,2,1,0:T(8,128)(2,1)}), bf16[16,2,128,128]{3,2,1,0:T(8,128)(2,1)S(1)}, u32[]{:S(2)}, u32[]{:S(2)}) async-start(bf16[16,2,128,128]{3,2,1,0:T(8,128)(2,1)} %bitcast.17), calls=%async_computation.2 | async-start | bytes 2097152 | tf_op jit(solution)/shard_map/all_to_all | solution.py:323
  78.4 1.5 %collective-permute-start.17 = (bf16[8,128,128]{2,1,0:T(8,128)(2,1)S(1)}, bf16[8,128,128]{2,1,0:T(8,128)(2,1)S(1)}, u32[]{:S(2)}, u32[]{:S(2)}) collective-permute-start(bf16[8,128,128]{2,1,0:T(8,128)(2,1)S(1)} %get-tuple-element.20.refs_0_), channel_id=1, source_target_pairs={{0,16},{16,0},{32,48},{48,32},{64,80},{80,64},{96,112},{112,96},{1... | collective-permute-start | bytes 786440 | tf_op jit(solution)/shard_map/ppermute | solution.py:287
  79.9 0.0 collective-permute-done.14.refs_1_
  79.9 0.1 collective-permute-start.18
  80.0 3.1 %collective-permute-done.15.refs_2_ = bf16[8,128,128]{2,1,0:T(8,128)(2,1)S(1)} collective-permute-done((bf16[8,128,128]{2,1,0:T(8,128)(2,1)S(1)}, bf16[8,128,128]{2,1,0:T(8,128)(2,1)S(1)}, u32[]{:S(2)}, u32[]{:S(2)}) %collective-permute-start.15) | collective-permute-done | bytes 262176 | tf_op jit(solution)/shard_map/ppermute | solution.py:291
  83.1 1.2 %collective-permute-start.19 = (bf16[8,128,128]{2,1,0:T(8,128)(2,1)S(1)}, bf16[8,128,128]{2,1,0:T(8,128)(2,1)S(1)}, u32[]{:S(2)}, u32[]{:S(2)}) collective-permute-start(bf16[8,128,128]{2,1,0:T(8,128)(2,1)S(1)} %collective-permute-done.15.refs_2_), channel_id=1, source_target_pairs={{0,16},{16,0},{32,48},{48,32},{64,80},{80,64},{96,112},{112,96},{1... | collective-permute-start | bytes 786440 | tf_op jit(solution)/shard_map/ppermute | solution.py:287
  84.3 0.0 collective-permute-done.16.refs_3_
  84.3 0.0 collective-permute-start.20
  84.3 0.0 collective-permute-done.17.refs_4_
  84.3 0.0 collective-permute-done.18.refs_5_
  84.3 1.1 %collective-permute-done.19.refs_6_ = bf16[8,128,128]{2,1,0:T(8,128)(2,1)S(1)} collective-permute-done((bf16[8,128,128]{2,1,0:T(8,128)(2,1)S(1)}, bf16[8,128,128]{2,1,0:T(8,128)(2,1)S(1)}, u32[]{:S(2)}, u32[]{:S(2)}) %collective-permute-start.19) | collective-permute-done | bytes 262176 | tf_op jit(solution)/shard_map/ppermute | solution.py:287
  85.5 0.4 collective-permute-done.20.refs_7_
  85.8 0.7 copy-done.10
  86.6 10.4 %row_part.3.refs_3_ = f32[32,128,128]{2,1,0:T(8,128)} custom-call(s32[8,32]{1,0:T(8,128)S(1)} %bitcast.14, f32[8,32]{1,0:T(8,128)S(1)} %bitcast.16, s32[32]{0:T(128)S(1)} %copy-done.4, f32[32]{0:T(128)S(1)} %copy-done.7, f32[32,128]{1,0:T(8,128)S(1)} %copy-done, bf16[8,128,128]{2,1,0:T(8,128)(2,1)S(1)} %get-tuple-element.20.refs_0_, ...), custom_call_target="tpu_custom_call" | custom-call | flops 6442450944 | bytes 16777216 | tf_op jit(solution)/shard_map/row_part/pallas_call | solution.py:191
  97.0 0.0 all-to-all-done.2
  97.0 9.4 %col_part.3 = (f32[32,128,128]{2,1,0:T(8,128)}, f32[32,128,128]{2,1,0:T(8,128)}) custom-call(s32[8,32]{1,0:T(8,128)S(1)} %bitcast.10, f32[8,32]{1,0:T(8,128)S(1)} %bitcast.12, s32[32]{0:T(128)S(1)} %copy-done.4, f32[32]{0:T(128)S(1)} %copy-done.7, f32[32,128]{1,0:T(8,128)S(1)} %copy-done, bf16[32,8,128,128]{3,2,1,0:T(8,128)(2,1)} %refs_0_.3, ...), custom_call_target="tpu_custom_call" | custom-call | flops 2147483648 | bytes 16777216 | tf_op jit(solution)/shard_map/col_part/pallas_call | solution.py:267
  (14 shorter events, 0.0 us)
Async XLA Ops:
  1.9 43.8 %copy-start.4 = (s32[32]{0:T(128)S(1)}, s32[32]{0:T(128)}, u32[]{:S(2)}) copy-start(s32[32]{0:T(128)} %sizes.9) | copy-start | bytes 388
  1.9 43.8 %copy-start.7 = (f32[32]{0:T(128)S(1)}, f32[32]{0:T(128)}, u32[]{:S(2)}) copy-start(f32[32]{0:T(128)} %shift.7) | copy-start | bytes 388
  1.9 43.8 %copy-start.8 = (s32[32,8]{0,1:T(8,128)S(1)}, s32[32,8]{0,1:T(8,128)}, u32[]{:S(2)}) copy-start(s32[32,8]{0,1:T(8,128)} %param.23) | copy-start | bytes 3076
  1.9 43.8 %copy-start.9 = (f32[32,8]{0,1:T(8,128)S(1)}, f32[32,8]{0,1:T(8,128)}, u32[]{:S(2)}) copy-start(f32[32,8]{0,1:T(8,128)} %param.20) | copy-start | bytes 3076
  1.9 19.2 %all-to-all-start = ((s32[16,1,128]{2,1,0:T(1,128)}), s32[16,1,128]{2,1,0:T(1,128)S(1)}, u32[]{:S(2)}, u32[]{:S(2)}) async-start(s32[16,1,128]{2,1,0:T(1,128)} %spread_wants.1), calls=%async_computation | async-start | bytes 16384 | tf_op jit(solution)/shard_map/all_to_all | solution.py:316
  9.6 36.1 %copy-start = (f32[32,128]{1,0:T(8,128)S(1)}, f32[32,128]{1,0:T(8,128)}, u32[]{:S(2)}) copy-start(f32[32,128]{1,0:T(8,128)} %eps.7) | copy-start | bytes 49156
  9.7 10.3 %collective-permute-start.3 = (s32[1,1,32]{2,1,0:T(1,128)}, s32[1,1,32]{2,1,0:T(1,128)S(1)}, u32[]{:S(2)}, u32[]{:S(2)}) collective-permute-start(s32[1,1,32]{2,1,0:T(1,128)} %refs_1_.1), channel_id=1, source_target_pairs={{0,16},{16,0},{32,48},{48,32},{64,80},{80,64},{96,112},{112,96},{1... | collective-permute-start | bytes 392 | tf_op jit(solution)/shard_map/ppermute | solution.py:287
  10.7 4.6 %collective-permute-start.2 = (s32[1,1,32]{2,1,0:T(1,128)}, s32[1,1,32]{2,1,0:T(1,128)S(1)}, u32[]{:S(2)}, u32[]{:S(2)}) collective-permute-start(s32[1,1,32]{2,1,0:T(1,128)} %refs_1_.1), channel_id=1, source_target_pairs={{0,96},{16,112},{32,0},{48,16},{64,32},{80,48},{96,64},{112,80},{1... | collective-permute-start | bytes 392 | tf_op jit(solution)/shard_map/ppermute | solution.py:291
  14.5 4.0 %collective-permute-start.1 = (s32[1,1,32]{2,1,0:T(1,128)}, s32[1,1,32]{2,1,0:T(1,128)S(1)}, u32[]{:S(2)}, u32[]{:S(2)}) collective-permute-start(s32[1,1,32]{2,1,0:T(1,128)} %refs_1_.1), channel_id=1, source_target_pairs={{0,64},{16,80},{32,96},{48,112},{64,0},{80,16},{96,32},{112,48},{1... | collective-permute-start | bytes 392 | tf_op jit(solution)/shard_map/ppermute | solution.py:291
  14.5 5.5 %collective-permute-start = (s32[1,1,32]{2,1,0:T(1,128)}, s32[1,1,32]{2,1,0:T(1,128)S(1)}, u32[]{:S(2)}, u32[]{:S(2)}) collective-permute-start(s32[1,1,32]{2,1,0:T(1,128)} %refs_1_.1), channel_id=1, source_target_pairs={{0,32},{16,48},{32,64},{48,80},{64,96},{80,112},{96,0},{112,16},{1... | collective-permute-start | bytes 392 | tf_op jit(solution)/shard_map/ppermute | solution.py:291
  15.3 4.7 %collective-permute-start.6 = (s32[1,1,32]{2,1,0:T(1,128)S(1)}, s32[1,1,32]{2,1,0:T(1,128)S(1)}, u32[]{:S(2)}, u32[]{:S(2)}) collective-permute-start(s32[1,1,32]{2,1,0:T(1,128)S(1)} %collective-permute-done.2.refs_3_.refs_4_), channel_id=1, source_target_pairs={{0,16},{16,0},{32,48},{48,32},{64,80},{80,64},{96,112},{112,96},{1... | collective-permute-start | bytes 392 | tf_op jit(solution)/shard_map/ppermute | solution.py:287
  18.5 2.3 %collective-permute-start.5 = (s32[1,1,32]{2,1,0:T(1,128)S(1)}, s32[1,1,32]{2,1,0:T(1,128)S(1)}, u32[]{:S(2)}, u32[]{:S(2)}) collective-permute-start(s32[1,1,32]{2,1,0:T(1,128)S(1)} %collective-permute-done.1.refs_2_.refs_3_), channel_id=1, source_target_pairs={{0,16},{16,0},{32,48},{48,32},{64,80},{80,64},{96,112},{112,96},{1... | collective-permute-start | bytes 392 | tf_op jit(solution)/shard_map/ppermute | solution.py:287
  20.0 1.1 %collective-permute-start.4 = (s32[1,1,32]{2,1,0:T(1,128)S(1)}, s32[1,1,32]{2,1,0:T(1,128)S(1)}, u32[]{:S(2)}, u32[]{:S(2)}) collective-permute-start(s32[1,1,32]{2,1,0:T(1,128)S(1)} %collective-permute-done.refs_1_.refs_2_), channel_id=1, source_target_pairs={{0,16},{16,0},{32,48},{48,32},{64,80},{80,64},{96,112},{112,96},{1... | collective-permute-start | bytes 392 | tf_op jit(solution)/shard_map/ppermute | solution.py:287
  21.1 0.7 copy-start.3
  21.8 0.7 copy-start.5
  27.5 14.6 %collective-permute-start.7 = (bf16[8,128,128]{2,1,0:T(8,128)(2,1)S(1)}, bf16[8,128,128]{2,1,0:T(8,128)(2,1)S(1)}, u32[]{:S(2)}, u32[]{:S(2)}) collective-permute-start(bf16[8,128,128]{2,1,0:T(8,128)(2,1)S(1)} %get-tuple-element.15), channel_id=1, source_target_pairs={{0,32},{16,48},{32,64},{48,80},{64,96},{80,112},{96,0},{112,16},{1... | collective-permute-start | bytes 786440 | tf_op jit(solution)/shard_map/ppermute | solution.py:291
  27.5 15.5 %collective-permute-start.8 = (bf16[8,128,128]{2,1,0:T(8,128)(2,1)S(1)}, bf16[8,128,128]{2,1,0:T(8,128)(2,1)S(1)}, u32[]{:S(2)}, u32[]{:S(2)}) collective-permute-start(bf16[8,128,128]{2,1,0:T(8,128)(2,1)S(1)} %get-tuple-element.16), channel_id=1, source_target_pairs={{0,64},{16,80},{32,96},{48,112},{64,0},{80,16},{96,32},{112,48},{1... | collective-permute-start | bytes 786440 | tf_op jit(solution)/shard_map/ppermute | solution.py:291
  29.1 14.0 %collective-permute-start.9 = (bf16[8,128,128]{2,1,0:T(8,128)(2,1)S(1)}, bf16[8,128,128]{2,1,0:T(8,128)(2,1)S(1)}, u32[]{:S(2)}, u32[]{:S(2)}) collective-permute-start(bf16[8,128,128]{2,1,0:T(8,128)(2,1)S(1)} %get-tuple-element.17), channel_id=1, source_target_pairs={{0,96},{16,112},{32,0},{48,16},{64,32},{80,48},{96,64},{112,80},{1... | collective-permute-start | bytes 786440 | tf_op jit(solution)/shard_map/ppermute | solution.py:291
  31.0 25.2 %all-to-all-start.1 = ((bf16[16,2,128,128]{3,2,1,0:T(8,128)(2,1)}), bf16[16,2,128,128]{3,2,1,0:T(8,128)(2,1)}, u32[]{:S(2)}, u32[]{:S(2)}) async-start(bf16[16,2,128,128]{3,2,1,0:T(8,128)(2,1)} %bitcast.18), calls=%async_computation.1 | async-start | bytes 2097152 | tf_op jit(solution)/shard_map/all_to_all | solution.py:323
  38.0 5.7 %collective-permute-start.10 = (bf16[8,128,128]{2,1,0:T(8,128)(2,1)S(1)}, bf16[8,128,128]{2,1,0:T(8,128)(2,1)S(1)}, u32[]{:S(2)}, u32[]{:S(2)}) collective-permute-start(bf16[8,128,128]{2,1,0:T(8,128)(2,1)S(1)} %get-tuple-element.14.refs_0_), channel_id=1, source_target_pairs={{0,16},{16,0},{32,48},{48,32},{64,80},{80,64},{96,112},{112,96},{1... | collective-permute-start | bytes 786440 | tf_op jit(solution)/shard_map/ppermute | solution.py:287
  42.1 2.2 %collective-permute-start.11 = (bf16[8,128,128]{2,1,0:T(8,128)(2,1)S(1)}, bf16[8,128,128]{2,1,0:T(8,128)(2,1)S(1)}, u32[]{:S(2)}, u32[]{:S(2)}) collective-permute-start(bf16[8,128,128]{2,1,0:T(8,128)(2,1)S(1)} %collective-permute-done.7.refs_1_), channel_id=1, source_target_pairs={{0,16},{16,0},{32,48},{48,32},{64,80},{80,64},{96,112},{112,96},{1... | collective-permute-start | bytes 786440 | tf_op jit(solution)/shard_map/ppermute | solution.py:287
  43.1 1.5 %collective-permute-start.12 = (bf16[8,128,128]{2,1,0:T(8,128)(2,1)S(1)}, bf16[8,128,128]{2,1,0:T(8,128)(2,1)S(1)}, u32[]{:S(2)}, u32[]{:S(2)}) collective-permute-start(bf16[8,128,128]{2,1,0:T(8,128)(2,1)S(1)} %collective-permute-done.8.refs_2_), channel_id=1, source_target_pairs={{0,16},{16,0},{32,48},{48,32},{64,80},{80,64},{96,112},{112,96},{1... | collective-permute-start | bytes 786440 | tf_op jit(solution)/shard_map/ppermute | solution.py:287
  43.1 1.9 %collective-permute-start.13 = (bf16[8,128,128]{2,1,0:T(8,128)(2,1)S(1)}, bf16[8,128,128]{2,1,0:T(8,128)(2,1)S(1)}, u32[]{:S(2)}, u32[]{:S(2)}) collective-permute-start(bf16[8,128,128]{2,1,0:T(8,128)(2,1)S(1)} %collective-permute-done.9.refs_3_), channel_id=1, source_target_pairs={{0,16},{16,0},{32,48},{48,32},{64,80},{80,64},{96,112},{112,96},{1... | collective-permute-start | bytes 786440 | tf_op jit(solution)/shard_map/ppermute | solution.py:287
  45.0 0.7 copy-start.11
  45.7 10.5 %copy-start.1 = (s32[32,8]{0,1:T(8,128)S(1)}, s32[32,8]{0,1:T(8,128)}, u32[]{:S(2)}) copy-start(s32[32,8]{0,1:T(8,128)} %param.22) | copy-start | bytes 3076
  45.7 10.5 %copy-start.2 = (f32[32,8]{0,1:T(8,128)S(1)}, f32[32,8]{0,1:T(8,128)}, u32[]{:S(2)}) copy-start(f32[32,8]{0,1:T(8,128)} %param.21) | copy-start | bytes 3076
  45.7 10.5 %copy-start.6 = (s32[1,1,32]{2,1,0:T(1,128)S(1)}, s32[1,1,32]{2,1,0:T(1,128)}, u32[]{:S(2)}) copy-start(s32[1,1,32]{2,1,0:T(1,128)} %refs_1_.1) | copy-start | bytes 388
  68.0 12.0 %collective-permute-start.14 = (bf16[8,128,128]{2,1,0:T(8,128)(2,1)S(1)}, bf16[8,128,128]{2,1,0:T(8,128)(2,1)S(1)}, u32[]{:S(2)}, u32[]{:S(2)}) collective-permute-start(bf16[8,128,128]{2,1,0:T(8,128)(2,1)S(1)} %get-tuple-element.21), channel_id=1, source_target_pairs={{0,32},{16,48},{32,64},{48,80},{64,96},{80,112},{96,0},{112,16},{1... | collective-permute-start | bytes 786440 | tf_op jit(solution)/shard_map/ppermute | solution.py:291
  68.7 14.4 %collective-permute-start.15 = (bf16[8,128,128]{2,1,0:T(8,128)(2,1)S(1)}, bf16[8,128,128]{2,1,0:T(8,128)(2,1)S(1)}, u32[]{:S(2)}, u32[]{:S(2)}) collective-permute-start(bf16[8,128,128]{2,1,0:T(8,128)(2,1)S(1)} %get-tuple-element.22), channel_id=1, source_target_pairs={{0,64},{16,80},{32,96},{48,112},{64,0},{80,16},{96,32},{112,48},{1... | collective-permute-start | bytes 786440 | tf_op jit(solution)/shard_map/ppermute | solution.py:291
  71.4 12.9 %collective-permute-start.16 = (bf16[8,128,128]{2,1,0:T(8,128)(2,1)S(1)}, bf16[8,128,128]{2,1,0:T(8,128)(2,1)S(1)}, u32[]{:S(2)}, u32[]{:S(2)}) collective-permute-start(bf16[8,128,128]{2,1,0:T(8,128)(2,1)S(1)} %get-tuple-element.23), channel_id=1, source_target_pairs={{0,96},{16,112},{32,0},{48,16},{64,32},{80,48},{96,64},{112,80},{1... | collective-permute-start | bytes 786440 | tf_op jit(solution)/shard_map/ppermute | solution.py:291
  71.4 25.5 %all-to-all-start.2 = ((bf16[16,2,128,128]{3,2,1,0:T(8,128)(2,1)}), bf16[16,2,128,128]{3,2,1,0:T(8,128)(2,1)S(1)}, u32[]{:S(2)}, u32[]{:S(2)}) async-start(bf16[16,2,128,128]{3,2,1,0:T(8,128)(2,1)} %bitcast.17), calls=%async_computation.2 | async-start | bytes 2097152 | tf_op jit(solution)/shard_map/all_to_all | solution.py:323
  78.4 5.9 %collective-permute-start.17 = (bf16[8,128,128]{2,1,0:T(8,128)(2,1)S(1)}, bf16[8,128,128]{2,1,0:T(8,128)(2,1)S(1)}, u32[]{:S(2)}, u32[]{:S(2)}) collective-permute-start(bf16[8,128,128]{2,1,0:T(8,128)(2,1)S(1)} %get-tuple-element.20.refs_0_), channel_id=1, source_target_pairs={{0,16},{16,0},{32,48},{48,32},{64,80},{80,64},{96,112},{112,96},{1... | collective-permute-start | bytes 786440 | tf_op jit(solution)/shard_map/ppermute | solution.py:287
  79.9 4.4 %collective-permute-start.18 = (bf16[8,128,128]{2,1,0:T(8,128)(2,1)S(1)}, bf16[8,128,128]{2,1,0:T(8,128)(2,1)S(1)}, u32[]{:S(2)}, u32[]{:S(2)}) collective-permute-start(bf16[8,128,128]{2,1,0:T(8,128)(2,1)S(1)} %collective-permute-done.14.refs_1_), channel_id=1, source_target_pairs={{0,16},{16,0},{32,48},{48,32},{64,80},{80,64},{96,112},{112,96},{1... | collective-permute-start | bytes 786440 | tf_op jit(solution)/shard_map/ppermute | solution.py:287
  83.1 2.4 %collective-permute-start.19 = (bf16[8,128,128]{2,1,0:T(8,128)(2,1)S(1)}, bf16[8,128,128]{2,1,0:T(8,128)(2,1)S(1)}, u32[]{:S(2)}, u32[]{:S(2)}) collective-permute-start(bf16[8,128,128]{2,1,0:T(8,128)(2,1)S(1)} %collective-permute-done.15.refs_2_), channel_id=1, source_target_pairs={{0,16},{16,0},{32,48},{48,32},{64,80},{80,64},{96,112},{112,96},{1... | collective-permute-start | bytes 786440 | tf_op jit(solution)/shard_map/ppermute | solution.py:287
  84.3 1.5 %collective-permute-start.20 = (bf16[8,128,128]{2,1,0:T(8,128)(2,1)S(1)}, bf16[8,128,128]{2,1,0:T(8,128)(2,1)S(1)}, u32[]{:S(2)}, u32[]{:S(2)}) collective-permute-start(bf16[8,128,128]{2,1,0:T(8,128)(2,1)S(1)} %collective-permute-done.16.refs_3_), channel_id=1, source_target_pairs={{0,16},{16,0},{32,48},{48,32},{64,80},{80,64},{96,112},{112,96},{1... | collective-permute-start | bytes 786440 | tf_op jit(solution)/shard_map/ppermute | solution.py:287
  85.8 0.7 copy-start.10

commit v3 on v2

--- a/solution.py
+++ b/solution.py
@@ -44,20 +44,18 @@
 
 
 def start_outgoing(rounded, col_asked, lists, out_col, out_row, sems):
+    copies = []
+    for k in range(PAIRS):
+        wanted = col_asked[k // 2, 0, k % 2]
+        copies.append(pltpu.make_async_copy(rounded.at[wanted], out_col.at[k], sems.at[k]))
+    for copy in copies:
+        copy.start()
     me = lax.axis_index("row")
-    copies = []
     for dz in range(NZ):
         back = (NZ - dz) % NZ
         for part in range(2):
             for e in range(4):
-                wanted = lists[4 * part + back][0, 0, 4 * me + e]
-                spot = 4 * part + e
-                copies.append(pltpu.make_async_copy(rounded.at[wanted], out_row[dz].at[spot], sems.at[8 * dz + spot]))
-    for k in range(PAIRS):
-        wanted = col_asked[k // 2, 0, k % 2]
-        copies.append(pltpu.make_async_copy(rounded.at[wanted], out_col.at[k], sems.at[PAIRS + k]))
-    for copy in copies:
-        copy.start()
+                out_row[dz][4 * part + e] = rounded[lists[4 * part + back][0, 0, 4 * me + e]]
     return copies
 
 
@@ -80,9 +78,9 @@
     return pl.pallas_call(
         first_body,
         in_specs=[SMEM] + [SMEM] * 9 + [VMEM],
-        out_specs=[ANY] * 5,
+        out_specs=[ANY] + [VMEM] * NZ,
         out_shape=OUTGOING,
-        scratch_shapes=[pltpu.VMEM((PAIRS, W, W), BF16), pltpu.SemaphoreType.DMA((2 * PAIRS,))],
+        scratch_shapes=[pltpu.VMEM((PAIRS, W, W), BF16), pltpu.SemaphoreType.DMA((PAIRS,))],
         compiler_params=pltpu.CompilerParams(vmem_limit_bytes=52 * 2**20),
         name="first_outgoing",
     )(sizes, *asked, amp_start)
@@ -133,17 +131,9 @@
     pieces, refs = refs[:8], refs[8:]
     over_h, amp_h, exch_h, refs = refs[0], refs[1], refs[2], refs[3:]
     base_h, refs = refs[0], refs[1:]
-    over, table, amp, exch, base, table_sem, over_sem, amp_sem, exch_sem, base_sem = refs
+    over, table, amp, exch, base, over_sem, amp_sem, exch_sem, base_sem = refs
     me = lax.axis_index("row")
     core = lax.rem(me, 2)
-    loads = []
-    for dz in range(NZ):
-        chip = 8 * lax.rem(me // 2 + NZ - dz, NZ)
-        for part, from_core in ((0, core), (1, 1 - core)):
-            source = pieces[NZ * part + dz].at[pl.ds(4 * part, 4)]
-            loads.append(pltpu.make_async_copy(source, table.at[pl.ds(chip + 4 * from_core, 4)], table_sem.at[NZ * part + dz]))
-    for copy in loads:
-        copy.start()
     def fetch(c):
         chunk_copy(over_h, over, over_sem, c).start()
         chunk_copy(amp_h, amp, amp_sem, c).start()
@@ -152,8 +142,11 @@
     for c in range(AHEAD):
         fetch(c)
     eps_t = jnp.transpose(eps[...])
-    for copy in loads:
-        copy.wait()
+    for dz in range(NZ):
+        chip = 8 * lax.rem(me // 2 + NZ - dz, NZ)
+        for part, from_core in ((0, core), (1, 1 - core)):
+            for e in range(4):
+                table[chip + 4 * from_core + e] = pieces[NZ * part + dz][4 * part + e]
 
     def ready(c):
         if c + AHEAD < CHUNKS:
@@ -199,7 +192,6 @@
             chunked(),
             chunked(),
             chunked(),
-            pltpu.SemaphoreType.DMA((8,)),
         ]
         + [pltpu.SemaphoreType.DMA((CHUNKS,))] * 4,
         compiler_params=pltpu.CompilerParams(vmem_limit_bytes=52 * 2**20),
@@ -267,7 +259,7 @@
     return pl.pallas_call(
         functools.partial(col_body, first),
         in_specs=[SMEM] * 4 + [VMEM] + [SMEM] * len(asked) + [ANY, VMEM, ANY, ANY],
-        out_specs=[ANY] * 6 if first else [ANY] * 2,
+        out_specs=[ANY] * 2 + [VMEM] * NZ if first else [ANY] * 2,
         out_shape=[whole] + OUTGOING if first else [whole] * 2,
         scratch_shapes=[
             pltpu.VMEM((PAIRS, NK, W, W), BF16),
@@ -276,7 +268,7 @@
             chunked(BF16 if first else F32),
         ]
         + [pltpu.SemaphoreType.DMA((CHUNKS,))] * 5
-        + [pltpu.SemaphoreType.DMA((2 * PAIRS,))],
+        + [pltpu.SemaphoreType.DMA((PAIRS,))],
         compiler_params=pltpu.CompilerParams(vmem_limit_bytes=52 * 2**20),
         cost_estimate=cost(1),
         name="col_part",

time: 107 us -> 100 us (0.935)
  Pallas kernels: 48.2 us -> 41.4 us
    pallas_call x2, Pallas kernels: 20.8 us -> 17.9 us  [row_part(): pl.pallas_call(functools.partial(row_body, first), in_specs=[SMEM] * 4 +...]
    pallas_call x2, Pallas kernels: 21.1 us -> 19 us  [col_part(): pl.pallas_call(functools.partial(col_body, first), in_specs=[SMEM] * 4 +...]
    pallas_call x1, Pallas kernels: 5.01 us -> 3.13 us  [first_outgoing(): pl.pallas_call(first_body, in_specs=[SMEM] + [SMEM] * 9 + [VMEM], out_spe...]
  transfers between devices with their start and end apart: 24 -> 24, of which waited for: 11 -> 11; matrix products, arithmetic and copies ran while one was open for 0% -> 0% of each run, Pallas kernels for 20% -> 18%
where the time goes in v3:
time: 100 us; the launch traced here: 99.7 us
  starting transfers between devices  42.6 us (43%)
  Pallas kernels  41.4 us (41%)
  waiting for transfers between devices  11.9 us (12%)
  local copies, waits for them, and re-layouts  2.76 us (3%)
  between operations  1.01 us (1%)
    pallas_call x2, Pallas kernels, col_part(): pl.pallas_call(functools.partial(col_body, first), in_specs=[SMEM] * 4 +...  19 us
    pallas_call x2, Pallas kernels, row_part(): pl.pallas_call(functools.partial(row_body, first), in_specs=[SMEM] * 4 +...  17.9 us
    all_to_all x2, starting transfers between devices, shards(): lax.all_to_all(out[0].reshape(16, 2, W, W), 'col', 0, 0, tiled=True)  13.9 us
    ppermute x9, starting transfers between devices, shift_z(): return lax.ppermute(x, 'row', [(i, (i + 2 * dz) % 8) for i in range(8)])  11.5 us
    ppermute x12, starting transfers between devices, swap_core(): return lax.ppermute(x, 'row', [(i, i ^ 1) for i in range(8)])  9.47 us
    ppermute x9, waiting for transfers between devices, shift_z(): return lax.ppermute(x, 'row', [(i, (i + 2 * dz) % 8) for i in range(8)])  7.99 us
    all_to_all x1, starting transfers between devices, shards(): col_asked = lax.all_to_all(spread_wants(col_wants), 'col', 0, 0, tiled=True)  7.73 us
    ppermute x12, waiting for transfers between devices, swap_core(): return lax.ppermute(x, 'row', [(i, i ^ 1) for i in range(8)])  3.92 us
  transfers between devices with their start and end apart: 24, of which 11 were waited for; matrix products, arithmetic and copies ran while one was open for 0% of the time, Pallas kernels for 18%

profile of v3, /device:TPU:1, one launch (start us, length us, event | category | flops | bytes accessed | tf_op | source)
XLA Modules:
  0.0 99.7 jit_solution(15172813064239045218)
XLA Ops:
  0.6 1.3 %spread_wants.1 = s32[16,1,128]{2,1,0:T(1,128)} custom-call(s32[1,1,32]{2,1,0:T(1,128)} %wants.1), custom_call_target="tpu_custom_call" | custom-call | tf_op jit(solution)/shard_map/spread_wants/pallas_call | solution.py:37
  1.9 7.7 %all-to-all-start = ((s32[16,1,128]{2,1,0:T(1,128)}), s32[16,1,128]{2,1,0:T(1,128)S(1)}, u32[]{:S(2)}, u32[]{:S(2)}) async-start(s32[16,1,128]{2,1,0:T(1,128)} %spread_wants.1), calls=%async_computation | async-start | bytes 16384 | tf_op jit(solution)/shard_map/all_to_all | solution.py:308
  9.6 0.0 copy-start
  9.7 1.0 %collective-permute-start.3 = (s32[1,1,32]{2,1,0:T(1,128)}, s32[1,1,32]{2,1,0:T(1,128)S(1)}, u32[]{:S(2)}, u32[]{:S(2)}) collective-permute-start(s32[1,1,32]{2,1,0:T(1,128)} %refs_1_.1), channel_id=1, source_target_pairs={{0,16},{16,0},{32,48},{48,32},{64,80},{80,64},{96,112},{112,96},{1... | collective-permute-start | bytes 392 | tf_op jit(solution)/shard_map/ppermute | solution.py:279
  10.7 3.8 %collective-permute-start.2 = (s32[1,1,32]{2,1,0:T(1,128)}, s32[1,1,32]{2,1,0:T(1,128)S(1)}, u32[]{:S(2)}, u32[]{:S(2)}) collective-permute-start(s32[1,1,32]{2,1,0:T(1,128)} %refs_1_.1), channel_id=1, source_target_pairs={{0,96},{16,112},{32,0},{48,16},{64,32},{80,48},{96,64},{112,80},{1... | collective-permute-start | bytes 392 | tf_op jit(solution)/shard_map/ppermute | solution.py:283
  14.5 0.0 collective-permute-start.1
  14.5 0.7 collective-permute-start
  15.2 0.2 collective-permute-done.2.refs_3_.refs_4_
  15.3 0.9 collective-permute-start.6
  16.2 2.2 %collective-permute-done.1.refs_2_.refs_3_ = s32[1,1,32]{2,1,0:T(1,128)S(1)} collective-permute-done((s32[1,1,32]{2,1,0:T(1,128)}, s32[1,1,32]{2,1,0:T(1,128)S(1)}, u32[]{:S(2)}, u32[]{:S(2)}) %collective-permute-start.1) | collective-permute-done | bytes 160 | tf_op jit(solution)/shard_map/ppermute | solution.py:283
  18.5 1.5 %collective-permute-start.5 = (s32[1,1,32]{2,1,0:T(1,128)S(1)}, s32[1,1,32]{2,1,0:T(1,128)S(1)}, u32[]{:S(2)}, u32[]{:S(2)}) collective-permute-start(s32[1,1,32]{2,1,0:T(1,128)S(1)} %collective-permute-done.1.refs_2_.refs_3_), channel_id=1, source_target_pairs={{0,16},{16,0},{32,48},{48,32},{64,80},{80,64},{96,112},{112,96},{1... | collective-permute-start | bytes 392 | tf_op jit(solution)/shard_map/ppermute | solution.py:279
  20.0 0.0 collective-permute-done.refs_1_.refs_2_
  20.0 0.0 collective-permute-start.4
  20.0 0.0 collective-permute-done.3.refs_4_.refs_5_
  20.0 0.0 collective-permute-done.6.refs_7_.refs_8_
  20.0 0.8 collective-permute-done.5.refs_6_.refs_7_
  20.8 0.3 collective-permute-done.4.refs_5_.refs_6_
  21.1 0.0 all-to-all-done.col_asked.refs_0_
  21.1 0.7 copy-done.3
  21.8 0.7 copy-done.5
  22.4 3.1 %first_outgoing.1 = (bf16[32,128,128]{2,1,0:T(8,128)(2,1)}, bf16[8,128,128]{2,1,0:T(8,128)(2,1)S(1)}, bf16[8,128,128]{2,1,0:T(8,128)(2,1)S(1)}, bf16[8,128,128]{2,1,0:T(8,128)(2,1)S(1)}, bf16[8,128,128]{2,1,0:T(8,128)(2,1)S(1)}) custom-call(s32[32]{0:T(128)S(1)} %copy-done.3, s32[16,1,128]{2,1,0:T(1,128)S(1)} %all-to-all-done.col_asked.refs_0_, ...), custom_call_target="tpu_custom_call" | custom-call | tf_op jit(solution)/shard_map/first_outgoing/pallas_call | solution.py:78
  25.6 0.1 collective-permute-start.7
  25.7 1.5 %collective-permute-start.8 = (bf16[8,128,128]{2,1,0:T(8,128)(2,1)S(1)}, bf16[8,128,128]{2,1,0:T(8,128)(2,1)S(1)}, u32[]{:S(2)}, u32[]{:S(2)}) collective-permute-start(bf16[8,128,128]{2,1,0:T(8,128)(2,1)S(1)} %get-tuple-element.16), channel_id=1, source_target_pairs={{0,64},{16,80},{32,96},{48,112},{64,0},{80,16},{96,32},{112,48},{1... | collective-permute-start | bytes 786440 | tf_op jit(solution)/shard_map/ppermute | solution.py:283
  27.2 2.0 %collective-permute-start.9 = (bf16[8,128,128]{2,1,0:T(8,128)(2,1)S(1)}, bf16[8,128,128]{2,1,0:T(8,128)(2,1)S(1)}, u32[]{:S(2)}, u32[]{:S(2)}) collective-permute-start(bf16[8,128,128]{2,1,0:T(8,128)(2,1)S(1)} %get-tuple-element.17), channel_id=1, source_target_pairs={{0,96},{16,112},{32,0},{48,16},{64,32},{80,48},{96,64},{112,80},{1... | collective-permute-start | bytes 786440 | tf_op jit(solution)/shard_map/ppermute | solution.py:283
  29.2 7.0 %all-to-all-start.1 = ((bf16[16,2,128,128]{3,2,1,0:T(8,128)(2,1)}), bf16[16,2,128,128]{3,2,1,0:T(8,128)(2,1)}, u32[]{:S(2)}, u32[]{:S(2)}) async-start(bf16[16,2,128,128]{3,2,1,0:T(8,128)(2,1)} %bitcast.18), calls=%async_computation.1 | async-start | bytes 2097152 | tf_op jit(solution)/shard_map/all_to_all | solution.py:315
  36.2 1.5 %collective-permute-start.10 = (bf16[8,128,128]{2,1,0:T(8,128)(2,1)S(1)}, bf16[8,128,128]{2,1,0:T(8,128)(2,1)S(1)}, u32[]{:S(2)}, u32[]{:S(2)}) collective-permute-start(bf16[8,128,128]{2,1,0:T(8,128)(2,1)S(1)} %get-tuple-element.14.refs_0_), channel_id=1, source_target_pairs={{0,16},{16,0},{32,48},{48,32},{64,80},{80,64},{96,112},{112,96},{1... | collective-permute-start | bytes 786440 | tf_op jit(solution)/shard_map/ppermute | solution.py:279
  37.7 2.5 %collective-permute-done.7.refs_1_ = bf16[8,128,128]{2,1,0:T(8,128)(2,1)S(1)} collective-permute-done((bf16[8,128,128]{2,1,0:T(8,128)(2,1)S(1)}, bf16[8,128,128]{2,1,0:T(8,128)(2,1)S(1)}, u32[]{:S(2)}, u32[]{:S(2)}) %collective-permute-start.7) | collective-permute-done | bytes 262176 | tf_op jit(solution)/shard_map/ppermute | solution.py:283
  40.2 1.0 %collective-permute-start.11 = (bf16[8,128,128]{2,1,0:T(8,128)(2,1)S(1)}, bf16[8,128,128]{2,1,0:T(8,128)(2,1)S(1)}, u32[]{:S(2)}, u32[]{:S(2)}) collective-permute-start(bf16[8,128,128]{2,1,0:T(8,128)(2,1)S(1)} %collective-permute-done.7.refs_1_), channel_id=1, source_target_pairs={{0,16},{16,0},{32,48},{48,32},{64,80},{80,64},{96,112},{112,96},{1... | collective-permute-start | bytes 786440 | tf_op jit(solution)/shard_map/ppermute | solution.py:279
  41.2 0.0 collective-permute-done.8.refs_2_
  41.2 0.0 collective-permute-start.12
  41.2 0.0 collective-permute-done.9.refs_3_
  41.2 0.6 collective-permute-start.13
  41.8 0.0 collective-permute-done.10.refs_4_
  41.8 0.5 collective-permute-done.11.refs_5_
  42.4 0.4 collective-permute-done.12.refs_6_
  42.7 0.4 collective-permute-done.13.refs_7_
  43.1 0.7 copy-done.11
  43.8 0.0 copy-done.4
  43.8 0.0 copy-done.8
  43.8 0.0 copy-start.1
  43.9 0.0 copy-start.2
  43.9 0.0 copy-start.6
  43.9 9.0 %row_part.2.refs_12_ = f32[32,128,128]{2,1,0:T(8,128)} custom-call(s32[8,32]{1,0:T(8,128)S(1)} %bitcast.13, f32[8,32]{1,0:T(8,128)S(1)} %bitcast.15, s32[32]{0:T(128)S(1)} %copy-done.4, f32[32]{0:T(128)S(1)} %copy-done.7, f32[32,128]{1,0:T(8,128)S(1)} %copy-done, bf16[8,128,128]{2,1,0:T(8,128)(2,1)S(1)} %get-tuple-element.14.refs_0_, ...), custom_call_target="tpu_custom_call" | custom-call | flops 6442450944 | bytes 16777216 | tf_op jit(solution)/shard_map/row_part/pallas_call | solution.py:184
  52.9 0.0 all-to-all-done.1
  52.9 10.0 %col_part.2 = (f32[32,128,128]{2,1,0:T(8,128)}, bf16[32,128,128]{2,1,0:T(8,128)(2,1)}, bf16[8,128,128]{2,1,0:T(8,128)(2,1)S(1)}, bf16[8,128,128]{2,1,0:T(8,128)(...) custom-call(s32[8,32]{1,0:T(8,128)S(1)} %bitcast.9, f32[8,32]{1,0:T(8,128)S(1)} %bitcast.11, ...), custom_call_target="tpu_custom_call" | custom-call | flops 2147483648 | bytes 16777216 | tf_op jit(solution)/shard_map/col_part/pallas_call | solution.py:259
  62.9 0.7 collective-permute-start.14
  63.6 2.7 %collective-permute-start.15 = (bf16[8,128,128]{2,1,0:T(8,128)(2,1)S(1)}, bf16[8,128,128]{2,1,0:T(8,128)(2,1)S(1)}, u32[]{:S(2)}, u32[]{:S(2)}) collective-permute-start(bf16[8,128,128]{2,1,0:T(8,128)(2,1)S(1)} %get-tuple-element.22), channel_id=1, source_target_pairs={{0,64},{16,80},{32,96},{48,112},{64,0},{80,16},{96,32},{112,48},{1... | collective-permute-start | bytes 786440 | tf_op jit(solution)/shard_map/ppermute | solution.py:283
  66.3 0.0 collective-permute-start.16
  66.4 6.9 %all-to-all-start.2 = ((bf16[16,2,128,128]{3,2,1,0:T(8,128)(2,1)}), bf16[16,2,128,128]{3,2,1,0:T(8,128)(2,1)S(1)}, u32[]{:S(2)}, u32[]{:S(2)}) async-start(bf16[16,2,128,128]{3,2,1,0:T(8,128)(2,1)} %bitcast.17), calls=%async_computation.2 | async-start | bytes 2097152 | tf_op jit(solution)/shard_map/all_to_all | solution.py:315
  73.3 1.6 %collective-permute-start.17 = (bf16[8,128,128]{2,1,0:T(8,128)(2,1)S(1)}, bf16[8,128,128]{2,1,0:T(8,128)(2,1)S(1)}, u32[]{:S(2)}, u32[]{:S(2)}) collective-permute-start(bf16[8,128,128]{2,1,0:T(8,128)(2,1)S(1)} %get-tuple-element.20.refs_0_), channel_id=1, source_target_pairs={{0,16},{16,0},{32,48},{48,32},{64,80},{80,64},{96,112},{112,96},{1... | collective-permute-start | bytes 786440 | tf_op jit(solution)/shard_map/ppermute | solution.py:279
  74.8 0.0 collective-permute-done.14.refs_1_
  74.9 0.1 collective-permute-start.18
  75.0 3.0 %collective-permute-done.15.refs_2_ = bf16[8,128,128]{2,1,0:T(8,128)(2,1)S(1)} collective-permute-done((bf16[8,128,128]{2,1,0:T(8,128)(2,1)S(1)}, bf16[8,128,128]{2,1,0:T(8,128)(2,1)S(1)}, u32[]{:S(2)}, u32[]{:S(2)}) %collective-permute-start.15) | collective-permute-done | bytes 262176 | tf_op jit(solution)/shard_map/ppermute | solution.py:283
  78.0 1.2 %collective-permute-start.19 = (bf16[8,128,128]{2,1,0:T(8,128)(2,1)S(1)}, bf16[8,128,128]{2,1,0:T(8,128)(2,1)S(1)}, u32[]{:S(2)}, u32[]{:S(2)}) collective-permute-start(bf16[8,128,128]{2,1,0:T(8,128)(2,1)S(1)} %collective-permute-done.15.refs_2_), channel_id=1, source_target_pairs={{0,16},{16,0},{32,48},{48,32},{64,80},{80,64},{96,112},{112,96},{1... | collective-permute-start | bytes 786440 | tf_op jit(solution)/shard_map/ppermute | solution.py:279
  79.2 0.0 collective-permute-done.16.refs_3_
  79.2 0.0 collective-permute-start.20
  79.2 0.0 collective-permute-done.17.refs_4_
  79.2 0.0 collective-permute-done.18.refs_5_
  79.2 1.1 %collective-permute-done.19.refs_6_ = bf16[8,128,128]{2,1,0:T(8,128)(2,1)S(1)} collective-permute-done((bf16[8,128,128]{2,1,0:T(8,128)(2,1)S(1)}, bf16[8,128,128]{2,1,0:T(8,128)(2,1)S(1)}, u32[]{:S(2)}, u32[]{:S(2)}) %collective-permute-start.19) | collective-permute-done | bytes 262176 | tf_op jit(solution)/shard_map/ppermute | solution.py:279
  80.4 0.4 collective-permute-done.20.refs_7_
  80.8 0.7 copy-done.10
  81.5 9.0 %row_part.3.refs_3_ = f32[32,128,128]{2,1,0:T(8,128)} custom-call(s32[8,32]{1,0:T(8,128)S(1)} %bitcast.14, f32[8,32]{1,0:T(8,128)S(1)} %bitcast.16, s32[32]{0:T(128)S(1)} %copy-done.4, f32[32]{0:T(128)S(1)} %copy-done.7, f32[32,128]{1,0:T(8,128)S(1)} %copy-done, bf16[8,128,128]{2,1,0:T(8,128)(2,1)S(1)} %get-tuple-element.20.refs_0_, ...), custom_call_target="tpu_custom_call" | custom-call | flops 6442450944 | bytes 16777216 | tf_op jit(solution)/shard_map/row_part/pallas_call | solution.py:184
  90.4 0.0 all-to-all-done.2
  90.4 9.1 %col_part.3 = (f32[32,128,128]{2,1,0:T(8,128)}, f32[32,128,128]{2,1,0:T(8,128)}) custom-call(s32[8,32]{1,0:T(8,128)S(1)} %bitcast.10, f32[8,32]{1,0:T(8,128)S(1)} %bitcast.12, s32[32]{0:T(128)S(1)} %copy-done.4, f32[32]{0:T(128)S(1)} %copy-done.7, f32[32,128]{1,0:T(8,128)S(1)} %copy-done, bf16[32,8,128,128]{3,2,1,0:T(8,128)(2,1)} %refs_0_.3, ...), custom_call_target="tpu_custom_call" | custom-call | flops 2147483648 | bytes 16777216 | tf_op jit(solution)/shard_map/col_part/pallas_call | solution.py:259
  (14 shorter events, 0.0 us)
Async XLA Ops:
  1.9 41.9 %copy-start.4 = (s32[32]{0:T(128)S(1)}, s32[32]{0:T(128)}, u32[]{:S(2)}) copy-start(s32[32]{0:T(128)} %sizes.9) | copy-start | bytes 388
  1.9 41.9 %copy-start.7 = (f32[32]{0:T(128)S(1)}, f32[32]{0:T(128)}, u32[]{:S(2)}) copy-start(f32[32]{0:T(128)} %shift.7) | copy-start | bytes 388
  1.9 41.9 %copy-start.8 = (s32[32,8]{0,1:T(8,128)S(1)}, s32[32,8]{0,1:T(8,128)}, u32[]{:S(2)}) copy-start(s32[32,8]{0,1:T(8,128)} %param.23) | copy-start | bytes 3076
  1.9 41.9 %copy-start.9 = (f32[32,8]{0,1:T(8,128)S(1)}, f32[32,8]{0,1:T(8,128)}, u32[]{:S(2)}) copy-start(f32[32,8]{0,1:T(8,128)} %param.20) | copy-start | bytes 3076
  1.9 19.2 %all-to-all-start = ((s32[16,1,128]{2,1,0:T(1,128)}), s32[16,1,128]{2,1,0:T(1,128)S(1)}, u32[]{:S(2)}, u32[]{:S(2)}) async-start(s32[16,1,128]{2,1,0:T(1,128)} %spread_wants.1), calls=%async_computation | async-start | bytes 16384 | tf_op jit(solution)/shard_map/all_to_all | solution.py:308
  9.6 34.2 %copy-start = (f32[32,128]{1,0:T(8,128)S(1)}, f32[32,128]{1,0:T(8,128)}, u32[]{:S(2)}) copy-start(f32[32,128]{1,0:T(8,128)} %eps.7) | copy-start | bytes 49156
  9.7 10.3 %collective-permute-start.3 = (s32[1,1,32]{2,1,0:T(1,128)}, s32[1,1,32]{2,1,0:T(1,128)S(1)}, u32[]{:S(2)}, u32[]{:S(2)}) collective-permute-start(s32[1,1,32]{2,1,0:T(1,128)} %refs_1_.1), channel_id=1, source_target_pairs={{0,16},{16,0},{32,48},{48,32},{64,80},{80,64},{96,112},{112,96},{1... | collective-permute-start | bytes 392 | tf_op jit(solution)/shard_map/ppermute | solution.py:279
  10.7 4.6 %collective-permute-start.2 = (s32[1,1,32]{2,1,0:T(1,128)}, s32[1,1,32]{2,1,0:T(1,128)S(1)}, u32[]{:S(2)}, u32[]{:S(2)}) collective-permute-start(s32[1,1,32]{2,1,0:T(1,128)} %refs_1_.1), channel_id=1, source_target_pairs={{0,96},{16,112},{32,0},{48,16},{64,32},{80,48},{96,64},{112,80},{1... | collective-permute-start | bytes 392 | tf_op jit(solution)/shard_map/ppermute | solution.py:283
  14.5 4.0 %collective-permute-start.1 = (s32[1,1,32]{2,1,0:T(1,128)}, s32[1,1,32]{2,1,0:T(1,128)S(1)}, u32[]{:S(2)}, u32[]{:S(2)}) collective-permute-start(s32[1,1,32]{2,1,0:T(1,128)} %refs_1_.1), channel_id=1, source_target_pairs={{0,64},{16,80},{32,96},{48,112},{64,0},{80,16},{96,32},{112,48},{1... | collective-permute-start | bytes 392 | tf_op jit(solution)/shard_map/ppermute | solution.py:283
  14.5 5.5 %collective-permute-start = (s32[1,1,32]{2,1,0:T(1,128)}, s32[1,1,32]{2,1,0:T(1,128)S(1)}, u32[]{:S(2)}, u32[]{:S(2)}) collective-permute-start(s32[1,1,32]{2,1,0:T(1,128)} %refs_1_.1), channel_id=1, source_target_pairs={{0,32},{16,48},{32,64},{48,80},{64,96},{80,112},{96,0},{112,16},{1... | collective-permute-start | bytes 392 | tf_op jit(solution)/shard_map/ppermute | solution.py:283
  15.3 4.7 %collective-permute-start.6 = (s32[1,1,32]{2,1,0:T(1,128)S(1)}, s32[1,1,32]{2,1,0:T(1,128)S(1)}, u32[]{:S(2)}, u32[]{:S(2)}) collective-permute-start(s32[1,1,32]{2,1,0:T(1,128)S(1)} %collective-permute-done.2.refs_3_.refs_4_), channel_id=1, source_target_pairs={{0,16},{16,0},{32,48},{48,32},{64,80},{80,64},{96,112},{112,96},{1... | collective-permute-start | bytes 392 | tf_op jit(solution)/shard_map/ppermute | solution.py:279
  18.5 2.3 %collective-permute-start.5 = (s32[1,1,32]{2,1,0:T(1,128)S(1)}, s32[1,1,32]{2,1,0:T(1,128)S(1)}, u32[]{:S(2)}, u32[]{:S(2)}) collective-permute-start(s32[1,1,32]{2,1,0:T(1,128)S(1)} %collective-permute-done.1.refs_2_.refs_3_), channel_id=1, source_target_pairs={{0,16},{16,0},{32,48},{48,32},{64,80},{80,64},{96,112},{112,96},{1... | collective-permute-start | bytes 392 | tf_op jit(solution)/shard_map/ppermute | solution.py:279
  20.0 1.1 %collective-permute-start.4 = (s32[1,1,32]{2,1,0:T(1,128)S(1)}, s32[1,1,32]{2,1,0:T(1,128)S(1)}, u32[]{:S(2)}, u32[]{:S(2)}) collective-permute-start(s32[1,1,32]{2,1,0:T(1,128)S(1)} %collective-permute-done.refs_1_.refs_2_), channel_id=1, source_target_pairs={{0,16},{16,0},{32,48},{48,32},{64,80},{80,64},{96,112},{112,96},{1... | collective-permute-start | bytes 392 | tf_op jit(solution)/shard_map/ppermute | solution.py:279
  21.1 0.7 copy-start.3
  21.8 0.7 copy-start.5
  25.6 14.6 %collective-permute-start.7 = (bf16[8,128,128]{2,1,0:T(8,128)(2,1)S(1)}, bf16[8,128,128]{2,1,0:T(8,128)(2,1)S(1)}, u32[]{:S(2)}, u32[]{:S(2)}) collective-permute-start(bf16[8,128,128]{2,1,0:T(8,128)(2,1)S(1)} %get-tuple-element.15), channel_id=1, source_target_pairs={{0,32},{16,48},{32,64},{48,80},{64,96},{80,112},{96,0},{112,16},{1... | collective-permute-start | bytes 786440 | tf_op jit(solution)/shard_map/ppermute | solution.py:283
  25.7 15.5 %collective-permute-start.8 = (bf16[8,128,128]{2,1,0:T(8,128)(2,1)S(1)}, bf16[8,128,128]{2,1,0:T(8,128)(2,1)S(1)}, u32[]{:S(2)}, u32[]{:S(2)}) collective-permute-start(bf16[8,128,128]{2,1,0:T(8,128)(2,1)S(1)} %get-tuple-element.16), channel_id=1, source_target_pairs={{0,64},{16,80},{32,96},{48,112},{64,0},{80,16},{96,32},{112,48},{1... | collective-permute-start | bytes 786440 | tf_op jit(solution)/shard_map/ppermute | solution.py:283
  27.2 14.0 %collective-permute-start.9 = (bf16[8,128,128]{2,1,0:T(8,128)(2,1)S(1)}, bf16[8,128,128]{2,1,0:T(8,128)(2,1)S(1)}, u32[]{:S(2)}, u32[]{:S(2)}) collective-permute-start(bf16[8,128,128]{2,1,0:T(8,128)(2,1)S(1)} %get-tuple-element.17), channel_id=1, source_target_pairs={{0,96},{16,112},{32,0},{48,16},{64,32},{80,48},{96,64},{112,80},{1... | collective-permute-start | bytes 786440 | tf_op jit(solution)/shard_map/ppermute | solution.py:283
  29.2 23.7 %all-to-all-start.1 = ((bf16[16,2,128,128]{3,2,1,0:T(8,128)(2,1)}), bf16[16,2,128,128]{3,2,1,0:T(8,128)(2,1)}, u32[]{:S(2)}, u32[]{:S(2)}) async-start(bf16[16,2,128,128]{3,2,1,0:T(8,128)(2,1)} %bitcast.18), calls=%async_computation.1 | async-start | bytes 2097152 | tf_op jit(solution)/shard_map/all_to_all | solution.py:315
  36.2 5.7 %collective-permute-start.10 = (bf16[8,128,128]{2,1,0:T(8,128)(2,1)S(1)}, bf16[8,128,128]{2,1,0:T(8,128)(2,1)S(1)}, u32[]{:S(2)}, u32[]{:S(2)}) collective-permute-start(bf16[8,128,128]{2,1,0:T(8,128)(2,1)S(1)} %get-tuple-element.14.refs_0_), channel_id=1, source_target_pairs={{0,16},{16,0},{32,48},{48,32},{64,80},{80,64},{96,112},{112,96},{1... | collective-permute-start | bytes 786440 | tf_op jit(solution)/shard_map/ppermute | solution.py:279
  40.2 2.2 %collective-permute-start.11 = (bf16[8,128,128]{2,1,0:T(8,128)(2,1)S(1)}, bf16[8,128,128]{2,1,0:T(8,128)(2,1)S(1)}, u32[]{:S(2)}, u32[]{:S(2)}) collective-permute-start(bf16[8,128,128]{2,1,0:T(8,128)(2,1)S(1)} %collective-permute-done.7.refs_1_), channel_id=1, source_target_pairs={{0,16},{16,0},{32,48},{48,32},{64,80},{80,64},{96,112},{112,96},{1... | collective-permute-start | bytes 786440 | tf_op jit(solution)/shard_map/ppermute | solution.py:279
  41.2 1.5 %collective-permute-start.12 = (bf16[8,128,128]{2,1,0:T(8,128)(2,1)S(1)}, bf16[8,128,128]{2,1,0:T(8,128)(2,1)S(1)}, u32[]{:S(2)}, u32[]{:S(2)}) collective-permute-start(bf16[8,128,128]{2,1,0:T(8,128)(2,1)S(1)} %collective-permute-done.8.refs_2_), channel_id=1, source_target_pairs={{0,16},{16,0},{32,48},{48,32},{64,80},{80,64},{96,112},{112,96},{1... | collective-permute-start | bytes 786440 | tf_op jit(solution)/shard_map/ppermute | solution.py:279
  41.2 1.9 %collective-permute-start.13 = (bf16[8,128,128]{2,1,0:T(8,128)(2,1)S(1)}, bf16[8,128,128]{2,1,0:T(8,128)(2,1)S(1)}, u32[]{:S(2)}, u32[]{:S(2)}) collective-permute-start(bf16[8,128,128]{2,1,0:T(8,128)(2,1)S(1)} %collective-permute-done.9.refs_3_), channel_id=1, source_target_pairs={{0,16},{16,0},{32,48},{48,32},{64,80},{80,64},{96,112},{112,96},{1... | collective-permute-start | bytes 786440 | tf_op jit(solution)/shard_map/ppermute | solution.py:279
  43.1 0.7 copy-start.11
  43.8 9.0 %copy-start.1 = (s32[32,8]{0,1:T(8,128)S(1)}, s32[32,8]{0,1:T(8,128)}, u32[]{:S(2)}) copy-start(s32[32,8]{0,1:T(8,128)} %param.22) | copy-start | bytes 3076
  43.9 9.0 %copy-start.2 = (f32[32,8]{0,1:T(8,128)S(1)}, f32[32,8]{0,1:T(8,128)}, u32[]{:S(2)}) copy-start(f32[32,8]{0,1:T(8,128)} %param.21) | copy-start | bytes 3076
  43.9 9.0 %copy-start.6 = (s32[1,1,32]{2,1,0:T(1,128)S(1)}, s32[1,1,32]{2,1,0:T(1,128)}, u32[]{:S(2)}) copy-start(s32[1,1,32]{2,1,0:T(1,128)} %refs_1_.1) | copy-start | bytes 388
  62.9 12.0 %collective-permute-start.14 = (bf16[8,128,128]{2,1,0:T(8,128)(2,1)S(1)}, bf16[8,128,128]{2,1,0:T(8,128)(2,1)S(1)}, u32[]{:S(2)}, u32[]{:S(2)}) collective-permute-start(bf16[8,128,128]{2,1,0:T(8,128)(2,1)S(1)} %get-tuple-element.21), channel_id=1, source_target_pairs={{0,32},{16,48},{32,64},{48,80},{64,96},{80,112},{96,0},{112,16},{1... | collective-permute-start | bytes 786440 | tf_op jit(solution)/shard_map/ppermute | solution.py:283
  63.6 14.4 %collective-permute-start.15 = (bf16[8,128,128]{2,1,0:T(8,128)(2,1)S(1)}, bf16[8,128,128]{2,1,0:T(8,128)(2,1)S(1)}, u32[]{:S(2)}, u32[]{:S(2)}) collective-permute-start(bf16[8,128,128]{2,1,0:T(8,128)(2,1)S(1)} %get-tuple-element.22), channel_id=1, source_target_pairs={{0,64},{16,80},{32,96},{48,112},{64,0},{80,16},{96,32},{112,48},{1... | collective-permute-start | bytes 786440 | tf_op jit(solution)/shard_map/ppermute | solution.py:283
  66.3 12.9 %collective-permute-start.16 = (bf16[8,128,128]{2,1,0:T(8,128)(2,1)S(1)}, bf16[8,128,128]{2,1,0:T(8,128)(2,1)S(1)}, u32[]{:S(2)}, u32[]{:S(2)}) collective-permute-start(bf16[8,128,128]{2,1,0:T(8,128)(2,1)S(1)} %get-tuple-element.23), channel_id=1, source_target_pairs={{0,96},{16,112},{32,0},{48,16},{64,32},{80,48},{96,64},{112,80},{1... | collective-permute-start | bytes 786440 | tf_op jit(solution)/shard_map/ppermute | solution.py:283
  66.4 24.1 %all-to-all-start.2 = ((bf16[16,2,128,128]{3,2,1,0:T(8,128)(2,1)}), bf16[16,2,128,128]{3,2,1,0:T(8,128)(2,1)S(1)}, u32[]{:S(2)}, u32[]{:S(2)}) async-start(bf16[16,2,128,128]{3,2,1,0:T(8,128)(2,1)} %bitcast.17), calls=%async_computation.2 | async-start | bytes 2097152 | tf_op jit(solution)/shard_map/all_to_all | solution.py:315
  73.3 5.9 %collective-permute-start.17 = (bf16[8,128,128]{2,1,0:T(8,128)(2,1)S(1)}, bf16[8,128,128]{2,1,0:T(8,128)(2,1)S(1)}, u32[]{:S(2)}, u32[]{:S(2)}) collective-permute-start(bf16[8,128,128]{2,1,0:T(8,128)(2,1)S(1)} %get-tuple-element.20.refs_0_), channel_id=1, source_target_pairs={{0,16},{16,0},{32,48},{48,32},{64,80},{80,64},{96,112},{112,96},{1... | collective-permute-start | bytes 786440 | tf_op jit(solution)/shard_map/ppermute | solution.py:279
  74.9 4.4 %collective-permute-start.18 = (bf16[8,128,128]{2,1,0:T(8,128)(2,1)S(1)}, bf16[8,128,128]{2,1,0:T(8,128)(2,1)S(1)}, u32[]{:S(2)}, u32[]{:S(2)}) collective-permute-start(bf16[8,128,128]{2,1,0:T(8,128)(2,1)S(1)} %collective-permute-done.14.refs_1_), channel_id=1, source_target_pairs={{0,16},{16,0},{32,48},{48,32},{64,80},{80,64},{96,112},{112,96},{1... | collective-permute-start | bytes 786440 | tf_op jit(solution)/shard_map/ppermute | solution.py:279
  78.0 2.4 %collective-permute-start.19 = (bf16[8,128,128]{2,1,0:T(8,128)(2,1)S(1)}, bf16[8,128,128]{2,1,0:T(8,128)(2,1)S(1)}, u32[]{:S(2)}, u32[]{:S(2)}) collective-permute-start(bf16[8,128,128]{2,1,0:T(8,128)(2,1)S(1)} %collective-permute-done.15.refs_2_), channel_id=1, source_target_pairs={{0,16},{16,0},{32,48},{48,32},{64,80},{80,64},{96,112},{112,96},{1... | collective-permute-start | bytes 786440 | tf_op jit(solution)/shard_map/ppermute | solution.py:279
  79.2 1.5 %collective-permute-start.20 = (bf16[8,128,128]{2,1,0:T(8,128)(2,1)S(1)}, bf16[8,128,128]{2,1,0:T(8,128)(2,1)S(1)}, u32[]{:S(2)}, u32[]{:S(2)}) collective-permute-start(bf16[8,128,128]{2,1,0:T(8,128)(2,1)S(1)} %collective-permute-done.16.refs_3_), channel_id=1, source_target_pairs={{0,16},{16,0},{32,48},{48,32},{64,80},{80,64},{96,112},{112,96},{1... | collective-permute-start | bytes 786440 | tf_op jit(solution)/shard_map/ppermute | solution.py:279
  80.8 0.7 copy-start.10

commit v4 on v3

--- a/solution.py
+++ b/solution.py
@@ -12,7 +12,7 @@
 W = 128
 PAIRS = 32
 NK = 8
-CUTS = (0, 4, 12, 20, 28, 32)
+CUTS = (0, 2, 10, 18, 26, 32)
 CHUNKS = len(CUTS) - 1
 AHEAD = 2
 NZ = 4

time: 100 us -> 101 us (1.010)
  no operation moved by 1% of the time
where the time goes in v4:
time: 101 us; the launch traced here: 100 us
  starting transfers between devices  42.6 us (42%)
  Pallas kernels  41.8 us (41%)
  waiting for transfers between devices  11.9 us (12%)
  local copies, waits for them, and re-layouts  2.76 us (3%)
  between operations  1.01 us (1%)
    pallas_call x2, Pallas kernels, col_part(): pl.pallas_call(functools.partial(col_body, first), in_specs=[SMEM] * 4 +...  19.3 us
    pallas_call x2, Pallas kernels, row_part(): pl.pallas_call(functools.partial(row_body, first), in_specs=[SMEM] * 4 +...  18.1 us
    all_to_all x2, starting transfers between devices, shards(): lax.all_to_all(out[0].reshape(16, 2, W, W), 'col', 0, 0, tiled=True)  13.9 us
    ppermute x9, starting transfers between devices, shift_z(): return lax.ppermute(x, 'row', [(i, (i + 2 * dz) % 8) for i in range(8)])  11.5 us
    ppermute x12, starting transfers between devices, swap_core(): return lax.ppermute(x, 'row', [(i, i ^ 1) for i in range(8)])  9.46 us
    ppermute x9, waiting for transfers between devices, shift_z(): return lax.ppermute(x, 'row', [(i, (i + 2 * dz) % 8) for i in range(8)])  7.99 us
    all_to_all x1, starting transfers between devices, shards(): col_asked = lax.all_to_all(spread_wants(col_wants), 'col', 0, 0, tiled=True)  7.73 us
    ppermute x12, waiting for transfers between devices, swap_core(): return lax.ppermute(x, 'row', [(i, i ^ 1) for i in range(8)])  3.92 us
  transfers between devices with their start and end apart: 24, of which 11 were waited for; matrix products, arithmetic and copies ran while one was open for 0% of the time, Pallas kernels for 18%

profile of v4, /device:TPU:1, one launch (start us, length us, event | category | flops | bytes accessed | tf_op | source)
XLA Modules:
  0.0 100.1 jit_solution(9392167888814352532)
XLA Ops:
  0.6 1.3 %spread_wants.1 = s32[16,1,128]{2,1,0:T(1,128)} custom-call(s32[1,1,32]{2,1,0:T(1,128)} %wants.1), custom_call_target="tpu_custom_call" | custom-call | tf_op jit(solution)/shard_map/spread_wants/pallas_call | solution.py:37
  1.9 7.7 %all-to-all-start = ((s32[16,1,128]{2,1,0:T(1,128)}), s32[16,1,128]{2,1,0:T(1,128)S(1)}, u32[]{:S(2)}, u32[]{:S(2)}) async-start(s32[16,1,128]{2,1,0:T(1,128)} %spread_wants.1), calls=%async_computation | async-start | bytes 16384 | tf_op jit(solution)/shard_map/all_to_all | solution.py:308
  9.6 0.0 copy-start
  9.7 1.0 %collective-permute-start.3 = (s32[1,1,32]{2,1,0:T(1,128)}, s32[1,1,32]{2,1,0:T(1,128)S(1)}, u32[]{:S(2)}, u32[]{:S(2)}) collective-permute-start(s32[1,1,32]{2,1,0:T(1,128)} %refs_1_.1), channel_id=1, source_target_pairs={{0,16},{16,0},{32,48},{48,32},{64,80},{80,64},{96,112},{112,96},{1... | collective-permute-start | bytes 392 | tf_op jit(solution)/shard_map/ppermute | solution.py:279
  10.7 3.8 %collective-permute-start.2 = (s32[1,1,32]{2,1,0:T(1,128)}, s32[1,1,32]{2,1,0:T(1,128)S(1)}, u32[]{:S(2)}, u32[]{:S(2)}) collective-permute-start(s32[1,1,32]{2,1,0:T(1,128)} %refs_1_.1), channel_id=1, source_target_pairs={{0,96},{16,112},{32,0},{48,16},{64,32},{80,48},{96,64},{112,80},{1... | collective-permute-start | bytes 392 | tf_op jit(solution)/shard_map/ppermute | solution.py:283
  14.5 0.0 collective-permute-start.1
  14.5 0.7 collective-permute-start
  15.2 0.2 collective-permute-done.2.refs_3_.refs_4_
  15.3 0.9 collective-permute-start.6
  16.2 2.2 %collective-permute-done.1.refs_2_.refs_3_ = s32[1,1,32]{2,1,0:T(1,128)S(1)} collective-permute-done((s32[1,1,32]{2,1,0:T(1,128)}, s32[1,1,32]{2,1,0:T(1,128)S(1)}, u32[]{:S(2)}, u32[]{:S(2)}) %collective-permute-start.1) | collective-permute-done | bytes 160 | tf_op jit(solution)/shard_map/ppermute | solution.py:283
  18.5 1.5 %collective-permute-start.5 = (s32[1,1,32]{2,1,0:T(1,128)S(1)}, s32[1,1,32]{2,1,0:T(1,128)S(1)}, u32[]{:S(2)}, u32[]{:S(2)}) collective-permute-start(s32[1,1,32]{2,1,0:T(1,128)S(1)} %collective-permute-done.1.refs_2_.refs_3_), channel_id=1, source_target_pairs={{0,16},{16,0},{32,48},{48,32},{64,80},{80,64},{96,112},{112,96},{1... | collective-permute-start | bytes 392 | tf_op jit(solution)/shard_map/ppermute | solution.py:279
  20.0 0.0 collective-permute-done.refs_1_.refs_2_
  20.0 0.0 collective-permute-start.4
  20.0 0.0 collective-permute-done.3.refs_4_.refs_5_
  20.0 0.0 collective-permute-done.6.refs_7_.refs_8_
  20.0 0.8 collective-permute-done.5.refs_6_.refs_7_
  20.8 0.3 collective-permute-done.4.refs_5_.refs_6_
  21.1 0.0 all-to-all-done.col_asked.refs_0_
  21.1 0.7 copy-done.3
  21.8 0.7 copy-done.5
  22.4 3.1 %first_outgoing.1 = (bf16[32,128,128]{2,1,0:T(8,128)(2,1)}, bf16[8,128,128]{2,1,0:T(8,128)(2,1)S(1)}, bf16[8,128,128]{2,1,0:T(8,128)(2,1)S(1)}, bf16[8,128,128]{2,1,0:T(8,128)(2,1)S(1)}, bf16[8,128,128]{2,1,0:T(8,128)(2,1)S(1)}) custom-call(s32[32]{0:T(128)S(1)} %copy-done.3, s32[16,1,128]{2,1,0:T(1,128)S(1)} %all-to-all-done.col_asked.refs_0_, ...), custom_call_target="tpu_custom_call" | custom-call | tf_op jit(solution)/shard_map/first_outgoing/pallas_call | solution.py:78
  25.6 0.1 collective-permute-start.7
  25.7 1.5 %collective-permute-start.8 = (bf16[8,128,128]{2,1,0:T(8,128)(2,1)S(1)}, bf16[8,128,128]{2,1,0:T(8,128)(2,1)S(1)}, u32[]{:S(2)}, u32[]{:S(2)}) collective-permute-start(bf16[8,128,128]{2,1,0:T(8,128)(2,1)S(1)} %get-tuple-element.16), channel_id=1, source_target_pairs={{0,64},{16,80},{32,96},{48,112},{64,0},{80,16},{96,32},{112,48},{1... | collective-permute-start | bytes 786440 | tf_op jit(solution)/shard_map/ppermute | solution.py:283
  27.2 2.0 %collective-permute-start.9 = (bf16[8,128,128]{2,1,0:T(8,128)(2,1)S(1)}, bf16[8,128,128]{2,1,0:T(8,128)(2,1)S(1)}, u32[]{:S(2)}, u32[]{:S(2)}) collective-permute-start(bf16[8,128,128]{2,1,0:T(8,128)(2,1)S(1)} %get-tuple-element.17), channel_id=1, source_target_pairs={{0,96},{16,112},{32,0},{48,16},{64,32},{80,48},{96,64},{112,80},{1... | collective-permute-start | bytes 786440 | tf_op jit(solution)/shard_map/ppermute | solution.py:283
  29.2 7.0 %all-to-all-start.1 = ((bf16[16,2,128,128]{3,2,1,0:T(8,128)(2,1)}), bf16[16,2,128,128]{3,2,1,0:T(8,128)(2,1)}, u32[]{:S(2)}, u32[]{:S(2)}) async-start(bf16[16,2,128,128]{3,2,1,0:T(8,128)(2,1)} %bitcast.18), calls=%async_computation.1 | async-start | bytes 2097152 | tf_op jit(solution)/shard_map/all_to_all | solution.py:315
  36.2 1.5 %collective-permute-start.10 = (bf16[8,128,128]{2,1,0:T(8,128)(2,1)S(1)}, bf16[8,128,128]{2,1,0:T(8,128)(2,1)S(1)}, u32[]{:S(2)}, u32[]{:S(2)}) collective-permute-start(bf16[8,128,128]{2,1,0:T(8,128)(2,1)S(1)} %get-tuple-element.14.refs_0_), channel_id=1, source_target_pairs={{0,16},{16,0},{32,48},{48,32},{64,80},{80,64},{96,112},{112,96},{1... | collective-permute-start | bytes 786440 | tf_op jit(solution)/shard_map/ppermute | solution.py:279
  37.7 2.5 %collective-permute-done.7.refs_1_ = bf16[8,128,128]{2,1,0:T(8,128)(2,1)S(1)} collective-permute-done((bf16[8,128,128]{2,1,0:T(8,128)(2,1)S(1)}, bf16[8,128,128]{2,1,0:T(8,128)(2,1)S(1)}, u32[]{:S(2)}, u32[]{:S(2)}) %collective-permute-start.7) | collective-permute-done | bytes 262176 | tf_op jit(solution)/shard_map/ppermute | solution.py:283
  40.2 1.0 %collective-permute-start.11 = (bf16[8,128,128]{2,1,0:T(8,128)(2,1)S(1)}, bf16[8,128,128]{2,1,0:T(8,128)(2,1)S(1)}, u32[]{:S(2)}, u32[]{:S(2)}) collective-permute-start(bf16[8,128,128]{2,1,0:T(8,128)(2,1)S(1)} %collective-permute-done.7.refs_1_), channel_id=1, source_target_pairs={{0,16},{16,0},{32,48},{48,32},{64,80},{80,64},{96,112},{112,96},{1... | collective-permute-start | bytes 786440 | tf_op jit(solution)/shard_map/ppermute | solution.py:279
  41.2 0.0 collective-permute-done.8.refs_2_
  41.2 0.0 collective-permute-start.12
  41.2 0.0 collective-permute-done.9.refs_3_
  41.2 0.6 collective-permute-start.13
  41.8 0.0 collective-permute-done.10.refs_4_
  41.8 0.5 collective-permute-done.11.refs_5_
  42.4 0.4 collective-permute-done.12.refs_6_
  42.7 0.4 collective-permute-done.13.refs_7_
  43.1 0.7 copy-done.11
  43.8 0.0 copy-done.4
  43.8 0.0 copy-done
  43.8 0.0 copy-start.1
  43.9 0.0 copy-start.2
  43.9 0.0 copy-start.6
  43.9 9.1 %row_part.2.refs_12_ = f32[32,128,128]{2,1,0:T(8,128)} custom-call(s32[8,32]{1,0:T(8,128)S(1)} %bitcast.13, f32[8,32]{1,0:T(8,128)S(1)} %bitcast.15, s32[32]{0:T(128)S(1)} %copy-done.4, f32[32]{0:T(128)S(1)} %copy-done.7, f32[32,128]{1,0:T(8,128)S(1)} %copy-done, bf16[8,128,128]{2,1,0:T(8,128)(2,1)S(1)} %get-tuple-element.14.refs_0_, ...), custom_call_target="tpu_custom_call" | custom-call | flops 6442450944 | bytes 16777216 | tf_op jit(solution)/shard_map/row_part/pallas_call | solution.py:184
  53.0 0.0 all-to-all-done.1
  53.0 10.0 %col_part.2 = (f32[32,128,128]{2,1,0:T(8,128)}, bf16[32,128,128]{2,1,0:T(8,128)(2,1)}, bf16[8,128,128]{2,1,0:T(8,128)(2,1)S(1)}, bf16[8,128,128]{2,1,0:T(8,128)(...) custom-call(s32[8,32]{1,0:T(8,128)S(1)} %bitcast.9, f32[8,32]{1,0:T(8,128)S(1)} %bitcast.11, ...), custom_call_target="tpu_custom_call" | custom-call | flops 2147483648 | bytes 16777216 | tf_op jit(solution)/shard_map/col_part/pallas_call | solution.py:259
  63.0 0.7 collective-permute-start.14
  63.8 2.7 %collective-permute-start.15 = (bf16[8,128,128]{2,1,0:T(8,128)(2,1)S(1)}, bf16[8,128,128]{2,1,0:T(8,128)(2,1)S(1)}, u32[]{:S(2)}, u32[]{:S(2)}) collective-permute-start(bf16[8,128,128]{2,1,0:T(8,128)(2,1)S(1)} %get-tuple-element.22), channel_id=1, source_target_pairs={{0,64},{16,80},{32,96},{48,112},{64,0},{80,16},{96,32},{112,48},{1... | collective-permute-start | bytes 786440 | tf_op jit(solution)/shard_map/ppermute | solution.py:283
  66.5 0.0 collective-permute-start.16
  66.5 6.9 %all-to-all-start.2 = ((bf16[16,2,128,128]{3,2,1,0:T(8,128)(2,1)}), bf16[16,2,128,128]{3,2,1,0:T(8,128)(2,1)S(1)}, u32[]{:S(2)}, u32[]{:S(2)}) async-start(bf16[16,2,128,128]{3,2,1,0:T(8,128)(2,1)} %bitcast.17), calls=%async_computation.2 | async-start | bytes 2097152 | tf_op jit(solution)/shard_map/all_to_all | solution.py:315
  73.5 1.5 %collective-permute-start.17 = (bf16[8,128,128]{2,1,0:T(8,128)(2,1)S(1)}, bf16[8,128,128]{2,1,0:T(8,128)(2,1)S(1)}, u32[]{:S(2)}, u32[]{:S(2)}) collective-permute-start(bf16[8,128,128]{2,1,0:T(8,128)(2,1)S(1)} %get-tuple-element.20.refs_0_), channel_id=1, source_target_pairs={{0,16},{16,0},{32,48},{48,32},{64,80},{80,64},{96,112},{112,96},{1... | collective-permute-start | bytes 786440 | tf_op jit(solution)/shard_map/ppermute | solution.py:279
  75.0 0.0 collective-permute-done.14.refs_1_
  75.0 0.1 collective-permute-start.18
  75.1 3.0 %collective-permute-done.15.refs_2_ = bf16[8,128,128]{2,1,0:T(8,128)(2,1)S(1)} collective-permute-done((bf16[8,128,128]{2,1,0:T(8,128)(2,1)S(1)}, bf16[8,128,128]{2,1,0:T(8,128)(2,1)S(1)}, u32[]{:S(2)}, u32[]{:S(2)}) %collective-permute-start.15) | collective-permute-done | bytes 262176 | tf_op jit(solution)/shard_map/ppermute | solution.py:283
  78.2 1.2 %collective-permute-start.19 = (bf16[8,128,128]{2,1,0:T(8,128)(2,1)S(1)}, bf16[8,128,128]{2,1,0:T(8,128)(2,1)S(1)}, u32[]{:S(2)}, u32[]{:S(2)}) collective-permute-start(bf16[8,128,128]{2,1,0:T(8,128)(2,1)S(1)} %collective-permute-done.15.refs_2_), channel_id=1, source_target_pairs={{0,16},{16,0},{32,48},{48,32},{64,80},{80,64},{96,112},{112,96},{1... | collective-permute-start | bytes 786440 | tf_op jit(solution)/shard_map/ppermute | solution.py:279
  79.4 0.0 collective-permute-done.16.refs_3_
  79.4 0.0 collective-permute-start.20
  79.4 0.0 collective-permute-done.17.refs_4_
  79.4 0.0 collective-permute-done.18.refs_5_
  79.4 1.1 %collective-permute-done.19.refs_6_ = bf16[8,128,128]{2,1,0:T(8,128)(2,1)S(1)} collective-permute-done((bf16[8,128,128]{2,1,0:T(8,128)(2,1)S(1)}, bf16[8,128,128]{2,1,0:T(8,128)(2,1)S(1)}, u32[]{:S(2)}, u32[]{:S(2)}) %collective-permute-start.19) | collective-permute-done | bytes 262176 | tf_op jit(solution)/shard_map/ppermute | solution.py:279
  80.5 0.4 collective-permute-done.20.refs_7_
  80.9 0.7 copy-done.10
  81.6 9.1 %row_part.3.refs_3_ = f32[32,128,128]{2,1,0:T(8,128)} custom-call(s32[8,32]{1,0:T(8,128)S(1)} %bitcast.14, f32[8,32]{1,0:T(8,128)S(1)} %bitcast.16, s32[32]{0:T(128)S(1)} %copy-done.4, f32[32]{0:T(128)S(1)} %copy-done.7, f32[32,128]{1,0:T(8,128)S(1)} %copy-done, bf16[8,128,128]{2,1,0:T(8,128)(2,1)S(1)} %get-tuple-element.20.refs_0_, ...), custom_call_target="tpu_custom_call" | custom-call | flops 6442450944 | bytes 16777216 | tf_op jit(solution)/shard_map/row_part/pallas_call | solution.py:184
  90.7 0.0 all-to-all-done.2
  90.7 9.2 %col_part.3 = (f32[32,128,128]{2,1,0:T(8,128)}, f32[32,128,128]{2,1,0:T(8,128)}) custom-call(s32[8,32]{1,0:T(8,128)S(1)} %bitcast.10, f32[8,32]{1,0:T(8,128)S(1)} %bitcast.12, s32[32]{0:T(128)S(1)} %copy-done.4, f32[32]{0:T(128)S(1)} %copy-done.7, f32[32,128]{1,0:T(8,128)S(1)} %copy-done, bf16[32,8,128,128]{3,2,1,0:T(8,128)(2,1)} %refs_0_.3, ...), custom_call_target="tpu_custom_call" | custom-call | flops 2147483648 | bytes 16777216 | tf_op jit(solution)/shard_map/col_part/pallas_call | solution.py:259
  (14 shorter events, 0.0 us)
Async XLA Ops:
  1.9 41.9 %copy-start.4 = (s32[32]{0:T(128)S(1)}, s32[32]{0:T(128)}, u32[]{:S(2)}) copy-start(s32[32]{0:T(128)} %sizes.9) | copy-start | bytes 388
  1.9 41.9 %copy-start.7 = (f32[32]{0:T(128)S(1)}, f32[32]{0:T(128)}, u32[]{:S(2)}) copy-start(f32[32]{0:T(128)} %shift.7) | copy-start | bytes 388
  1.9 41.9 %copy-start.8 = (s32[32,8]{0,1:T(8,128)S(1)}, s32[32,8]{0,1:T(8,128)}, u32[]{:S(2)}) copy-start(s32[32,8]{0,1:T(8,128)} %param.23) | copy-start | bytes 3076
  1.9 41.9 %copy-start.9 = (f32[32,8]{0,1:T(8,128)S(1)}, f32[32,8]{0,1:T(8,128)}, u32[]{:S(2)}) copy-start(f32[32,8]{0,1:T(8,128)} %param.20) | copy-start | bytes 3076
  1.9 19.2 %all-to-all-start = ((s32[16,1,128]{2,1,0:T(1,128)}), s32[16,1,128]{2,1,0:T(1,128)S(1)}, u32[]{:S(2)}, u32[]{:S(2)}) async-start(s32[16,1,128]{2,1,0:T(1,128)} %spread_wants.1), calls=%async_computation | async-start | bytes 16384 | tf_op jit(solution)/shard_map/all_to_all | solution.py:308
  9.6 34.2 %copy-start = (f32[32,128]{1,0:T(8,128)S(1)}, f32[32,128]{1,0:T(8,128)}, u32[]{:S(2)}) copy-start(f32[32,128]{1,0:T(8,128)} %eps.7) | copy-start | bytes 49156
  9.7 10.3 %collective-permute-start.3 = (s32[1,1,32]{2,1,0:T(1,128)}, s32[1,1,32]{2,1,0:T(1,128)S(1)}, u32[]{:S(2)}, u32[]{:S(2)}) collective-permute-start(s32[1,1,32]{2,1,0:T(1,128)} %refs_1_.1), channel_id=1, source_target_pairs={{0,16},{16,0},{32,48},{48,32},{64,80},{80,64},{96,112},{112,96},{1... | collective-permute-start | bytes 392 | tf_op jit(solution)/shard_map/ppermute | solution.py:279
  10.7 4.6 %collective-permute-start.2 = (s32[1,1,32]{2,1,0:T(1,128)}, s32[1,1,32]{2,1,0:T(1,128)S(1)}, u32[]{:S(2)}, u32[]{:S(2)}) collective-permute-start(s32[1,1,32]{2,1,0:T(1,128)} %refs_1_.1), channel_id=1, source_target_pairs={{0,96},{16,112},{32,0},{48,16},{64,32},{80,48},{96,64},{112,80},{1... | collective-permute-start | bytes 392 | tf_op jit(solution)/shard_map/ppermute | solution.py:283
  14.5 4.0 %collective-permute-start.1 = (s32[1,1,32]{2,1,0:T(1,128)}, s32[1,1,32]{2,1,0:T(1,128)S(1)}, u32[]{:S(2)}, u32[]{:S(2)}) collective-permute-start(s32[1,1,32]{2,1,0:T(1,128)} %refs_1_.1), channel_id=1, source_target_pairs={{0,64},{16,80},{32,96},{48,112},{64,0},{80,16},{96,32},{112,48},{1... | collective-permute-start | bytes 392 | tf_op jit(solution)/shard_map/ppermute | solution.py:283
  14.5 5.5 %collective-permute-start = (s32[1,1,32]{2,1,0:T(1,128)}, s32[1,1,32]{2,1,0:T(1,128)S(1)}, u32[]{:S(2)}, u32[]{:S(2)}) collective-permute-start(s32[1,1,32]{2,1,0:T(1,128)} %refs_1_.1), channel_id=1, source_target_pairs={{0,32},{16,48},{32,64},{48,80},{64,96},{80,112},{96,0},{112,16},{1... | collective-permute-start | bytes 392 | tf_op jit(solution)/shard_map/ppermute | solution.py:283
  15.3 4.7 %collective-permute-start.6 = (s32[1,1,32]{2,1,0:T(1,128)S(1)}, s32[1,1,32]{2,1,0:T(1,128)S(1)}, u32[]{:S(2)}, u32[]{:S(2)}) collective-permute-start(s32[1,1,32]{2,1,0:T(1,128)S(1)} %collective-permute-done.2.refs_3_.refs_4_), channel_id=1, source_target_pairs={{0,16},{16,0},{32,48},{48,32},{64,80},{80,64},{96,112},{112,96},{1... | collective-permute-start | bytes 392 | tf_op jit(solution)/shard_map/ppermute | solution.py:279
  18.5 2.3 %collective-permute-start.5 = (s32[1,1,32]{2,1,0:T(1,128)S(1)}, s32[1,1,32]{2,1,0:T(1,128)S(1)}, u32[]{:S(2)}, u32[]{:S(2)}) collective-permute-start(s32[1,1,32]{2,1,0:T(1,128)S(1)} %collective-permute-done.1.refs_2_.refs_3_), channel_id=1, source_target_pairs={{0,16},{16,0},{32,48},{48,32},{64,80},{80,64},{96,112},{112,96},{1... | collective-permute-start | bytes 392 | tf_op jit(solution)/shard_map/ppermute | solution.py:279
  20.0 1.1 %collective-permute-start.4 = (s32[1,1,32]{2,1,0:T(1,128)S(1)}, s32[1,1,32]{2,1,0:T(1,128)S(1)}, u32[]{:S(2)}, u32[]{:S(2)}) collective-permute-start(s32[1,1,32]{2,1,0:T(1,128)S(1)} %collective-permute-done.refs_1_.refs_2_), channel_id=1, source_target_pairs={{0,16},{16,0},{32,48},{48,32},{64,80},{80,64},{96,112},{112,96},{1... | collective-permute-start | bytes 392 | tf_op jit(solution)/shard_map/ppermute | solution.py:279
  21.1 0.7 copy-start.3
  21.8 0.7 copy-start.5
  25.6 14.6 %collective-permute-start.7 = (bf16[8,128,128]{2,1,0:T(8,128)(2,1)S(1)}, bf16[8,128,128]{2,1,0:T(8,128)(2,1)S(1)}, u32[]{:S(2)}, u32[]{:S(2)}) collective-permute-start(bf16[8,128,128]{2,1,0:T(8,128)(2,1)S(1)} %get-tuple-element.15), channel_id=1, source_target_pairs={{0,32},{16,48},{32,64},{48,80},{64,96},{80,112},{96,0},{112,16},{1... | collective-permute-start | bytes 786440 | tf_op jit(solution)/shard_map/ppermute | solution.py:283
  25.7 15.5 %collective-permute-start.8 = (bf16[8,128,128]{2,1,0:T(8,128)(2,1)S(1)}, bf16[8,128,128]{2,1,0:T(8,128)(2,1)S(1)}, u32[]{:S(2)}, u32[]{:S(2)}) collective-permute-start(bf16[8,128,128]{2,1,0:T(8,128)(2,1)S(1)} %get-tuple-element.16), channel_id=1, source_target_pairs={{0,64},{16,80},{32,96},{48,112},{64,0},{80,16},{96,32},{112,48},{1... | collective-permute-start | bytes 786440 | tf_op jit(solution)/shard_map/ppermute | solution.py:283
  27.2 14.0 %collective-permute-start.9 = (bf16[8,128,128]{2,1,0:T(8,128)(2,1)S(1)}, bf16[8,128,128]{2,1,0:T(8,128)(2,1)S(1)}, u32[]{:S(2)}, u32[]{:S(2)}) collective-permute-start(bf16[8,128,128]{2,1,0:T(8,128)(2,1)S(1)} %get-tuple-element.17), channel_id=1, source_target_pairs={{0,96},{16,112},{32,0},{48,16},{64,32},{80,48},{96,64},{112,80},{1... | collective-permute-start | bytes 786440 | tf_op jit(solution)/shard_map/ppermute | solution.py:283
  29.2 23.8 %all-to-all-start.1 = ((bf16[16,2,128,128]{3,2,1,0:T(8,128)(2,1)}), bf16[16,2,128,128]{3,2,1,0:T(8,128)(2,1)}, u32[]{:S(2)}, u32[]{:S(2)}) async-start(bf16[16,2,128,128]{3,2,1,0:T(8,128)(2,1)} %bitcast.18), calls=%async_computation.1 | async-start | bytes 2097152 | tf_op jit(solution)/shard_map/all_to_all | solution.py:315
  36.2 5.7 %collective-permute-start.10 = (bf16[8,128,128]{2,1,0:T(8,128)(2,1)S(1)}, bf16[8,128,128]{2,1,0:T(8,128)(2,1)S(1)}, u32[]{:S(2)}, u32[]{:S(2)}) collective-permute-start(bf16[8,128,128]{2,1,0:T(8,128)(2,1)S(1)} %get-tuple-element.14.refs_0_), channel_id=1, source_target_pairs={{0,16},{16,0},{32,48},{48,32},{64,80},{80,64},{96,112},{112,96},{1... | collective-permute-start | bytes 786440 | tf_op jit(solution)/shard_map/ppermute | solution.py:279
  40.2 2.2 %collective-permute-start.11 = (bf16[8,128,128]{2,1,0:T(8,128)(2,1)S(1)}, bf16[8,128,128]{2,1,0:T(8,128)(2,1)S(1)}, u32[]{:S(2)}, u32[]{:S(2)}) collective-permute-start(bf16[8,128,128]{2,1,0:T(8,128)(2,1)S(1)} %collective-permute-done.7.refs_1_), channel_id=1, source_target_pairs={{0,16},{16,0},{32,48},{48,32},{64,80},{80,64},{96,112},{112,96},{1... | collective-permute-start | bytes 786440 | tf_op jit(solution)/shard_map/ppermute | solution.py:279
  41.2 1.5 %collective-permute-start.12 = (bf16[8,128,128]{2,1,0:T(8,128)(2,1)S(1)}, bf16[8,128,128]{2,1,0:T(8,128)(2,1)S(1)}, u32[]{:S(2)}, u32[]{:S(2)}) collective-permute-start(bf16[8,128,128]{2,1,0:T(8,128)(2,1)S(1)} %collective-permute-done.8.refs_2_), channel_id=1, source_target_pairs={{0,16},{16,0},{32,48},{48,32},{64,80},{80,64},{96,112},{112,96},{1... | collective-permute-start | bytes 786440 | tf_op jit(solution)/shard_map/ppermute | solution.py:279
  41.2 1.9 %collective-permute-start.13 = (bf16[8,128,128]{2,1,0:T(8,128)(2,1)S(1)}, bf16[8,128,128]{2,1,0:T(8,128)(2,1)S(1)}, u32[]{:S(2)}, u32[]{:S(2)}) collective-permute-start(bf16[8,128,128]{2,1,0:T(8,128)(2,1)S(1)} %collective-permute-done.9.refs_3_), channel_id=1, source_target_pairs={{0,16},{16,0},{32,48},{48,32},{64,80},{80,64},{96,112},{112,96},{1... | collective-permute-start | bytes 786440 | tf_op jit(solution)/shard_map/ppermute | solution.py:279
  43.1 0.7 copy-start.11
  43.8 9.1 %copy-start.1 = (s32[32,8]{0,1:T(8,128)S(1)}, s32[32,8]{0,1:T(8,128)}, u32[]{:S(2)}) copy-start(s32[32,8]{0,1:T(8,128)} %param.22) | copy-start | bytes 3076
  43.9 9.1 %copy-start.2 = (f32[32,8]{0,1:T(8,128)S(1)}, f32[32,8]{0,1:T(8,128)}, u32[]{:S(2)}) copy-start(f32[32,8]{0,1:T(8,128)} %param.21) | copy-start | bytes 3076
  43.9 9.1 %copy-start.6 = (s32[1,1,32]{2,1,0:T(1,128)S(1)}, s32[1,1,32]{2,1,0:T(1,128)}, u32[]{:S(2)}) copy-start(s32[1,1,32]{2,1,0:T(1,128)} %refs_1_.1) | copy-start | bytes 388
  63.0 12.0 %collective-permute-start.14 = (bf16[8,128,128]{2,1,0:T(8,128)(2,1)S(1)}, bf16[8,128,128]{2,1,0:T(8,128)(2,1)S(1)}, u32[]{:S(2)}, u32[]{:S(2)}) collective-permute-start(bf16[8,128,128]{2,1,0:T(8,128)(2,1)S(1)} %get-tuple-element.21), channel_id=1, source_target_pairs={{0,32},{16,48},{32,64},{48,80},{64,96},{80,112},{96,0},{112,16},{1... | collective-permute-start | bytes 786440 | tf_op jit(solution)/shard_map/ppermute | solution.py:283
  63.8 14.4 %collective-permute-start.15 = (bf16[8,128,128]{2,1,0:T(8,128)(2,1)S(1)}, bf16[8,128,128]{2,1,0:T(8,128)(2,1)S(1)}, u32[]{:S(2)}, u32[]{:S(2)}) collective-permute-start(bf16[8,128,128]{2,1,0:T(8,128)(2,1)S(1)} %get-tuple-element.22), channel_id=1, source_target_pairs={{0,64},{16,80},{32,96},{48,112},{64,0},{80,16},{96,32},{112,48},{1... | collective-permute-start | bytes 786440 | tf_op jit(solution)/shard_map/ppermute | solution.py:283
  66.5 12.9 %collective-permute-start.16 = (bf16[8,128,128]{2,1,0:T(8,128)(2,1)S(1)}, bf16[8,128,128]{2,1,0:T(8,128)(2,1)S(1)}, u32[]{:S(2)}, u32[]{:S(2)}) collective-permute-start(bf16[8,128,128]{2,1,0:T(8,128)(2,1)S(1)} %get-tuple-element.23), channel_id=1, source_target_pairs={{0,96},{16,112},{32,0},{48,16},{64,32},{80,48},{96,64},{112,80},{1... | collective-permute-start | bytes 786440 | tf_op jit(solution)/shard_map/ppermute | solution.py:283
  66.5 24.2 %all-to-all-start.2 = ((bf16[16,2,128,128]{3,2,1,0:T(8,128)(2,1)}), bf16[16,2,128,128]{3,2,1,0:T(8,128)(2,1)S(1)}, u32[]{:S(2)}, u32[]{:S(2)}) async-start(bf16[16,2,128,128]{3,2,1,0:T(8,128)(2,1)} %bitcast.17), calls=%async_computation.2 | async-start | bytes 2097152 | tf_op jit(solution)/shard_map/all_to_all | solution.py:315
  73.5 5.9 %collective-permute-start.17 = (bf16[8,128,128]{2,1,0:T(8,128)(2,1)S(1)}, bf16[8,128,128]{2,1,0:T(8,128)(2,1)S(1)}, u32[]{:S(2)}, u32[]{:S(2)}) collective-permute-start(bf16[8,128,128]{2,1,0:T(8,128)(2,1)S(1)} %get-tuple-element.20.refs_0_), channel_id=1, source_target_pairs={{0,16},{16,0},{32,48},{48,32},{64,80},{80,64},{96,112},{112,96},{1... | collective-permute-start | bytes 786440 | tf_op jit(solution)/shard_map/ppermute | solution.py:279
  75.0 4.4 %collective-permute-start.18 = (bf16[8,128,128]{2,1,0:T(8,128)(2,1)S(1)}, bf16[8,128,128]{2,1,0:T(8,128)(2,1)S(1)}, u32[]{:S(2)}, u32[]{:S(2)}) collective-permute-start(bf16[8,128,128]{2,1,0:T(8,128)(2,1)S(1)} %collective-permute-done.14.refs_1_), channel_id=1, source_target_pairs={{0,16},{16,0},{32,48},{48,32},{64,80},{80,64},{96,112},{112,96},{1... | collective-permute-start | bytes 786440 | tf_op jit(solution)/shard_map/ppermute | solution.py:279
  78.2 2.4 %collective-permute-start.19 = (bf16[8,128,128]{2,1,0:T(8,128)(2,1)S(1)}, bf16[8,128,128]{2,1,0:T(8,128)(2,1)S(1)}, u32[]{:S(2)}, u32[]{:S(2)}) collective-permute-start(bf16[8,128,128]{2,1,0:T(8,128)(2,1)S(1)} %collective-permute-done.15.refs_2_), channel_id=1, source_target_pairs={{0,16},{16,0},{32,48},{48,32},{64,80},{80,64},{96,112},{112,96},{1... | collective-permute-start | bytes 786440 | tf_op jit(solution)/shard_map/ppermute | solution.py:279
  79.4 1.5 %collective-permute-start.20 = (bf16[8,128,128]{2,1,0:T(8,128)(2,1)S(1)}, bf16[8,128,128]{2,1,0:T(8,128)(2,1)S(1)}, u32[]{:S(2)}, u32[]{:S(2)}) collective-permute-start(bf16[8,128,128]{2,1,0:T(8,128)(2,1)S(1)} %collective-permute-done.16.refs_3_), channel_id=1, source_target_pairs={{0,16},{16,0},{32,48},{48,32},{64,80},{80,64},{96,112},{112,96},{1... | collective-permute-start | bytes 786440 | tf_op jit(solution)/shard_map/ppermute | solution.py:279
  80.9 0.7 copy-start.10
